TPU v7x, 32 devices: a whole 2x2x4 slice. The times are simulated.
32 devices in a mesh: dp: 4 (over y, core), blk: 8 (over z, x).
Axes of the slice: x: 2, y: 2, z: 4, core: 2. Of those that a mesh axis runs over, the one named last changes fastest.
Arguments:
- block_in: bfloat16 [4, 1024, 512], P('dp', 'blk'), may hold values from -6 to 6
- seq_lengths: int32 [4], P('dp'), may hold values from 897 to 1024, as said below
- norm1_gain: float32 [512], replicated, may hold values from 0.5 to 1.5
- norm1_bias: float32 [512], replicated, may hold values from -3 to 3
- log_step: float32 [512], replicated, may hold values from -7 to -5.5
- log_rate: float32 [512, 64], replicated, may hold values from -12 to -2.99
- frequency: float32 [512, 64], replicated, may hold values from 0 to 192
- out_coef: float32 [2, 512, 64], replicated, may hold values from -3 to 3
- skip_gain: float32 [512], replicated, may hold values from -4 to 4
- glu_weight: bfloat16 [512, 1024], replicated, may hold values from -0.25 to 0.25
- glu_bias: float32 [1024], replicated, may hold values from -3 to 3
- norm2_gain: float32 [512], replicated, may hold values from 0.5 to 1.5
- norm2_bias: float32 [512], replicated, may hold values from -3 to 3
- ffn_in: bfloat16 [512, 2048], replicated, may hold values from -0.25 to 0.25
- ffn_in_bias: float32 [2048], replicated, may hold values from -3 to 3
- ffn_out: bfloat16 [2048, 512], replicated, may hold values from -0.125 to 0.125
- ffn_out_bias: float32 [512], replicated, may hold values from -3 to 3
- cotangent: bfloat16 [4, 1024, 512], P('dp', 'blk'), may hold values from -6 to 6
Outputs:
- block_out: bfloat16 [4, 1024, 512], P('dp', 'blk')
- grad_block_in: float32 [4, 1024, 512], P('dp', 'blk')
- grad_norm1_gain: float32 [512], replicated
- grad_norm1_bias: float32 [512], replicated
- grad_log_step: float32 [512], replicated
- grad_log_rate: float32 [512, 64], replicated
- grad_frequency: float32 [512, 64], replicated
- grad_out_coef: float32 [2, 512, 64], replicated
- grad_skip_gain: float32 [512], replicated
- grad_glu_weight: float32 [512, 1024], replicated
- grad_glu_bias: float32 [1024], replicated
- grad_norm2_gain: float32 [512], replicated
- grad_norm2_bias: float32 [512], replicated
- grad_ffn_in: float32 [512, 2048], replicated
- grad_ffn_in_bias: float32 [2048], replicated
- grad_ffn_out: float32 [2048, 512], replicated
- grad_ffn_out_bias: float32 [512], replicated
Inputs may be any that keep to these rules, and one draw needn't show every extreme that they name: `seq_lengths`: every sequence has at least its last block partly live; some sequence is live to its end.
All inputs are finite; a program needn't handle non-finite values.
Results may differ from a plain program's by a relative error of at most 0.014.
Values sent between devices are 32-bit elements; how exact they have to be, the bound alone decides.
A program may use at most 128 MiB of HBM per device.

v0:
```python
import jax
import jax.numpy as jnp
from jax import lax
from jax.sharding import PartitionSpec as P

NORM_EPSILON = 1e-05
PRECISE = lax.Precision.HIGHEST


def prefix_2(value, axis, combine, identity, reverse):
    devices, position = (lax.axis_size(axis), lax.axis_index(axis))
    everything = jax.tree.map(lambda part: lax.all_gather(part, axis), value)
    start = jax.tree.map(
        lambda part, zero: jnp.broadcast_to(jnp.asarray(zero, part.dtype), part.shape),
        value,
        identity,
    )

    def hop(k, before):
        at = devices - 1 - k if reverse else k
        reached = at > position if reverse else at < position
        new = combine(before, jax.tree.map(lambda part: part[at], everything))
        return jax.tree.map(lambda a, b: jnp.where(reached, a, b), new, before)

    return lax.fori_loop(0, devices, hop, start)


def complex_mul(left, right):
    return jnp.stack(
        [left[0] * right[0] - left[1] * right[1], left[0] * right[1] + left[1] * right[0]]
    )


def powers(log_pole, counts):
    growth = jnp.exp(log_pole[0][..., None] * counts)
    angles = log_pole[1][..., None] * counts
    return jnp.stack([growth * jnp.cos(angles), growth * jnp.sin(angles)])


def ssm_setup(log_step, log_rate, frequency, out_coef):
    step_size = jnp.exp(log_step)
    pole_real = -jnp.exp(log_rate)
    pole_imag = step_size[:, None] * frequency
    half_turn = jnp.sin(0.5 * pole_imag)
    minus_real = jnp.expm1(pole_real) * jnp.cos(pole_imag) - 2.0 * half_turn * half_turn
    minus_imag = jnp.exp(pole_real) * jnp.sin(pole_imag)
    modulus = pole_real * pole_real + pole_imag * pole_imag
    ratios = jnp.stack(
        [
            (minus_real * pole_real + minus_imag * pole_imag) / modulus,
            (minus_imag * pole_real - minus_real * pole_imag) / modulus,
        ]
    )
    return (
        jnp.stack([pole_real, pole_imag]),
        complex_mul(out_coef * step_size[None, :, None], ratios),
    )


def pole_only(log_step, log_rate, frequency, out_coef):
    return ssm_setup(log_step, log_rate, frequency, out_coef)[0]


def group_size():
    return 64


def split_parts(values):
    high_part = values.astype(jnp.bfloat16)
    rest_part = (values - high_part.astype(jnp.float32)).astype(jnp.bfloat16)
    return (high_part, rest_part)


def band_matrix(rows):
    length = rows.shape[-1]
    lag_table = (
        jnp.arange(length, dtype=jnp.int32)[:, None] - jnp.arange(length, dtype=jnp.int32)[None, :]
    )
    picked = rows[..., jnp.maximum(lag_table, 0)]
    return jnp.where(lag_table >= 0, picked, jnp.zeros_like(picked))


def to_groups(values, size_one):
    count_seq, block_rows, channels = values.shape
    return values.reshape(count_seq, block_rows, channels // size_one, size_one).transpose(
        2, 0, 1, 3
    )


def from_groups(values):
    groups, count_seq, block_rows, size_one = values.shape
    return values.transpose(1, 2, 0, 3).reshape(count_seq, block_rows, groups * size_one)


def near_conv(mixed_low, kernel):
    channels = kernel.shape[0]
    size_one = group_size()
    kernel_groups = kernel.reshape(channels // size_one, size_one, kernel.shape[1])

    def per_group(group_args):
        kernel_one, input_one = group_args
        band_high, band_rest = split_parts(kernel_one)
        band_high = band_matrix(band_high)
        band_rest = band_matrix(band_rest)
        result = jnp.einsum(
            "cts,bsc->btc", band_high, input_one, preferred_element_type=jnp.float32
        )
        return result + jnp.einsum(
            "cts,bsc->btc", band_rest, input_one, preferred_element_type=jnp.float32
        )

    return from_groups(lax.map(per_group, (kernel_groups, to_groups(mixed_low, size_one))))


def near_back(grad_conv, mixed_low, kernel):
    channels = kernel.shape[0]
    size_one = group_size()
    kernel_groups = kernel.reshape(channels // size_one, size_one, kernel.shape[1])

    def per_group(group_args):
        kernel_one, input_one, grad_one = group_args
        band_high, band_rest = split_parts(kernel_one)
        band_high = band_matrix(band_high)
        band_rest = band_matrix(band_rest)
        grad_high, grad_rest = split_parts(grad_one)
        grad_input = jnp.einsum(
            "cts,btc->bsc", band_high, grad_high, preferred_element_type=jnp.float32
        )
        grad_input = grad_input + jnp.einsum(
            "cts,btc->bsc", band_high, grad_rest, preferred_element_type=jnp.float32
        )
        grad_input = grad_input + jnp.einsum(
            "cts,btc->bsc", band_rest, grad_high, preferred_element_type=jnp.float32
        )
        input_band = band_matrix(input_one.transpose(0, 2, 1))
        grad_kernel = jnp.einsum(
            "btc,bctl->cl", grad_high, input_band, preferred_element_type=jnp.float32
        )
        grad_kernel = grad_kernel + jnp.einsum(
            "btc,bctl->cl", grad_rest, input_band, preferred_element_type=jnp.float32
        )
        return (grad_input, grad_kernel)

    grad_groups, kernel_grads = lax.map(
        per_group, (kernel_groups, to_groups(mixed_low, size_one), to_groups(grad_conv, size_one))
    )
    return (from_groups(grad_groups), kernel_grads.reshape(channels, kernel.shape[1]))


def state_counts(block_rows):
    return (block_rows - 1 - jnp.arange(block_rows)).astype(jnp.float32)


def pole_groups_of(log_pole, size_one):
    channels, states = (log_pole.shape[1], log_pole.shape[2])
    return log_pole.reshape(2, channels // size_one, size_one, states).transpose(1, 0, 2, 3)


def local_state(log_pole, mixed_low):
    count_seq, block_rows, channels = mixed_low.shape
    states = log_pole.shape[2]
    size_one = group_size()
    counts = state_counts(block_rows)

    def per_group(group_args):
        pole_one, input_one = group_args
        weights = powers(pole_one, counts)
        weight_high, weight_rest = split_parts(weights)
        real_part = jnp.einsum(
            "cnt,stc->scn", weight_high[0], input_one, preferred_element_type=jnp.float32
        )
        real_part = real_part + jnp.einsum(
            "cnt,stc->scn", weight_rest[0], input_one, preferred_element_type=jnp.float32
        )
        imag_part = jnp.einsum(
            "cnt,stc->scn", weight_high[1], input_one, preferred_element_type=jnp.float32
        )
        imag_part = imag_part + jnp.einsum(
            "cnt,stc->scn", weight_rest[1], input_one, preferred_element_type=jnp.float32
        )
        return jnp.stack([real_part, imag_part])

    summed = lax.map(
        per_group, (pole_groups_of(log_pole, size_one), to_groups(mixed_low, size_one))
    )
    return summed.transpose(1, 2, 0, 3, 4).reshape(2, count_seq, channels, states)


def state_back(log_pole, mixed_low, grad_state):
    count_seq, block_rows, channels = mixed_low.shape
    states = log_pole.shape[2]
    size_one = group_size()
    groups = channels // size_one
    counts = state_counts(block_rows)
    grad_groups = grad_state.reshape(2, count_seq, groups, size_one, states).transpose(
        2, 0, 1, 3, 4
    )

    def per_group(group_args):
        pole_one, input_one, grad_one = group_args
        weights, pull_weights = jax.vjp(lambda pole_arg: powers(pole_arg, counts), pole_one)
        weight_high, weight_rest = split_parts(weights)
        grad_high, grad_rest = split_parts(grad_one)
        grad_input = jnp.zeros(input_one.shape, jnp.float32)
        for part_index in range(2):
            grad_input = grad_input + jnp.einsum(
                "scn,cnt->stc",
                grad_high[part_index],
                weight_high[part_index],
                preferred_element_type=jnp.float32,
            )
            grad_input = grad_input + jnp.einsum(
                "scn,cnt->stc",
                grad_rest[part_index],
                weight_high[part_index],
                preferred_element_type=jnp.float32,
            )
            grad_input = grad_input + jnp.einsum(
                "scn,cnt->stc",
                grad_high[part_index],
                weight_rest[part_index],
                preferred_element_type=jnp.float32,
            )
        input_wide = input_one.astype(jnp.float32).transpose(0, 2, 1)
        grad_weights = jnp.sum(grad_one[:, :, :, :, None] * input_wide[None, :, :, None, :], axis=1)
        return (grad_input, pull_weights(grad_weights)[0])

    grad_inputs, grad_poles = lax.map(
        per_group, (pole_groups_of(log_pole, size_one), to_groups(mixed_low, size_one), grad_groups)
    )
    return (from_groups(grad_inputs), grad_poles.transpose(1, 0, 2, 3).reshape(2, channels, states))


def block_power_of(log_pole, block_rows):
    return powers(log_pole, jnp.full((1,), block_rows, jnp.float32))[..., 0]


def near_far(ssm_params, carried, block_rows):
    log_pole, residue = ssm_setup(*ssm_params)
    count_seq, channels, states = (carried.shape[1], carried.shape[2], carried.shape[3])
    size_one = group_size()
    groups = channels // size_one
    first_power = powers(log_pole, jnp.ones((1,), jnp.float32))[..., 0]
    lead_coef = complex_mul(complex_mul(residue, first_power)[:, None], carried)
    pole_groups = pole_groups_of(log_pole, size_one)
    residue_groups = pole_groups_of(residue, size_one)
    lead_groups = lead_coef.reshape(2, count_seq, groups, size_one, states).transpose(2, 0, 1, 3, 4)
    counts = jnp.arange(block_rows).astype(jnp.float32)

    def per_group(group_args):
        pole_one, residue_one, lead_one = group_args
        weights = powers(pole_one, counts)
        kernel = jnp.einsum("cn,cnt->ct", residue_one[0], weights[0], precision=PRECISE)
        kernel = 2.0 * (
            kernel - jnp.einsum("cn,cnt->ct", residue_one[1], weights[1], precision=PRECISE)
        )
        far_part = jnp.einsum("scn,cnt->stc", lead_one[0], weights[0], precision=PRECISE)
        far_part = 2.0 * (
            far_part - jnp.einsum("scn,cnt->stc", lead_one[1], weights[1], precision=PRECISE)
        )
        return (kernel, far_part)

    kernel_groups, far_groups = lax.map(
        jax.checkpoint(per_group), (pole_groups, residue_groups, lead_groups)
    )
    kernel = kernel_groups.reshape(channels, block_rows)
    far_part = far_groups.transpose(1, 2, 0, 3).reshape(count_seq, block_rows, channels)
    return (kernel, far_part)


def ahead(block_state, block_power):
    zeros_state = jnp.zeros_like(block_state)
    unit_power = jnp.stack([jnp.ones_like(block_power[0]), jnp.zeros_like(block_power[0])])

    def combine(earlier, later):
        power_early, slope_early, state_early, deriv_early = earlier
        power_later, slope_later, state_later, deriv_later = later
        return (
            complex_mul(power_early, power_later),
            complex_mul(slope_early, power_later) + complex_mul(power_early, slope_later),
            complex_mul(power_later[:, None], state_early) + state_later,
            complex_mul(slope_later[:, None], state_early)
            + complex_mul(power_later[:, None], deriv_early)
            + deriv_later,
        )

    prefix = prefix_2(
        (block_power, unit_power, block_state, zeros_state),
        "blk",
        combine,
        (unit_power, jnp.zeros_like(block_power), zeros_state, zeros_state),
        False,
    )
    return (prefix[2], prefix[3])


def behind(grad_state, block_power):
    unit_power = jnp.stack([jnp.ones_like(block_power[0]), jnp.zeros_like(block_power[0])])
    flipped = jnp.stack([block_power[0], -block_power[1]])

    def combine(earlier, later):
        return (
            complex_mul(earlier[0], later[0]),
            complex_mul(later[0][:, None], earlier[1]) + later[1],
        )

    suffix = prefix_2(
        (flipped, grad_state), "blk", combine, (unit_power, jnp.zeros_like(grad_state)), True
    )
    return suffix[1]


def layer_norm(values, gain, shift):
    center = values - jnp.mean(values, axis=-1, keepdims=True)
    scale = lax.rsqrt(jnp.mean(center * center, axis=-1, keepdims=True) + NORM_EPSILON)
    normed = center * scale
    return (normed * gain + shift, normed, scale)


def norm_back(grad_out, gain, normed, scale):
    scaled = grad_out * gain
    return scale * (
        scaled
        - jnp.mean(scaled, axis=-1, keepdims=True)
        - normed * jnp.mean(scaled * normed, axis=-1, keepdims=True)
    )


def token_sum(values):
    return jnp.sum(values, axis=(0, 1))


def on_device(
    block_in,
    seq_lengths,
    norm1_gain,
    norm1_bias,
    log_step,
    log_rate,
    frequency,
    out_coef,
    skip_gain,
    glu_weight,
    glu_bias,
    norm2_gain,
    norm2_bias,
    ffn_in,
    ffn_in_bias,
    ffn_out,
    ffn_out_bias,
    cotangent,
):
    count_seq, block_rows, channels = block_in.shape
    inputs = block_in.astype(jnp.float32)
    places = lax.axis_index("blk") * block_rows + jnp.arange(block_rows, dtype=jnp.int32)
    live = (places[None, :] < seq_lengths[:, None]).astype(jnp.float32)[..., None]
    normed_in, unit_in, scale_in = layer_norm(inputs, norm1_gain, norm1_bias)
    mixed_low = normed_in.astype(jnp.bfloat16) * live.astype(jnp.bfloat16)
    mixed_in = mixed_low.astype(jnp.float32)
    ssm_params = (log_step, log_rate, frequency, out_coef)
    log_pole, pull_pole = jax.vjp(pole_only, *ssm_params)
    block_state = local_state(log_pole, mixed_low)
    block_power, pull_power = jax.vjp(
        lambda pole_arg: block_power_of(pole_arg, block_rows), log_pole
    )
    earlier_state, state_slope = ahead(block_state, block_power)
    (kernel, far_part), pull_far = jax.vjp(
        lambda params_arg, carried_arg: near_far(params_arg, carried_arg, block_rows),
        ssm_params,
        earlier_state,
    )
    conv_out = near_conv(mixed_low, kernel) + far_part + skip_gain * mixed_in
    gelu_out = jax.nn.gelu(conv_out).astype(jnp.bfloat16)
    glu_pre = (
        jnp.einsum("sbd,de->sbe", gelu_out, glu_weight, preferred_element_type=jnp.float32)
        + glu_bias
    )
    glu_left = glu_pre[..., :channels]
    glu_gate = jax.nn.sigmoid(glu_pre[..., channels:])
    residual = inputs + live * glu_left * glu_gate
    normed_mid, unit_mid, scale_mid = layer_norm(residual, norm2_gain, norm2_bias)
    ffn_feed = normed_mid.astype(jnp.bfloat16)
    hidden_pre = (
        jnp.einsum("sbd,df->sbf", ffn_feed, ffn_in, preferred_element_type=jnp.float32)
        + ffn_in_bias
    )
    hidden = jax.nn.gelu(hidden_pre).astype(jnp.bfloat16)
    ffn_result = (
        jnp.einsum("sbf,fd->sbd", hidden, ffn_out, preferred_element_type=jnp.float32)
        + ffn_out_bias
    )
    block_out = (residual + live * ffn_result).astype(jnp.bfloat16)
    upstream = cotangent.astype(jnp.float32)
    grad_result = (live * upstream).astype(jnp.bfloat16)
    grad_ffn_out = jnp.einsum(
        "sbf,sbd->fd", hidden, grad_result, preferred_element_type=jnp.float32
    )
    grad_ffn_out_bias = token_sum(grad_result.astype(jnp.float32))
    grad_hidden = jnp.einsum(
        "sbd,fd->sbf", grad_result, ffn_out, preferred_element_type=jnp.float32
    )
    grad_pre = jax.vjp(jax.nn.gelu, hidden_pre)[1](grad_hidden)[0].astype(jnp.bfloat16)
    grad_ffn_in = jnp.einsum("sbd,sbf->df", ffn_feed, grad_pre, preferred_element_type=jnp.float32)
    grad_ffn_in_bias = token_sum(grad_pre.astype(jnp.float32))
    grad_feed = jnp.einsum("sbf,df->sbd", grad_pre, ffn_in, preferred_element_type=jnp.float32)
    grad_norm2_gain = token_sum(grad_feed * unit_mid)
    grad_norm2_bias = token_sum(grad_feed)
    grad_residual = upstream + norm_back(grad_feed, norm2_gain, unit_mid, scale_mid)
    grad_left = live * grad_residual
    grad_glu = jnp.concatenate(
        [grad_left * glu_gate, grad_left * glu_left * glu_gate * (1.0 - glu_gate)], axis=-1
    ).astype(jnp.bfloat16)
    grad_glu_weight = jnp.einsum(
        "sbd,sbe->de", gelu_out, grad_glu, preferred_element_type=jnp.float32
    )
    grad_glu_bias = token_sum(grad_glu.astype(jnp.float32))
    grad_gelu = jnp.einsum("sbe,de->sbd", grad_glu, glu_weight, preferred_element_type=jnp.float32)
    grad_conv = jax.vjp(jax.nn.gelu, conv_out)[1](grad_gelu)[0]
    grad_skip = token_sum(grad_conv * mixed_in)
    grad_mixed_near, grad_kernel = near_back(grad_conv, mixed_low, kernel)
    grad_params_out, grad_earlier = pull_far((grad_kernel, grad_conv))
    grad_block_state = behind(grad_earlier, block_power)
    slope_conj = jnp.stack([state_slope[0], -state_slope[1]])
    grad_power = jnp.sum(complex_mul(grad_earlier, slope_conj), axis=1)
    grad_mixed_state, grad_pole_state = state_back(log_pole, mixed_low, grad_block_state)
    grad_pole_total = grad_pole_state + pull_power(grad_power)[0]
    grad_params_state = pull_pole(grad_pole_total)
    grad_ssm = jax.tree.map(jnp.add, tuple(grad_params_out), tuple(grad_params_state))
    grad_mixed = grad_mixed_near + grad_mixed_state + skip_gain * grad_conv
    grad_normed_in = live * grad_mixed
    grad_norm1_gain = token_sum(grad_normed_in * unit_in)
    grad_norm1_bias = token_sum(grad_normed_in)
    grad_block_in = grad_residual + norm_back(grad_normed_in, norm1_gain, unit_in, scale_in)
    totals = lax.psum(
        (
            grad_norm1_gain,
            grad_norm1_bias,
            grad_ssm[0],
            grad_ssm[1],
            grad_ssm[2],
            grad_ssm[3],
            grad_skip,
            grad_glu_weight,
            grad_glu_bias,
            grad_norm2_gain,
            grad_norm2_bias,
            grad_ffn_in,
            grad_ffn_in_bias,
            grad_ffn_out,
            grad_ffn_out_bias,
        ),
        ("dp", "blk"),
    )
    return (
        block_out,
        grad_block_in,
        totals[0],
        totals[1],
        totals[2],
        totals[3],
        totals[4],
        totals[5],
        totals[6],
        totals[7],
        totals[8],
        totals[9],
        totals[10],
        totals[11],
        totals[12],
        totals[13],
        totals[14],
    )


def solution(mesh):
    return jax.shard_map(
        on_device,
        mesh=mesh,
        in_specs=(
            P("dp", "blk", None),
            P("dp"),
            P(),
            P(),
            P(),
            P(),
            P(),
            P(),
            P(),
            P(),
            P(),
            P(),
            P(),
            P(),
            P(),
            P(),
            P(),
            P("dp", "blk", None),
        ),
        out_specs=(
            P("dp", "blk", None),
            P("dp", "blk", None),
            P(),
            P(),
            P(),
            P(),
            P(),
            P(),
            P(),
            P(),
            P(),
            P(),
            P(),
            P(),
            P(),
            P(),
            P(),
        ),
        check_vma=False,
    )
```

profile of v0, /device:TPU:0, one launch (start us, length us, event | category | flops | bytes accessed | tf_op | source)
XLA Modules:
  0.0 4424.1 jit_solution(7283667310428899119)
XLA Ops:
  15.8 92.1 %while.117 = (s32[]{:T(128)}, f32[8,2,1,64,64]{4,3,2,1,0:T(8,128)S(1)}, bf16[8,1,128,64]{3,2,1,0:T(8,128)(2,1)S(1)}, f32[8,2,64,64]{3,2,1,0:T(8,128)S(1)}, s32[]{:T(128)}, /*index=5*/s32[]{:T(128)}, s32[]{}) while((s32[]{:T(128)}, f32[8,2,1,64,64]{4,3,2,1,0:T(8,128)S(1)}, bf16[8,1,128,64]{3,2,1,0:T(8,128)(2,1)S(1)}, ...), condition=%wide.region_3.4_spmd.clone.clone, body=%wide.region_2.3_spmd.clone.clone.sunk | while | flops 12599555 | bytes 21562480 | solution.py:183
  213.0 129.9 %while.120 = (s32[]{:T(128)}, f32[2,1,512,64]{3,2,1,0:T(8,128)}, f32[2,1,512,64]{3,2,1,0:T(8,128)}, s32[]{:T(128)}, f32[8,2,512,64]{2,3,1,0:T(8,128)}, /*index=5...) while((s32[]{:T(128)}, f32[2,1,512,64]{3,2,1,0:T(8,128)}, ...), condition=%wide.region_5.6_spmd.clone, body=%wide.region_4.5_spmd.clone.sunk | while | flops 1179653 | bytes 9699566 | solution.py:25
  353.2 340.7 %while.118 = (s32[]{:T(128)}, f32[8,64,128]{2,1,0:T(8,128)S(1)}, f32[8,1,128,64]{2,3,1,0:T(8,128)}, f32[8,2,64,64]{3,2,1,0:T(8,128)S(1)}, f32[8,2,64,64]{3,2,1,0...) while((s32[]{:T(128)}, f32[8,64,128]{2,1,0:T(8,128)S(1)}, ...), condition=%wide.region_7.8_spmd.clone.clone, body=%wide.region_6.7_spmd.clone.clone.sunk | while | flops 31490180 | bytes 723601 | solution.py:263
  695.1 1003.9 %while.114 = (s32[]{:T(128)}, f32[8,1,128,64]{2,3,0,1:T(8,128)S(1)}, bf16[8,1,128,64]{3,2,1,0:T(8,128)(2,1)}, f32[8,64,128]{1,2,0:T(8,128)S(1)}, s32[]{:T(128)}) while((s32[]{:T(128)}, f32[8,1,128,64]{2,3,0,1:T(8,128)S(1)}, bf16[8,1,128,64]{3,2,1,0:T(8,128)(2,1)}, f32[8,64,128]{1,2,0:T(8,128)S(1)}, s32[]{:T(128)}) %tuple.428), condition=%wide.region_9.10_spmd, body=%wide.region_8.9_spmd.sunk | while | flops 8495106 | bytes 13271121 | solution.py:112
  695.9 57.9 %gather_fusion = bf16[16384,64]{1,0:T(8,128)(2,1)} fusion(bf16[64,128]{0,1:T(8,128)(2,1)S(1)} %get-tuple-element.1631, s32[16384]{0:T(1024)S(1)} %bitcast_clamp_fusion.4), kind=kCustom, calls=%fused_computation.1.clone.1 | custom fusion | bytes 4259840 | tf_op jit(solution)/shard_map/while/body/eval_jaxpr/gather | solution.py:79
  753.8 57.9 %gather_fusion.1 = bf16[16384,64]{1,0:T(8,128)(2,1)} fusion(bf16[64,128]{0,1:T(8,128)(2,1)S(1)} %get-tuple-element.1632, s32[16384]{0:T(1024)S(1)} %bitcast_clamp_fusion.4), kind=kCustom, calls=%fused_computation.clone.1 | custom fusion | bytes 4259840 | tf_op jit(solution)/shard_map/while/body/eval_jaxpr/gather | solution.py:79
  821.4 57.9 %gather_fusion = bf16[16384,64]{1,0:T(8,128)(2,1)} fusion(bf16[64,128]{0,1:T(8,128)(2,1)S(1)} %get-tuple-element.1631, s32[16384]{0:T(1024)S(1)} %bitcast_clamp_fusion.4), kind=kCustom, calls=%fused_computation.1.clone.1 | custom fusion | bytes 4259840 | tf_op jit(solution)/shard_map/while/body/eval_jaxpr/gather | solution.py:79
  879.3 57.9 %gather_fusion.1 = bf16[16384,64]{1,0:T(8,128)(2,1)} fusion(bf16[64,128]{0,1:T(8,128)(2,1)S(1)} %get-tuple-element.1632, s32[16384]{0:T(1024)S(1)} %bitcast_clamp_fusion.4), kind=kCustom, calls=%fused_computation.clone.1 | custom fusion | bytes 4259840 | tf_op jit(solution)/shard_map/while/body/eval_jaxpr/gather | solution.py:79
  946.8 57.9 %gather_fusion = bf16[16384,64]{1,0:T(8,128)(2,1)} fusion(bf16[64,128]{0,1:T(8,128)(2,1)S(1)} %get-tuple-element.1631, s32[16384]{0:T(1024)S(1)} %bitcast_clamp_fusion.4), kind=kCustom, calls=%fused_computation.1.clone.1 | custom fusion | bytes 4259840 | tf_op jit(solution)/shard_map/while/body/eval_jaxpr/gather | solution.py:79
  1004.8 57.9 %gather_fusion.1 = bf16[16384,64]{1,0:T(8,128)(2,1)} fusion(bf16[64,128]{0,1:T(8,128)(2,1)S(1)} %get-tuple-element.1632, s32[16384]{0:T(1024)S(1)} %bitcast_clamp_fusion.4), kind=kCustom, calls=%fused_computation.clone.1 | custom fusion | bytes 4259840 | tf_op jit(solution)/shard_map/while/body/eval_jaxpr/gather | solution.py:79
  1072.3 57.9 %gather_fusion = bf16[16384,64]{1,0:T(8,128)(2,1)} fusion(bf16[64,128]{0,1:T(8,128)(2,1)S(1)} %get-tuple-element.1631, s32[16384]{0:T(1024)S(1)} %bitcast_clamp_fusion.4), kind=kCustom, calls=%fused_computation.1.clone.1 | custom fusion | bytes 4259840 | tf_op jit(solution)/shard_map/while/body/eval_jaxpr/gather | solution.py:79
  1130.2 57.9 %gather_fusion.1 = bf16[16384,64]{1,0:T(8,128)(2,1)} fusion(bf16[64,128]{0,1:T(8,128)(2,1)S(1)} %get-tuple-element.1632, s32[16384]{0:T(1024)S(1)} %bitcast_clamp_fusion.4), kind=kCustom, calls=%fused_computation.clone.1 | custom fusion | bytes 4259840 | tf_op jit(solution)/shard_map/while/body/eval_jaxpr/gather | solution.py:79
  1197.8 57.9 %gather_fusion = bf16[16384,64]{1,0:T(8,128)(2,1)} fusion(bf16[64,128]{0,1:T(8,128)(2,1)S(1)} %get-tuple-element.1631, s32[16384]{0:T(1024)S(1)} %bitcast_clamp_fusion.4), kind=kCustom, calls=%fused_computation.1.clone.1 | custom fusion | bytes 4259840 | tf_op jit(solution)/shard_map/while/body/eval_jaxpr/gather | solution.py:79
  1255.7 57.9 %gather_fusion.1 = bf16[16384,64]{1,0:T(8,128)(2,1)} fusion(bf16[64,128]{0,1:T(8,128)(2,1)S(1)} %get-tuple-element.1632, s32[16384]{0:T(1024)S(1)} %bitcast_clamp_fusion.4), kind=kCustom, calls=%fused_computation.clone.1 | custom fusion | bytes 4259840 | tf_op jit(solution)/shard_map/while/body/eval_jaxpr/gather | solution.py:79
  1323.2 57.9 %gather_fusion = bf16[16384,64]{1,0:T(8,128)(2,1)} fusion(bf16[64,128]{0,1:T(8,128)(2,1)S(1)} %get-tuple-element.1631, s32[16384]{0:T(1024)S(1)} %bitcast_clamp_fusion.4), kind=kCustom, calls=%fused_computation.1.clone.1 | custom fusion | bytes 4259840 | tf_op jit(solution)/shard_map/while/body/eval_jaxpr/gather | solution.py:79
  1381.1 57.9 %gather_fusion.1 = bf16[16384,64]{1,0:T(8,128)(2,1)} fusion(bf16[64,128]{0,1:T(8,128)(2,1)S(1)} %get-tuple-element.1632, s32[16384]{0:T(1024)S(1)} %bitcast_clamp_fusion.4), kind=kCustom, calls=%fused_computation.clone.1 | custom fusion | bytes 4259840 | tf_op jit(solution)/shard_map/while/body/eval_jaxpr/gather | solution.py:79
  1448.7 57.9 %gather_fusion = bf16[16384,64]{1,0:T(8,128)(2,1)} fusion(bf16[64,128]{0,1:T(8,128)(2,1)S(1)} %get-tuple-element.1631, s32[16384]{0:T(1024)S(1)} %bitcast_clamp_fusion.4), kind=kCustom, calls=%fused_computation.1.clone.1 | custom fusion | bytes 4259840 | tf_op jit(solution)/shard_map/while/body/eval_jaxpr/gather | solution.py:79
  1506.6 57.9 %gather_fusion.1 = bf16[16384,64]{1,0:T(8,128)(2,1)} fusion(bf16[64,128]{0,1:T(8,128)(2,1)S(1)} %get-tuple-element.1632, s32[16384]{0:T(1024)S(1)} %bitcast_clamp_fusion.4), kind=kCustom, calls=%fused_computation.clone.1 | custom fusion | bytes 4259840 | tf_op jit(solution)/shard_map/while/body/eval_jaxpr/gather | solution.py:79
  1574.1 57.9 %gather_fusion = bf16[16384,64]{1,0:T(8,128)(2,1)} fusion(bf16[64,128]{0,1:T(8,128)(2,1)S(1)} %get-tuple-element.1631, s32[16384]{0:T(1024)S(1)} %bitcast_clamp_fusion.4), kind=kCustom, calls=%fused_computation.1.clone.1 | custom fusion | bytes 4259840 | tf_op jit(solution)/shard_map/while/body/eval_jaxpr/gather | solution.py:79
  1632.0 57.9 %gather_fusion.1 = bf16[16384,64]{1,0:T(8,128)(2,1)} fusion(bf16[64,128]{0,1:T(8,128)(2,1)S(1)} %get-tuple-element.1632, s32[16384]{0:T(1024)S(1)} %bitcast_clamp_fusion.4), kind=kCustom, calls=%fused_computation.clone.1 | custom fusion | bytes 4259840 | tf_op jit(solution)/shard_map/while/body/eval_jaxpr/gather | solution.py:79
  1711.4 1484.8 %while.115 = (s32[]{:T(128)}, f32[8,1,128,64]{2,3,0,1:T(8,128)}, f32[8,64,128]{2,1,0:T(8,128)}, f32[8,1,128,64]{2,3,0,1:T(8,128)S(1)}, f32[8,64,128]{1,2,0:T(8,1...) while((s32[]{:T(128)}, f32[8,1,128,64]{2,3,0,1:T(8,128)}, f32[8,64,128]{2,1,0:T(8,128)}, ...), condition=%wide.region_15.16_spmd, body=%wide.region_14.15_spmd.sunk | while | flops 16924672 | bytes 20267112 | solution.py:144
  1711.6 57.9 %gather_fusion.2 = bf16[16384,64]{1,0:T(8,128)(2,1)} fusion(bf16[64,128]{0,1:T(8,128)(2,1)S(1)} %get-tuple-element.1641, s32[16384]{0:T(1024)S(1)} %bitcast_clamp_fusion.5), kind=kCustom, calls=%fused_computation.2.clone.1 | custom fusion | bytes 4259840 | tf_op jit(solution)/shard_map/while/body/eval_jaxpr/gather | solution.py:79
  1897.2 57.9 %gather_fusion.2 = bf16[16384,64]{1,0:T(8,128)(2,1)} fusion(bf16[64,128]{0,1:T(8,128)(2,1)S(1)} %get-tuple-element.1641, s32[16384]{0:T(1024)S(1)} %bitcast_clamp_fusion.5), kind=kCustom, calls=%fused_computation.2.clone.1 | custom fusion | bytes 4259840 | tf_op jit(solution)/shard_map/while/body/eval_jaxpr/gather | solution.py:79
  2082.8 57.9 %gather_fusion.2 = bf16[16384,64]{1,0:T(8,128)(2,1)} fusion(bf16[64,128]{0,1:T(8,128)(2,1)S(1)} %get-tuple-element.1641, s32[16384]{0:T(1024)S(1)} %bitcast_clamp_fusion.5), kind=kCustom, calls=%fused_computation.2.clone.1 | custom fusion | bytes 4259840 | tf_op jit(solution)/shard_map/while/body/eval_jaxpr/gather | solution.py:79
  2268.4 57.9 %gather_fusion.2 = bf16[16384,64]{1,0:T(8,128)(2,1)} fusion(bf16[64,128]{0,1:T(8,128)(2,1)S(1)} %get-tuple-element.1641, s32[16384]{0:T(1024)S(1)} %bitcast_clamp_fusion.5), kind=kCustom, calls=%fused_computation.2.clone.1 | custom fusion | bytes 4259840 | tf_op jit(solution)/shard_map/while/body/eval_jaxpr/gather | solution.py:79
  2454.0 57.9 %gather_fusion.2 = bf16[16384,64]{1,0:T(8,128)(2,1)} fusion(bf16[64,128]{0,1:T(8,128)(2,1)S(1)} %get-tuple-element.1641, s32[16384]{0:T(1024)S(1)} %bitcast_clamp_fusion.5), kind=kCustom, calls=%fused_computation.2.clone.1 | custom fusion | bytes 4259840 | tf_op jit(solution)/shard_map/while/body/eval_jaxpr/gather | solution.py:79
  2639.6 57.9 %gather_fusion.2 = bf16[16384,64]{1,0:T(8,128)(2,1)} fusion(bf16[64,128]{0,1:T(8,128)(2,1)S(1)} %get-tuple-element.1641, s32[16384]{0:T(1024)S(1)} %bitcast_clamp_fusion.5), kind=kCustom, calls=%fused_computation.2.clone.1 | custom fusion | bytes 4259840 | tf_op jit(solution)/shard_map/while/body/eval_jaxpr/gather | solution.py:79
  2825.2 57.9 %gather_fusion.2 = bf16[16384,64]{1,0:T(8,128)(2,1)} fusion(bf16[64,128]{0,1:T(8,128)(2,1)S(1)} %get-tuple-element.1641, s32[16384]{0:T(1024)S(1)} %bitcast_clamp_fusion.5), kind=kCustom, calls=%fused_computation.2.clone.1 | custom fusion | bytes 4259840 | tf_op jit(solution)/shard_map/while/body/eval_jaxpr/gather | solution.py:79
  3010.8 57.9 %gather_fusion.2 = bf16[16384,64]{1,0:T(8,128)(2,1)} fusion(bf16[64,128]{0,1:T(8,128)(2,1)S(1)} %get-tuple-element.1641, s32[16384]{0:T(1024)S(1)} %bitcast_clamp_fusion.5), kind=kCustom, calls=%fused_computation.2.clone.1 | custom fusion | bytes 4259840 | tf_op jit(solution)/shard_map/while/body/eval_jaxpr/gather | solution.py:79
  3197.8 529.0 %while.116 = (s32[]{:T(128)}, f32[8,2,64,64]{3,2,1,0:T(8,128)S(1)}, f32[8,2,64,64]{3,2,1,0:T(8,128)S(1)}, f32[8,2,1,64,64]{4,3,2,1,0:T(8,128)}, f32[8,2,64,64]{3...) while((s32[]{:T(128)}, f32[8,2,64,64]{3,2,1,0:T(8,128)S(1)}, ...), condition=%wide.region_19.20_spmd.clone, body=%wide.region_16.19_spmd.clone.sunk | while | flops 45138048 | bytes 26905756 | solution.py:263
  3879.8 295.4 %while.119 = (s32[]{:T(128)}, f32[8,1,128,64]{2,3,0,1:T(8,128)}, f32[8,2,64,64]{3,2,1,0:T(8,128)}, f32[8,2,64,64]{3,2,1,0:T(8,128)}, f32[8,2,1,64,64]{4,3,1,2,0:...) while((s32[]{:T(128)}, f32[8,1,128,64]{2,3,0,1:T(8,128)}, ...), condition=%wide.region_25.26_spmd.clone.clone, body=%wide.region_22.25_spmd.clone.clone.sunk | while | flops 24191236 | bytes 66619132 | solution.py:228
  4230.4 172.8 %all-reduce.44.cloned.1.call-done = (f32[512,64]{0,1:T(8,128)}, f32[512,64]{0,1:T(8,128)}, f32[2,512,64]{1,2,0:T(8,128)}, f32[512,1024]{1,0:T(8,128)}, f32[512,2048]{1,0:T(8,128)}, /*index=5*/f32[2048,512]{1,0:T(8,128)}) async-done(((f32[512,64]{0,1:T(8,128)}, f32[512,64]{0,1:T(8,128)}, f32[2,512,64]{1,2,0:T(8,128)}, f32[512,1024]{1,0:T(8,128)}, f32[512,2048]{1,0:T(8,128)}, ...) | async-done | bytes 11010064 | tf_op jit(solution)/shard_map/psum | solution.py:434
  (1366 shorter events, 2866.9 us)
Async XLA Ops:
  7.2 1696.0 %copy-start = (bf16[2048,512]{1,0:T(8,128)(2,1)S(1)}, bf16[2048,512]{1,0:T(8,128)(2,1)}, u32[]{:S(2)}) copy-start(bf16[2048,512]{1,0:T(8,128)(2,1)} %param.49) | copy-start | bytes 6291460
  7.2 6.5 copy-start.14
  7.2 7.5 copy-start.78
  7.2 7.5 copy-start.76
  7.2 107.3 %all-gather.13.cloned.1.call-start = ((), (), s32[]{:S(2)}) async-start(), calls=%async_computation.2 | async-start | bytes 2359296 | tf_op jit(solution)/shard_map/all_gather | solution.py:12
  8.1 104.8 %copy-start.74 = (f32[512]{0:T(512)}, f32[512]{0:T(512)S(1)}, u32[]{:S(2)}) copy-start(f32[512]{0:T(512)S(1)} %exp.64) | copy-start | bytes 6148
  10.2 5.1 copy-start.17
  13.5 149.5 %all-gather.9.cloned.1.call-start = ((), (), s32[]{:S(2)}) async-start(), calls=%async_computation | async-start | bytes 2359296 | tf_op jit(solution)/shard_map/all_gather | solution.py:12
  13.8 1694.8 %copy-start.82 = (f32[128]{0:T(128)}, f32[128]{0:T(128)S(1)}, u32[]{:S(2)}) copy-start(f32[128]{0:T(128)S(1)} %broadcast_multiply_fusion.11) | copy-start | bytes 1540
  14.7 1693.1 %copy-start.80 = (f32[128]{0:T(128)}, f32[128]{0:T(128)S(1)}, u32[]{:S(2)}) copy-start(f32[128]{0:T(128)S(1)} %get-tuple-element.1192) | copy-start | bytes 1540
  107.9 105.1 %copy-start.13 = (f32[8,2,64,64]{3,2,1,0:T(8,128)}, f32[8,2,64,64]{3,2,1,0:T(8,128)S(1)}, u32[]{:S(2)}) copy-start(f32[8,2,64,64]{3,2,1,0:T(8,128)S(1)} %get-tuple-element.1989) | copy-start | bytes 786436
  107.9 105.1 %copy-start.35 = (bf16[8,1,128,64]{3,2,1,0:T(8,128)(2,1)}, bf16[8,1,128,64]{3,2,1,0:T(8,128)(2,1)S(1)}, u32[]{:S(2)}) copy-start(bf16[8,1,128,64]{3,2,1,0:T(8,128)(2,1)S(1)} %get-tuple-element.1999) | copy-start | bytes 393220
  110.9 102.1 %all-gather.11.cloned.1.call-start = ((), (), s32[]{:S(2)}) async-start(), calls=%async_computation.1 | async-start | bytes 2359296 | tf_op jit(solution)/shard_map/all_gather | solution.py:12
  112.6 3678.8 %all-gather.15.cloned.1.call-start = ((), (), s32[]{:S(2)}) async-start(), calls=%async_computation.3 | async-start | bytes 2359296 | tf_op jit(solution)/shard_map/all_gather | solution.py:12
  344.1 6.2 copy-start.26
  695.0 1005.1 %copy-start.15 = (bf16[1,128,512]{2,1,0:T(8,128)(2,1)S(1)}, bf16[1,128,512]{2,1,0:T(8,128)(2,1)}, u32[]{:S(2)}) copy-start(bf16[1,128,512]{2,1,0:T(8,128)(2,1)} %param.34) | copy-start | bytes 393220
  695.0 1005.1 %copy-start.87 = (f32[128]{0:T(128)S(1)}, f32[128]{0:T(128)}, u32[]{:S(2)}) copy-start(f32[128]{0:T(128)} %copy-done.86) | copy-start | bytes 1540
  695.0 1005.1 %copy-start.92 = (f32[512]{0:T(512)S(1)}, f32[512]{0:T(512)}, u32[]{:S(2)}) copy-start(f32[512]{0:T(512)} %param.42) | copy-start | bytes 6148
  695.0 1005.1 %copy-start.96 = (bf16[128]{0:T(256)(128)(2,1)S(1)}, bf16[128]{0:T(256)(128)(2,1)}, u32[]{:S(2)}) copy-start(bf16[128]{0:T(256)(128)(2,1)} %copy-done.95) | copy-start | bytes 772
  695.0 1005.4 %copy-start.101 = (f32[1024]{0:T(1024)S(1)}, f32[1024]{0:T(1024)}, u32[]{:S(2)}) copy-start(f32[1024]{0:T(1024)} %param.44) | copy-start | bytes 12292
  3197.8 532.6 %copy-start.27 = (f32[2,1,512,64]{2,3,1,0:T(8,128)S(1)}, f32[2,1,512,64]{2,3,1,0:T(8,128)}, u32[]{:S(2)}) copy-start(f32[2,1,512,64]{2,3,1,0:T(8,128)} %copy-done.26) | copy-start | bytes 786436
  3726.8 4.6 copy-start.54
  3733.3 4.8 copy-start.18
  3733.3 4.8 copy-start.19
  3738.1 5.3 copy-start.31
  3743.5 97.7 %all-gather.17.cloned.1.call-start = ((), (), s32[]{:S(2)}) async-start(), calls=%async_computation.4 | async-start | bytes 2359296 | tf_op jit(solution)/shard_map/all_gather | solution.py:12
  3744.1 659.1 %all-reduce.44.cloned.1.call-start = ((), (), s32[]{:S(2)}) async-start(), calls=%async_computation.5 | async-start | bytes 22020096 | tf_op jit(solution)/shard_map/psum | solution.py:434
  3746.2 6.6 copy-start.34
  3879.8 297.6 %copy-start.67 = (f32[1,512,64]{1,2,0:T(8,128)S(1)}, f32[1,512,64]{1,2,0:T(8,128)}, u32[]{:S(2)}) copy-start(f32[1,512,64]{1,2,0:T(8,128)} %get-tuple-element.1296) | copy-start | bytes 393220
  4185.1 44.4 %copy-start.30 = (f32[1,128,512]{2,1,0:T(8,128)S(1)}, f32[1,128,512]{2,1,0:T(8,128)}, u32[]{:S(2)}) copy-start(f32[1,128,512]{2,1,0:T(8,128)} %copy-done.29) | copy-start | bytes 786436
  4185.1 44.4 %copy-start.83 = (f32[128]{0:T(128)S(1)}, f32[128]{0:T(128)}, u32[]{:S(2)}) copy-start(f32[128]{0:T(128)} %copy-done.82) | copy-start | bytes 1540
  4185.1 44.4 %copy-start.88 = (f32[128]{0:T(128)S(1)}, f32[128]{0:T(128)}, u32[]{:S(2)}) copy-start(f32[128]{0:T(128)} %copy-done.86) | copy-start | bytes 1540
  (125 other events, 290.4 us)
Sparse Core Ops, SparseCore 0:
  13.6 51.9 all-gather.12
  111.0 51.9 all-gather.8
  165.1 47.7 all-gather.10
  3743.6 47.7 all-gather.14
  3793.4 47.7 all-gather.16
  4181.4 221.7 all-reduce.43
where the time goes:
time: 4440 us; the launch traced here: 4420 us
  local copies, waits for them, and re-layouts  2560 us (58%)
  matrix products  790 us (18%)
  other arithmetic  651 us (15%)
  waiting for transfers between devices  350 us (8%)
    gather x40, local copies, waits for them, and re-layouts, band_matrix(): picked = rows[..., jnp.maximum(lag_table, 0)]  2310 us
    all_gather x5, waiting for transfers between devices, prefix_2(): everything = jax.tree.map(lambda part: lax.all_gather(part, axis), value)  176 us
    dot_general x16, matrix products, per_group(): jnp.einsum('scn,cnt->stc', lead_one[1], weights[1], precision=PRECISE)  175 us
    dot_general x16, matrix products, per_group(): jnp.einsum('cn,cnt->ct', residue_one[1], weights[1], precision=PRECISE)  175 us
    dot_general x16, matrix products, per_group(): jnp.einsum('scn,cnt->stc', lead_one[0], weights[0], precision=PRECISE)  174 us
    dot_general x16, matrix products, per_group(): jnp.einsum('cn,cnt->ct', residue_one[0], weights[0], precision=PRECISE)  174 us
    psum x1, waiting for transfers between devices, on_device(): lax.psum((grad_norm1_gain, grad_norm1_bias, grad_ssm[0], grad_ssm[1], gra...  173 us
    reduce_sum x16, other arithmetic, powers(): angles = log_pole[1][..., None] * counts  160 us
  transfers between devices with their start and end apart: 6, of which 5 were waited for; matrix products, arithmetic and copies ran while one was open for 3% of the time, Pallas kernels for 0%

commit v1 on v0

v1 whole, which is shorter than its diff:
```python
import functools

import jax
import jax.numpy as jnp
from jax import lax
from jax.experimental import pallas as pl
from jax.experimental.pallas import tpu as pltpu
from jax.sharding import PartitionSpec as P

NORM_EPSILON = 1e-05
F32 = jnp.float32
BF16 = jnp.bfloat16
PRECISE = lax.Precision.HIGHEST
SERIES = 16
VMEM = pltpu.VMEM


def iota(shape, axis):
    return lax.broadcasted_iota(jnp.int32, shape, axis)


def is_left(shape):
    half = shape[-1] // 2
    return iota(shape, len(shape) - 1) < half


def swap(v):
    return pltpu.roll(v, v.shape[-1] // 2, v.ndim - 1)


def times(v, const):
    return v * const[0] + swap(v) * const[1]


def split(v):
    high = v.astype(BF16)
    return high, (v - high.astype(F32)).astype(BF16)


def nn(a, b):
    return lax.dot_general(a, b, (((1,), (0,)), ((), ())), preferred_element_type=F32)


def nt(a, b):
    return lax.dot_general(a, b, (((1,), (1,)), ((), ())), preferred_element_type=F32)


def tn(a, b):
    return lax.dot_general(a, b, (((0,), (0,)), ((), ())), preferred_element_type=F32)


def cmul(a, b):
    return a[0] * b[0] - a[1] * b[1], a[0] * b[1] + a[1] * b[0]


def twice(v):
    return jnp.concatenate([v, v], axis=-1)


def pole_parts(log_step, log_rate, frequency):
    step = jnp.exp(log_step)
    rate = jnp.exp(twice(log_rate))
    pole = (-rate, step * twice(frequency))
    phi = (jnp.full_like(rate, 0.0), jnp.zeros_like(rate))
    slope = (jnp.zeros_like(rate), jnp.zeros_like(rate))
    fact = [1.0]
    for k in range(1, SERIES + 2):
        fact.append(fact[-1] * k)
    for k in range(SERIES, -1, -1):
        phi = cmul(phi, pole)
        phi = (phi[0] + 1.0 / fact[k + 1], phi[1])
    for k in range(SERIES, 0, -1):
        slope = cmul(slope, pole)
        slope = (slope[0] + k / fact[k + 1], slope[1])
    grow = cmul(pole, phi)
    z = (1.0 + grow[0], grow[1])
    return step, rate, z, phi, slope


def as_const(value):
    sign = jnp.where(is_left(value[0].shape), -1.0, 1.0)
    return value[0], value[1] * sign


def packed(value):
    return jnp.where(is_left(value[0].shape), value[0], value[1])


def ssm_setup(chans, rows, refs, consts, base, q_ref, t_ref):
    ls, lr, fr, coef, skip = refs
    step, rate, z, phi, slope = pole_parts(ls[...], lr[...], fr[...])
    b = (twice(coef[0]), twice(coef[1]))
    residue = cmul(b, (step * phi[0], step * phi[1]))
    power = (jnp.ones_like(rate), jnp.zeros_like(rate))
    for r in range(8):
        base[r] = packed(power)
        power = cmul(power, z)
    slot = 0

    def keep(value):
        nonlocal slot
        c = as_const(value)
        consts[2 * slot] = c[0]
        consts[2 * slot + 1] = c[1]
        slot += 1

    for k in range(4):
        keep(power)
        power = cmul(power, power)
    for k in range((rows - 1).bit_length()):
        keep(power)
        power = cmul(power, power)
    lead = cmul(residue, z)
    lead = (2.0 * lead[0], 2.0 * lead[1])
    sign = jnp.where(is_left(rate.shape), 1.0, -1.0)
    consts[2 * slot] = lead[0] * sign
    consts[2 * slot + 1] = -lead[1]
    slot += 1
    kern = jnp.where(is_left(rate.shape), 2.0 * residue[0], -2.0 * residue[1])
    kern_high = kern.astype(BF16).astype(F32)
    consts[2 * slot] = kern_high
    consts[2 * slot + 1] = kern - kern_high
    return slot


def row_of(ref, index, chan):
    return ref[index, pl.ds(chan, 1), :]


def const_of(consts, slot, chan):
    return row_of(consts, 2 * slot, chan), row_of(consts, 2 * slot + 1, chan)


def make_powers(chan, chans, consts, kern_slot, base_flat, q_ref, taps_ref):
    powers = base_flat[pl.ds(chan, 8, stride=chans), :]
    for k in range(4):
        powers = jnp.concatenate([powers, times(powers, const_of(consts, k, chan))], axis=0)
    q_high, q_rest = split(powers)
    q_ref[chan, :128, :] = q_high
    q_ref[chan, 128:, :] = q_rest
    taps = jnp.concatenate([row_of(consts, 2 * kern_slot, chan), row_of(consts, 2 * kern_slot + 1, chan)], axis=0)
    kern = nt(twice(taps.astype(BF16)), jnp.concatenate([q_high, q_rest], axis=1))
    taps_ref[pl.ds(chan, 1), :] = kern[0:1] + kern[1:2]


def shift_taps(skip, taps_ref, base):
    taps = taps_ref[...]
    taps = taps + jnp.where(iota(taps.shape, 1) == 0, skip[...], 0.0)
    for r in range(8):
        base[r] = taps if r == 7 else pltpu.roll(taps, 7 - r, 1)


def make_band(chan, chans, base_flat, t_ref):
    tile = base_flat[pl.ds(chan, 8, stride=chans), :]
    band = jnp.concatenate([pltpu.roll(tile, 120 - 8 * m, 1) if m < 15 else tile for m in range(16)], axis=0)
    band = jnp.where(iota((128, 128), 0) + iota((128, 128), 1) >= 127, band, 0.0)
    t_high, t_rest = split(band)
    t_ref[chan, :128, :] = t_high
    t_ref[chan, 128:, :] = t_rest


def scan(v, consts, first, chan, reverse):
    rows = v.shape[0]
    places = iota(v.shape, 0)

    def moved(x, d):
        if reverse:
            return jnp.where(places < rows - d, pltpu.roll(x, rows - d, 0), 0.0)
        return jnp.where(places >= d, pltpu.roll(x, d, 0), 0.0)

    v = moved(v, 1)
    d, k = 1, 0
    while d < rows:
        v = v + times(moved(v, d), const_of(consts, first + k, chan))
        d, k = 2 * d, k + 1
    return v


def wide(chan, q_ref, t_ref):
    return jnp.concatenate([q_ref[chan], t_ref[chan]], axis=1)


def far_part(lead, chan, q_ref):
    rows = lead.shape[0]
    high, rest = split(lead)
    both = twice(jnp.concatenate([high, rest], axis=0))
    out = nt(both, jnp.concatenate([q_ref[chan, :128, :], q_ref[chan, 128:, :]], axis=1))
    return out[:rows] + out[rows:]


def forward_channel(chan, chans, rows, consts, lead_slot, x_flat, q_ref, t_ref, h_ref, y_flat):
    u = x_flat[pl.ds(chan, rows, stride=chans), :]
    out = nn(twice(u.astype(BF16)), wide(chan, q_ref, t_ref))
    h = scan(out[:, :128], consts, 4, chan, False)
    h_ref[chan] = h
    far = far_part(times(h, const_of(consts, lead_slot, chan)), chan, q_ref)
    y_flat[pl.ds(chan, rows, stride=chans), :] = out[:, 128:] + far


def backward_channel(chan, chans, rows, consts, lead_slot, x_flat, dy_flat, q_ref, t_ref, h_ref, dx_flat, a_ref, b_ref, g_ref):
    u = x_flat[pl.ds(chan, rows, stride=chans), :]
    dy = dy_flat[pl.ds(chan, rows, stride=chans), :]
    places = iota((1, 128), 1).astype(F32)
    high = dy.astype(BF16).astype(F32)
    left = twice(jnp.concatenate([high, dy - high, dy * places, u * places], axis=0).astype(BF16))
    out = nn(left, wide(chan, q_ref, t_ref))
    near = out[:rows, 128:] + out[rows : 2 * rows, 128:]
    d0 = out[:rows, :128] + out[rows : 2 * rows, :128]
    d1 = out[2 * rows : 3 * rows, :128]
    s1 = out[3 * rows :, :128]
    h = h_ref[chan]
    decay = const_of(consts, 4, chan)
    h1 = scan(s1 + 128.0 * times(h, decay), consts, 4, chan, False)
    e = scan(d0, consts, 4, chan, True)
    far = far_part(times(e, const_of(consts, lead_slot, chan)), chan, q_ref)
    dx_flat[pl.ds(chan, rows, stride=chans), :] = near + far
    mask = is_left(h.shape)

    def prod(p, q):
        q_swap = swap(q)
        return p * jnp.where(mask, q, q_swap) + swap(p) * jnp.where(mask, -q_swap, q)

    a_far = jnp.sum(prod(d0, h), axis=0, keepdims=True)
    b_far = a_far + jnp.sum(prod(d1, h) + prod(d0, h1), axis=0, keepdims=True)
    pairs = tn(u.astype(BF16), dy.astype(BF16))
    skew = pltpu.roll(pairs, 1, 1, stride=1, stride_axis=0)
    skew = jnp.where(iota((128, 128), 1) <= iota((128, 128), 0), skew, 0.0)
    lags = jnp.sum(skew, axis=0, keepdims=True)
    g_ref[pl.ds(chan, 1), :] = lags
    rows4 = jnp.concatenate([lags, lags * places], axis=0)
    high, rest = split(rows4)
    near_sums = nn(jnp.concatenate([jnp.concatenate([high, rest], axis=0)] * 2, axis=1), q_ref[chan])
    a_ref[pl.ds(chan, 1), :] = near_sums[0:1] + near_sums[2:3]
    b_ref[pl.ds(chan, 1), :] = near_sums[1:2] + near_sums[3:4]
    a_ref[pl.ds(chans + chan, 1), :] = a_far
    b_ref[pl.ds(chans + chan, 1), :] = b_far


def finish(chans, refs, a_ref, b_ref, g_ref):
    ls, lr, fr, coef, skip = refs
    step, rate, z, phi, slope = pole_parts(ls[...], lr[...], fr[...])
    b = (twice(coef[0]), twice(coef[1]))

    def dup(v):
        left = is_left(v.shape)
        moved = swap(v)
        return jnp.where(left, v, moved), jnp.where(left, moved, v)

    def total(ref):
        near, far = dup(ref[:chans, :]), dup(ref[chans:, :])
        far = cmul(far, z)
        return near[0] + far[0], near[1] + far[1]

    a, bb = total(a_ref), total(b_ref)
    residue = cmul(b, (step * phi[0], step * phi[1]))
    g_res = (2.0 * a[0], -2.0 * a[1])
    rb = cmul(residue, bb)
    g_pole = (2.0 * rb[0], -2.0 * rb[1])
    conj = lambda v: (v[0], -v[1])
    g_coef = cmul(conj((step * phi[0], step * phi[1])), g_res)
    bs = cmul(b, (step * slope[0], step * slope[1]))
    more = cmul(conj(bs), g_res)
    g_pole = (g_pole[0] + more[0], g_pole[1] + more[1])
    d_rate = -rate * g_pole[0]
    d_freq = step * g_pole[1]
    by_step = cmul(conj(cmul(b, phi)), g_res)[0] + g_pole[1] * twice(fr[...])
    left = is_left(by_step.shape)
    d_step = step * jnp.sum(jnp.where(left, by_step, 0.0), axis=1, keepdims=True)
    return jnp.where(left, d_rate, d_freq), jnp.where(left, g_coef[0], g_coef[1]), d_step, g_ref[:, 0:1]


def forward_kernel(chans, rows, x_ref, ls, lr, fr, coef, skip, y_ref, q_ref, t_ref, h_ref, consts, base, taps):
    refs = (ls, lr, fr, coef, skip)
    kern_slot = ssm_setup(chans, rows, refs, consts, base, q_ref, t_ref)
    base_flat = base.reshape(8 * chans, 128)
    x_flat = x_ref.reshape(rows * chans, 128)
    y_flat = y_ref.reshape(rows * chans, 128)

    def make(chan, carry):
        make_powers(chan, chans, consts, kern_slot, base_flat, q_ref, taps)
        return carry

    lax.fori_loop(0, chans, make, 0, unroll=4)
    shift_taps(skip, taps, base)

    def band(chan, carry):
        make_band(chan, chans, base_flat, t_ref)
        return carry

    lax.fori_loop(0, chans, band, 0, unroll=4)

    def go(chan, carry):
        forward_channel(chan, chans, rows, consts, kern_slot - 1, x_flat, q_ref, t_ref, h_ref, y_flat)
        return carry

    lax.fori_loop(0, chans, go, 0, unroll=4)


def backward_kernel(chans, rows, x_ref, dy_ref, q_ref, t_ref, h_ref, consts, ls, lr, fr, coef, skip, dx_ref, rf_ref, co_ref, st_ref, sk_ref, a_ref, b_ref, g_ref):
    refs = (ls, lr, fr, coef, skip)
    x_flat = x_ref.reshape(rows * chans, 128)
    dy_flat = dy_ref.reshape(rows * chans, 128)
    dx_flat = dx_ref.reshape(rows * chans, 128)
    lead_slot = consts.shape[0] // 2 - 2

    def go(chan, carry):
        backward_channel(chan, chans, rows, consts, lead_slot, x_flat, dy_flat, q_ref, t_ref, h_ref, dx_flat, a_ref, b_ref, g_ref)
        return carry

    lax.fori_loop(0, chans, go, 0, unroll=4)
    out = finish(chans, refs, a_ref, b_ref, g_ref)
    rf_ref[...] = out[0]
    co_ref[...] = out[1]
    st_ref[...] = out[2]
    sk_ref[...] = out[3]


def n_consts(rows):
    return 2 * (4 + (rows - 1).bit_length() + 2)


def ssm_forward(x, params):
    rows, chans, _ = x.shape
    shapes = [
        jax.ShapeDtypeStruct(x.shape, F32),
        jax.ShapeDtypeStruct((chans, 256, 128), BF16),
        jax.ShapeDtypeStruct((chans, 256, 128), BF16),
        jax.ShapeDtypeStruct((chans, rows, 128), F32),
        jax.ShapeDtypeStruct((n_consts(rows), chans, 128), F32),
    ]
    return pl.pallas_call(
        functools.partial(forward_kernel, chans, rows),
        out_shape=shapes,
        in_specs=[pl.BlockSpec(memory_space=VMEM)] * 6,
        out_specs=[pl.BlockSpec(memory_space=VMEM)] * 5,
        scratch_shapes=[VMEM((8, chans, 128), F32), VMEM((chans, 128), F32)],
        compiler_params=pltpu.CompilerParams(vmem_limit_bytes=50 * 2**20),
    )(x, *params)


def ssm_backward(x, dy, saved, params):
    rows, chans, _ = x.shape
    shapes = [
        jax.ShapeDtypeStruct(x.shape, F32),
        jax.ShapeDtypeStruct((chans, 128), F32),
        jax.ShapeDtypeStruct((chans, 128), F32),
        jax.ShapeDtypeStruct((chans, 1), F32),
        jax.ShapeDtypeStruct((chans, 1), F32),
    ]
    return pl.pallas_call(
        functools.partial(backward_kernel, chans, rows),
        out_shape=shapes,
        in_specs=[pl.BlockSpec(memory_space=VMEM)] * 11,
        out_specs=[pl.BlockSpec(memory_space=VMEM)] * 5,
        scratch_shapes=[VMEM((2 * chans, 128), F32), VMEM((2 * chans, 128), F32), VMEM((chans, 128), F32)],
        compiler_params=pltpu.CompilerParams(vmem_limit_bytes=50 * 2**20),
    )(x, dy, *saved, *params)


def layer_norm(values, gain, shift):
    center = values - jnp.mean(values, axis=-1, keepdims=True)
    scale = lax.rsqrt(jnp.mean(center * center, axis=-1, keepdims=True) + NORM_EPSILON)
    normed = center * scale
    return (normed * gain + shift, normed, scale)


def norm_back(grad_out, gain, normed, scale):
    scaled = grad_out * gain
    return scale * (
        scaled
        - jnp.mean(scaled, axis=-1, keepdims=True)
        - normed * jnp.mean(scaled * normed, axis=-1, keepdims=True)
    )


def token_sum(values):
    return jnp.sum(values, axis=0)


def dot(spec, a, b):
    return jnp.einsum(spec, a, b, preferred_element_type=F32)


def to_channels(v, blocks):
    rows, width = v.shape
    parts = v.T.reshape(blocks, width // blocks, rows)
    return lax.all_to_all(parts, "blk", 0, 0)


def to_tokens(v):
    parts = lax.all_to_all(v, "blk", 0, 0)
    return parts.reshape(-1, v.shape[-1]).T


def on_device(block_in, seq_lengths, norm1_gain, norm1_bias, log_step, log_rate, frequency, out_coef, skip_gain, glu_weight, glu_bias, norm2_gain, norm2_bias, ffn_in, ffn_in_bias, ffn_out, ffn_out_bias, cotangent):
    _, block_rows, channels = block_in.shape
    blocks = lax.axis_size("blk")
    mine = channels // blocks
    start = lax.axis_index("blk") * mine
    inputs = block_in[0].astype(F32)
    places = lax.axis_index("blk") * block_rows + jnp.arange(block_rows, dtype=jnp.int32)
    live = (places < seq_lengths[0]).astype(F32)[:, None]
    normed_in, unit_in, scale_in = layer_norm(inputs, norm1_gain, norm1_bias)
    mixed = normed_in.astype(BF16).astype(F32) * live
    cut = lambda v, axis: lax.dynamic_slice_in_dim(v, start, mine, axis)
    params = (cut(log_step[:, None], 0), cut(log_rate, 0), cut(frequency, 0), cut(out_coef, 1), cut(skip_gain[:, None], 0))
    x = to_channels(mixed[::-1], blocks)
    y, *saved = ssm_forward(x, params)
    conv_out = to_tokens(y)
    gelu_out = jax.nn.gelu(conv_out).astype(BF16)
    glu_pre = dot("bd,de->be", gelu_out, glu_weight) + glu_bias
    glu_left = glu_pre[..., :channels]
    glu_gate = jax.nn.sigmoid(glu_pre[..., channels:])
    residual = inputs + live * glu_left * glu_gate
    normed_mid, unit_mid, scale_mid = layer_norm(residual, norm2_gain, norm2_bias)
    ffn_feed = normed_mid.astype(BF16)
    hidden_pre = dot("bd,df->bf", ffn_feed, ffn_in) + ffn_in_bias
    hidden = jax.nn.gelu(hidden_pre).astype(BF16)
    ffn_result = dot("bf,fd->bd", hidden, ffn_out) + ffn_out_bias
    block_out = (residual + live * ffn_result).astype(BF16)
    upstream = cotangent[0].astype(F32)
    grad_result = (live * upstream).astype(BF16)
    grad_ffn_out = dot("bf,bd->fd", hidden, grad_result)
    grad_ffn_out_bias = token_sum(grad_result.astype(F32))
    grad_hidden = dot("bd,fd->bf", grad_result, ffn_out)
    grad_pre = jax.vjp(jax.nn.gelu, hidden_pre)[1](grad_hidden)[0].astype(BF16)
    grad_ffn_in = dot("bd,bf->df", ffn_feed, grad_pre)
    grad_ffn_in_bias = token_sum(grad_pre.astype(F32))
    grad_feed = dot("bf,df->bd", grad_pre, ffn_in)
    grad_norm2_gain = token_sum(grad_feed * unit_mid)
    grad_norm2_bias = token_sum(grad_feed)
    grad_residual = upstream + norm_back(grad_feed, norm2_gain, unit_mid, scale_mid)
    grad_left = live * grad_residual
    grad_glu = jnp.concatenate([grad_left * glu_gate, grad_left * glu_left * glu_gate * (1.0 - glu_gate)], axis=-1).astype(BF16)
    grad_glu_weight = dot("bd,be->de", gelu_out, grad_glu)
    grad_glu_bias = token_sum(grad_glu.astype(F32))
    grad_gelu = dot("be,de->bd", grad_glu, glu_weight)
    grad_conv = jax.vjp(jax.nn.gelu, conv_out)[1](grad_gelu)[0]
    dx, rf, co, st, sk = ssm_backward(x, to_channels(grad_conv, blocks), saved, params)
    grad_normed_in = live * to_tokens(dx)[::-1]
    grad_norm1_gain = token_sum(grad_normed_in * unit_in)
    grad_norm1_bias = token_sum(grad_normed_in)
    grad_block_in = grad_residual + norm_back(grad_normed_in, norm1_gain, unit_in, scale_in)
    half = log_rate.shape[1]
    own = jnp.concatenate([rf, co, st, sk], axis=1)
    own = lax.all_gather(lax.psum(own, "dp"), "blk", axis=0, tiled=True)
    totals = lax.psum((grad_norm1_gain, grad_norm1_bias, grad_glu_weight, grad_glu_bias, grad_norm2_gain, grad_norm2_bias, grad_ffn_in, grad_ffn_in_bias, grad_ffn_out, grad_ffn_out_bias), ("dp", "blk"))
    return (
        block_out[None],
        grad_block_in[None],
        totals[0],
        totals[1],
        own[:, 4 * half],
        own[:, :half],
        own[:, half : 2 * half],
        jnp.stack([own[:, 2 * half : 3 * half], own[:, 3 * half : 4 * half]]),
        own[:, 4 * half + 1],
        *totals[2:],
    )


def solution(mesh):
    split_spec, whole = P("dp", "blk", None), P()
    return jax.shard_map(
        on_device,
        mesh=mesh,
        in_specs=(split_spec, P("dp")) + (whole,) * 15 + (split_spec,),
        out_specs=(split_spec, split_spec) + (whole,) * 15,
        check_vma=False,
    )
```

time: 4440 us -> 391 us (0.09)
  local copies, waits for them, and re-layouts: 2560 us -> 27.1 us
  matrix products: 790 us -> 18.2 us
  other arithmetic: 651 us -> 7.69 us
  waiting for transfers between devices: 350 us -> 161 us
  Pallas kernels: 0 us -> 59.2 us
  blocking collectives: 40.9 us -> 86.4 us
    gather x40 -> x0, local copies, waits for them, and re-layouts: 2310 us -> none  [band_matrix(): picked = rows[..., jnp.maximum(lag_table, 0)]]
    dot_general x153 -> x9, matrix products: 790 us -> 18.2 us  [dot(): return jnp.einsum(spec, a, b, preferred_element_type=F32)]
    all_gather x5 -> x0, waiting for transfers between devices: 176 us -> none  [prefix_2(): everything = jax.tree.map(lambda part: lax.all_gather(part, axis), value)]
    reduce_sum x20 -> x2, other arithmetic: 165 us -> 1.4 us  [token_sum(): return jnp.sum(values, axis=0)]
    dot_general x16 -> x0, other arithmetic: 150 us -> none  [the longest x8 80 us: per_group(): jnp.einsum('cts,btc->bsc', band_high, grad_rest, preferred_element_type=j...]
    mul x45 -> x1, other arithmetic: 143 us -> 1.05 us  [on_device(): mixed = normed_in.astype(BF16).astype(F32) * live]
    while x164 -> x0, local copies, waits for them, and re-layouts: 71.1 us -> none
    pallas_call x0 -> x2, Pallas kernels: none -> 59.2 us  [the longest x1 35.7 us: ssm_backward(): pl.pallas_call(functools.partial(backward_kernel, chans, rows), out_shape...]
  transfers between devices with their start and end apart: 6 -> 5, of which waited for: 5 -> 4; matrix products, arithmetic and copies ran while one was open for 3% -> 6% of each run, Pallas kernels for 0% -> 0%
where the time goes in v1:
time: 391 us; the launch traced here: 390 us
  waiting for transfers between devices  161 us (41%)
  blocking collectives  86.4 us (22%)
  Pallas kernels  59.2 us (15%)
  local copies, waits for them, and re-layouts  27.1 us (7%)
  matrix products  18.2 us (5%)
  between operations  15.3 us (4%)
  starting transfers between devices  15.1 us (4%)
  other arithmetic  7.69 us (2%)
    psum x1, waiting for transfers between devices, on_device(): lax.psum((grad_norm1_gain, grad_norm1_bias, grad_glu_weight, grad_glu_bia...  132 us
    psum x1, blocking collectives, on_device(): lax.psum((grad_norm1_gain, grad_norm1_bias, grad_glu_weight, grad_glu_bia...  39.9 us
    pallas_call x1, Pallas kernels, ssm_backward(): pl.pallas_call(functools.partial(backward_kernel, chans, rows), out_shape...  35.7 us
    all_gather x1, blocking collectives, on_device(): own = lax.all_gather(lax.psum(own, 'dp'), 'blk', axis=0, tiled=True)  34.3 us
    pallas_call x1, Pallas kernels, ssm_forward(): pl.pallas_call(functools.partial(forward_kernel, chans, rows), out_shape=...  23.5 us
    psum x1, waiting for transfers between devices, on_device(): own = lax.all_gather(lax.psum(own, 'dp'), 'blk', axis=0, tiled=True)  21.4 us
    dot_general x9, matrix products, dot(): return jnp.einsum(spec, a, b, preferred_element_type=F32)  18.2 us
    unnamed x79, local copies, waits for them, and re-layouts  16.7 us
  transfers between devices with their start and end apart: 5, of which 4 were waited for; matrix products, arithmetic and copies ran while one was open for 6% of the time, Pallas kernels for 0%

profile of v1, /device:TPU:0, one launch (start us, length us, event | category | flops | bytes accessed | tf_op | source)
XLA Modules:
  0.0 390.1 jit_solution(10774628408302378205)
XLA Ops:
  9.1 1.1 fusion.27
  12.2 7.3 %all-to-all-start = ((f32[8,64,128]{2,1,0:T(8,128)}), f32[8,64,128]{2,1,0:T(8,128)S(1)}, u32[]{:S(2)}, u32[]{:S(2)}) async-start(f32[8,64,128]{2,1,0:T(8,128)} %bitcast.3), calls=%async_computation | async-start | bytes 524288 | tf_op jit(solution)/shard_map/all_to_all | solution.py:387
  22.5 5.9 %all-to-all-done.x_ref = f32[8,64,128]{2,1,0:T(8,128)S(1)} async-done(((f32[8,64,128]{2,1,0:T(8,128)}), f32[8,64,128]{2,1,0:T(8,128)S(1)}, u32[]{:S(2)}, u32[]{:S(2)}) %all-to-all-start) | async-done | bytes 262176 | tf_op jit(solution)/shard_map/all_to_all | solution.py:387
  28.4 23.5 %shard_map.305 = (f32[8,64,128]{2,1,0:T(8,128)S(1)}, bf16[64,256,128]{2,1,0:T(8,128)(2,1)}, bf16[64,256,128]{2,1,0:T(8,128)(2,1)}, f32[64,8,128]{2,1,0:T(8,128)S(1)}, f32[18,64,128]{2,1,0:T(8,128)S(1)}) custom-call(f32[8,64,128]{2,1,0:T(8,128)S(1)} %all-to-all-done.x_ref, f32[64,1]{1,0:T(8,128)S(1)} %copy.58.ls, f32[64,64]{1,0:T(8,128)S(1)} %copy.73.lr, ...), custom_call_target="tpu_custom_call" | custom-call | tf_op jit(solution)/shard_map/pallas_call | solution.py:331
  51.9 12.2 %all_to_all.20 = f32[8,64,128]{2,1,0:T(8,128)} all-to-all(f32[8,64,128]{2,1,0:T(8,128)S(1)} %get-tuple-element.27), channel_id=1, replica_groups=mesh['dp'=4,'blk'=8] {'blk'}, dimensions={0} | all-to-all | bytes 524288 | tf_op jit(solution)/shard_map/all_to_all | solution.py:391
  64.1 1.8 copy.60
  65.9 1.8 convolution_add_fusion.1
  68.2 1.2 convolution_add_fusion
  69.4 1.7 convert_reduce_fusion
  71.2 1.5 multiply_reduce_fusion
  73.7 1.3 fusion.34
  74.9 1.8 copy.66
  76.7 3.6 all-to-all-start.2
  80.4 4.0 %fusion.57 = f32[512,2048]{1,0:T(8,128)} fusion(bf16[128,2048]{1,0:T(8,128)(2,1)} %copy-done.15, f32[128,512]{1,0:T(8,128)} %copy-done.3, f32[512]{0:T(512)S(1)} %copy-done.24, f32[512]{0:T(512)S(1)} %copy-done.22, f32[128]{0:T(128)} %copy-done.27, f32[128]{0:T(128)S(1)} %broadcast_multiply_fusion.4), kind=kOutput, calls=%fused_computation.101 | convolution fusion | flops 268763136 | bytes 4985856 | tf_op jit(solution)/shard_map/bd,bf->df/dot_general | solution.py:381
  84.4 2.7 fusion.49
  87.1 1.7 all-to-all-done.2.dy_ref
  89.8 35.7 %shard_map.306 = (f32[8,64,128]{2,1,0:T(8,128)}, f32[64,128]{1,0:T(8,128)S(1)}, f32[64,128]{1,0:T(8,128)S(1)}, f32[64,1]{1,0:T(8,128)S(1)}, f32[64,1]{1,0:T(8,128)S(1)}) custom-call(f32[8,64,128]{2,1,0:T(8,128)S(1)} %all-to-all-done.x_ref, f32[8,64,128]{2,1,0:T(8,128)S(1)} %all-to-all-done.2.dy_ref, bf16[64,256,128]{2,1,0:T(8,128)(2,1)} %get-tuple-element.28.q_ref, ...), custom_call_target="tpu_custom_call" | custom-call | tf_op jit(solution)/shard_map/pallas_call | solution.py:350
  126.2 2.8 fusion.46
  129.1 1.1 convert_reduce_fusion.1
  130.5 1.2 fusion.3
  131.7 4.2 %all-to-all-start.3 = ((f32[8,64,128]{2,1,0:T(8,128)}), f32[8,64,128]{2,1,0:T(8,128)}, u32[]{:S(2)}, u32[]{:S(2)}) async-start(f32[8,64,128]{2,1,0:T(8,128)} %get-tuple-element.32), calls=%async_computation.3 | async-start | bytes 524288 | tf_op jit(solution)/shard_map/all_to_all | solution.py:391
  135.9 21.4 %all-reduce.5.cloned.1.call-done = f32[64,258]{1,0:T(8,128)} async-done(((f32[64,258]{1,0:T(8,128)}), f32[64,258]{1,0:T(8,128)}) %all-reduce.5.cloned.1.call-update) | async-done | bytes 66064 | tf_op jit(solution)/shard_map/psum | solution.py:446
  157.3 34.3 %all_gather.3 = f32[512,258]{1,0:T(8,128)S(1)} all-gather(f32[64,258]{1,0:T(8,128)} %all-reduce.5.cloned.1.call-done), channel_id=1, replica_groups=mesh['dp'=4,'blk'=8] {'blk'}, dimensions={0}, use_global_device_ids=true | all-gather | bytes 594432 | tf_op jit(solution)/shard_map/all_gather | solution.py:446
  193.4 2.0 copy.72
  195.4 1.7 copy.71
  197.1 1.7 copy.70
  201.3 39.9 %all-reduce = (f32[512]{0:T(512)}, f32[512]{0:T(512)}, f32[1024]{0:T(1024)}, f32[512]{0:T(512)}, f32[512]{0:T(512)}, /*index=5*/f32[2048]{0:T(1024)}, f32[512]{0:T(512)}) all-reduce(f32[512]{0:T(512)S(1)} %get-tuple-element.75, f32[512]{0:T(512)S(1)} %get-tuple-element.79, ...), channel_id=1, replica_groups=mesh['dp'=4,'blk'=8] {'dp','blk'}, use_global_device_ids=true, to_apply=%region_9.0 | all-reduce | flops 5632 | bytes 45056 | tf_op jit(solution)/shard_map/psum | solution.py:447
  242.0 132.2 %all-reduce.7.cloned.1.call-done = (f32[512,1024]{1,0:T(8,128)}, f32[512,2048]{1,0:T(8,128)}, f32[2048,512]{1,0:T(8,128)}) async-done(((f32[512,1024]{1,0:T(8,128)}, f32[512,2048]{1,0:T(8,128)}, f32[2048,512]{1,0:T(8,128)}), (f32[512,1024]{1,0:T(8,128)}, f32[512,2048]{1,0:T(8,128)}, f32[2048,512]{1,0:T(8,128)})) %all-reduce.7.cloned.1.call-update) | async-done | bytes 10485776 | tf_op jit(solution)/shard_map/psum | solution.py:447
  374.2 3.3 copy.81
  377.5 2.1 copy.82
  379.6 1.6 copy-done.7
  381.2 2.0 copy.83
  (107 shorter events, 14.7 us)
Async XLA Ops:
  7.2 62.2 %copy-start = (bf16[2048,512]{1,0:T(8,128)(2,1)S(1)}, bf16[2048,512]{1,0:T(8,128)(2,1)}, u32[]{:S(2)}) copy-start(bf16[2048,512]{1,0:T(8,128)(2,1)} %param.33) | copy-start | bytes 6291460
  9.0 3.2 copy-start.25
  9.0 56.9 %copy-start.33 = (f32[1024]{0:T(1024)S(1)}, f32[1024]{0:T(1024)}, u32[]{:S(2)}) copy-start(f32[1024]{0:T(1024)} %param.28) | copy-start | bytes 12292
  10.2 2.1 copy-start.31
  12.2 16.2 %all-to-all-start = ((f32[8,64,128]{2,1,0:T(8,128)}), f32[8,64,128]{2,1,0:T(8,128)S(1)}, u32[]{:S(2)}, u32[]{:S(2)}) async-start(f32[8,64,128]{2,1,0:T(8,128)} %bitcast.3), calls=%async_computation | async-start | bytes 524288 | tf_op jit(solution)/shard_map/all_to_all | solution.py:387
  19.5 48.2 %copy-start.6 = (bf16[1,128,512]{2,1,0:T(8,128)(2,1)S(1)}, bf16[1,128,512]{2,1,0:T(8,128)(2,1)}, u32[]{:S(2)}) copy-start(bf16[1,128,512]{2,1,0:T(8,128)(2,1)} %param.18) | copy-start | bytes 393220
  51.9 17.5 %copy-start.1 = (f32[64,8,128]{2,1,0:T(8,128)}, f32[64,8,128]{2,1,0:T(8,128)S(1)}, u32[]{:S(2)}) copy-start(f32[64,8,128]{2,1,0:T(8,128)S(1)} %get-tuple-element.30.h_ref) | copy-start | bytes 786436
  51.9 16.2 %copy-start.22 = (f32[512]{0:T(512)S(1)}, f32[512]{0:T(512)}, u32[]{:S(2)}) copy-start(f32[512]{0:T(512)} %param.29) | copy-start | bytes 6148
  51.9 16.2 %copy-start.24 = (f32[512]{0:T(512)S(1)}, f32[512]{0:T(512)}, u32[]{:S(2)}) copy-start(f32[512]{0:T(512)} %param.30) | copy-start | bytes 6148
  65.9 2.3 copy-start.5
  67.9 4.7 %copy-start.3 = (f32[128,512]{1,0:T(8,128)}, f32[128,512]{1,0:T(8,128)S(1)}, u32[]{:S(2)}) copy-start(f32[128,512]{1,0:T(8,128)S(1)} %get-tuple-element.95) | copy-start | bytes 786436
  68.2 4.5 %copy-start.27 = (f32[128]{0:T(128)}, f32[128]{0:T(128)S(1)}, u32[]{:S(2)}) copy-start(f32[128]{0:T(128)S(1)} %add_rsqrt_fusion) | copy-start | bytes 1540
  69.4 1.8 copy-start.9
  71.2 2.5 copy-start.14
  71.2 2.5 copy-start.21
  72.9 3.8 copy-start.12
  76.7 12.1 %all-to-all-start.2 = ((f32[8,64,128]{2,1,0:T(8,128)}), f32[8,64,128]{2,1,0:T(8,128)S(1)}, u32[]{:S(2)}, u32[]{:S(2)}) async-start(f32[8,64,128]{2,1,0:T(8,128)} %bitcast.88), calls=%async_computation.2 | async-start | bytes 524288 | tf_op jit(solution)/shard_map/all_to_all | solution.py:387
  80.3 77.0 %all-reduce.5.cloned.1.call-start = ((), (), s32[]{:S(2)}) async-start(), calls=%async_computation.4 | async-start | bytes 196608 | tf_op jit(solution)/shard_map/psum | solution.py:446
  80.4 4.0 %copy-start.10 = (f32[128,2048]{1,0:T(8,128)S(1)}, f32[128,2048]{1,0:T(8,128)}, u32[]{:S(2)}) copy-start(f32[128,2048]{1,0:T(8,128)} %copy-done.9) | copy-start | bytes 3145732
  80.4 4.0 %copy-start.17 = (bf16[1,128,512]{2,1,0:T(8,128)(2,1)S(1)}, bf16[1,128,512]{2,1,0:T(8,128)(2,1)}, u32[]{:S(2)}) copy-start(bf16[1,128,512]{2,1,0:T(8,128)(2,1)} %param.35) | copy-start | bytes 393220
  126.2 248.0 %all-reduce.7.cloned.1.call-start = ((), (), s32[]{:S(2)}) async-start(), calls=%async_computation.5 | async-start | bytes 20971520 | tf_op jit(solution)/shard_map/psum | solution.py:447
  131.7 68.0 %all-to-all-start.3 = ((f32[8,64,128]{2,1,0:T(8,128)}), f32[8,64,128]{2,1,0:T(8,128)}, u32[]{:S(2)}, u32[]{:S(2)}) async-start(f32[8,64,128]{2,1,0:T(8,128)} %get-tuple-element.32), calls=%async_computation.3 | async-start | bytes 524288 | tf_op jit(solution)/shard_map/all_to_all | solution.py:391
  192.5 8.4 %copy-start.18 = (bf16[1,128,512]{2,1,0:T(8,128)(2,1)S(1)}, bf16[1,128,512]{2,1,0:T(8,128)(2,1)}, u32[]{:S(2)}) copy-start(bf16[1,128,512]{2,1,0:T(8,128)(2,1)} %param.35) | copy-start | bytes 393220
  192.5 8.4 %copy-start.23 = (f32[512]{0:T(512)S(1)}, f32[512]{0:T(512)}, u32[]{:S(2)}) copy-start(f32[512]{0:T(512)} %param.20) | copy-start | bytes 6148
  192.5 8.4 %copy-start.26 = (f32[128]{0:T(128)S(1)}, f32[128]{0:T(128)}, u32[]{:S(2)}) copy-start(f32[128]{0:T(128)} %copy-done.25) | copy-start | bytes 1540
  192.5 8.4 %copy-start.32 = (f32[128]{0:T(128)S(1)}, f32[128]{0:T(128)}, u32[]{:S(2)}) copy-start(f32[128]{0:T(128)} %copy-done.31) | copy-start | bytes 1540
  193.4 7.9 %copy-start.28 = (f32[512]{0:T(512)S(1)}, f32[512]{0:T(512)}, u32[]{:S(2)}) copy-start(f32[512]{0:T(512)} %get-tuple-element.73) | copy-start | bytes 6148
  193.4 7.9 %copy-start.29 = (f32[512]{0:T(512)S(1)}, f32[512]{0:T(512)}, u32[]{:S(2)}) copy-start(f32[512]{0:T(512)} %get-tuple-element.80) | copy-start | bytes 6148
  193.4 7.9 %copy-start.30 = (f32[2048]{0:T(1024)S(1)}, f32[2048]{0:T(1024)}, u32[]{:S(2)}) copy-start(f32[2048]{0:T(1024)} %get-tuple-element.101) | copy-start | bytes 24580
  193.4 47.8 %copy-start.13 = (f32[128,512]{1,0:T(8,128)S(1)}, f32[128,512]{1,0:T(8,128)}, u32[]{:S(2)}) copy-start(f32[128,512]{1,0:T(8,128)} %copy-done.12) | copy-start | bytes 786436
  374.2 3.3 copy-start.8
  377.5 3.7 copy-start.7
  (8 other events, 9.7 us)
Sparse Core Ops, SparseCore 0:
  126.3 30.9 all-reduce.4
  165.0 209.1 all-reduce.6

commit v2 on v1

v2 whole, which is shorter than its diff:
```python
import functools

import jax
import jax.numpy as jnp
from jax import lax
from jax.experimental import pallas as pl
from jax.experimental.pallas import tpu as pltpu
from jax.sharding import PartitionSpec as P

NORM_EPSILON = 1e-05
F32 = jnp.float32
BF16 = jnp.bfloat16
PRECISE = lax.Precision.HIGHEST
SERIES = 16
GROUP = 16
LINK_SEMS = 128
VMEM = pltpu.VMEM


def iota(shape, axis):
    return lax.broadcasted_iota(jnp.int32, shape, axis)


def is_left(shape):
    half = shape[-1] // 2
    return iota(shape, len(shape) - 1) < half


def swap(v):
    return pltpu.roll(v, v.shape[-1] // 2, v.ndim - 1)


def times(v, const):
    return v * const[0] + swap(v) * const[1]


def split(v):
    high = v.astype(BF16)
    return high, (v - high.astype(F32)).astype(BF16)


def nn(a, b):
    return lax.dot_general(a, b, (((1,), (0,)), ((), ())), preferred_element_type=F32)


def nt(a, b):
    return lax.dot_general(a, b, (((1,), (1,)), ((), ())), preferred_element_type=F32)


def tn(a, b):
    return lax.dot_general(a, b, (((0,), (0,)), ((), ())), preferred_element_type=F32)


def cmul(a, b):
    return a[0] * b[0] - a[1] * b[1], a[0] * b[1] + a[1] * b[0]


def twice(v):
    return jnp.concatenate([v, v], axis=-1)


def pole_parts(log_step, log_rate, frequency):
    step = jnp.exp(log_step)
    rate = jnp.exp(twice(log_rate))
    pole = (-rate, step * twice(frequency))
    phi = (jnp.zeros_like(rate), jnp.zeros_like(rate))
    slope = (jnp.zeros_like(rate), jnp.zeros_like(rate))
    fact = [1.0]
    for k in range(1, SERIES + 2):
        fact.append(fact[-1] * k)
    for k in range(SERIES, -1, -1):
        phi = cmul(phi, pole)
        phi = (phi[0] + 1.0 / fact[k + 1], phi[1])
    for k in range(SERIES, 0, -1):
        slope = cmul(slope, pole)
        slope = (slope[0] + k / fact[k + 1], slope[1])
    grow = cmul(pole, phi)
    z = (1.0 + grow[0], grow[1])
    return step, rate, z, phi, slope


def as_const(value):
    sign = jnp.where(is_left(value[0].shape), -1.0, 1.0)
    return value[0], value[1] * sign


def packed(value):
    return jnp.where(is_left(value[0].shape), value[0], value[1])


def ssm_setup(rows, ssm, consts, base):
    log_step, log_rate, frequency, coef = ssm
    step, rate, z, phi, slope = pole_parts(log_step, log_rate, frequency)
    b = (twice(coef[0]), twice(coef[1]))
    residue = cmul(b, (step * phi[0], step * phi[1]))
    power = (jnp.ones_like(rate), jnp.zeros_like(rate))
    for r in range(8):
        base[r] = packed(power)
        power = cmul(power, z)
    slot = 0

    def keep(value):
        nonlocal slot
        c = as_const(value)
        consts[2 * slot] = c[0]
        consts[2 * slot + 1] = c[1]
        slot += 1

    for k in range(4):
        keep(power)
        power = cmul(power, power)
    for k in range((rows - 1).bit_length()):
        keep(power)
        power = cmul(power, power)
    lead = cmul(residue, z)
    lead = (2.0 * lead[0], 2.0 * lead[1])
    sign = jnp.where(is_left(rate.shape), 1.0, -1.0)
    consts[2 * slot] = lead[0] * sign
    consts[2 * slot + 1] = -lead[1]
    slot += 1
    kern = jnp.where(is_left(rate.shape), 2.0 * residue[0], -2.0 * residue[1])
    kern_high = kern.astype(BF16).astype(F32)
    consts[2 * slot] = kern_high
    consts[2 * slot + 1] = kern - kern_high
    return slot


def row_of(ref, index, chan):
    return ref[index, pl.ds(chan, 1), :]


def const_of(consts, slot, chan):
    return row_of(consts, 2 * slot, chan), row_of(consts, 2 * slot + 1, chan)


def make_powers(group, chans, consts, kern_slot, base_flat, q_ref, taps_ref):
    every = [base_flat[pl.ds(chan, 8, stride=chans), :] for chan in group]
    for k in range(4):
        every = [
            jnp.concatenate([powers, times(powers, const_of(consts, k, chan))], axis=0)
            for chan, powers in zip(group, every)
        ]
    parts = [split(powers) for powers in every]
    for chan, (high, rest) in zip(group, parts):
        q_ref[chan, :128, :] = high
        q_ref[chan, 128:, :] = rest
    kerns = []
    for chan, (high, rest) in zip(group, parts):
        taps = [row_of(consts, 2 * kern_slot + k, chan) for k in range(2)]
        taps = jnp.concatenate([taps[0], taps[1]], axis=0).astype(BF16)
        kerns.append(nt(twice(taps), jnp.concatenate([high, rest], axis=1)))
    for chan, kern in zip(group, kerns):
        taps_ref[pl.ds(chan, 1), :] = kern[0:1] + kern[1:2]


def shift_taps(skip, taps_ref, base):
    taps = taps_ref[...]
    taps = taps + jnp.where(iota(taps.shape, 1) == 0, skip, 0.0)
    for r in range(8):
        base[r] = taps if r == 7 else pltpu.roll(taps, 7 - r, 1)


def make_band(group, chans, base_flat, t_ref):
    for chan in group:
        tile = base_flat[pl.ds(chan, 8, stride=chans), :]
        band = jnp.concatenate([pltpu.roll(tile, 120 - 8 * m, 1) if m < 15 else tile for m in range(16)], axis=0)
        band = jnp.where(iota((128, 128), 0) + iota((128, 128), 1) >= 127, band, 0.0)
        t_high, t_rest = split(band)
        t_ref[chan, :128, :] = t_high
        t_ref[chan, 128:, :] = t_rest


def scan(values, consts, first, group, reverse):
    rows = values[0].shape[0]
    places = iota(values[0].shape, 0)

    def moved(x, d):
        if reverse:
            return jnp.where(places < rows - d, pltpu.roll(x, rows - d, 0), 0.0)
        return jnp.where(places >= d, pltpu.roll(x, d, 0), 0.0)

    values = [moved(v, 1) for v in values]
    d, k = 1, 0
    while d < rows:
        values = [v + times(moved(v, d), const_of(consts, first + k, chan)) for v, chan in zip(values, group)]
        d, k = 2 * d, k + 1
    return values


def wide(chan, q_ref, t_ref):
    return jnp.concatenate([q_ref[chan], t_ref[chan]], axis=1)


def far_parts(states, consts, lead_slot, group, q_ref):
    rows = states[0].shape[0]
    outs = []
    for chan, state in zip(group, states):
        high, rest = split(times(state, const_of(consts, lead_slot, chan)))
        both = twice(jnp.concatenate([high, rest], axis=0))
        outs.append(nt(both, jnp.concatenate([q_ref[chan, :128, :], q_ref[chan, 128:, :]], axis=1)))
    return [out[:rows] + out[rows:] for out in outs]


def forward_group(group, chans, rows, consts, lead_slot, x_flat, q_ref, t_ref, h_ref, y_flat):
    outs = [
        nn(twice(x_flat[pl.ds(chan, rows, stride=chans), :].astype(BF16)), wide(chan, q_ref, t_ref))
        for chan in group
    ]
    states = scan([out[:, :128] for out in outs], consts, 4, group, False)
    for chan, state in zip(group, states):
        h_ref[chan] = state
    fars = far_parts(states, consts, lead_slot, group, q_ref)
    for chan, out, far in zip(group, outs, fars):
        y_flat[pl.ds(chan, rows, stride=chans), :] = out[:, 128:] + far


def backward_group(group, chans, rows, consts, lead_slot, x_flat, dy_flat, q_ref, t_ref, h_ref, dx_flat, a_ref, b_ref, g_ref):
    places = iota((1, 128), 1).astype(F32)
    us = [x_flat[pl.ds(chan, rows, stride=chans), :] for chan in group]
    dys = [dy_flat[pl.ds(chan, rows, stride=chans), :] for chan in group]
    outs = []
    for chan, u, dy in zip(group, us, dys):
        high = dy.astype(BF16).astype(F32)
        left = twice(jnp.concatenate([high, dy - high, dy * places, u * places], axis=0).astype(BF16))
        outs.append(nn(left, wide(chan, q_ref, t_ref)))
    pairs = [tn(u.astype(BF16), dy.astype(BF16)) for u, dy in zip(us, dys)]
    d0s = [out[:rows, :128] + out[rows : 2 * rows, :128] for out in outs]
    d1s = [out[2 * rows : 3 * rows, :128] for out in outs]
    hs = [h_ref[chan] for chan in group]
    ends = scan(d0s, consts, 4, group, True)
    fars = far_parts(ends, consts, lead_slot, group, q_ref)
    for chan, out, far in zip(group, outs, fars):
        dx_flat[pl.ds(chan, rows, stride=chans), :] = out[:rows, 128:] + out[rows : 2 * rows, 128:] + far
    h1s = scan(
        [out[3 * rows :, :128] + 128.0 * times(h, const_of(consts, 4, chan)) for chan, out, h in zip(group, outs, hs)],
        consts, 4, group, False,
    )
    mask = is_left(hs[0].shape)

    def prod(p, q):
        q_swap = swap(q)
        return p * jnp.where(mask, q, q_swap) + swap(p) * jnp.where(mask, -q_swap, q)

    for chan, d0, d1, h, h1 in zip(group, d0s, d1s, hs, h1s):
        a_far = jnp.sum(prod(d0, h), axis=0, keepdims=True)
        b_far = a_far + jnp.sum(prod(d1, h) + prod(d0, h1), axis=0, keepdims=True)
        a_ref[pl.ds(chans + chan, 1), :] = a_far
        b_ref[pl.ds(chans + chan, 1), :] = b_far
    keep = iota((128, 128), 1) <= iota((128, 128), 0)
    for chan, pair in zip(group, pairs):
        skew = jnp.where(keep, pltpu.roll(pair, 1, 1, stride=1, stride_axis=0), 0.0)
        g_ref[pl.ds(chan, 1), :] = jnp.sum(skew, axis=0, keepdims=True)


def split_lags(g_ref, base):
    lags = g_ref[...]
    weighted = lags * iota(lags.shape, 1).astype(F32)
    for k, v in enumerate((lags, weighted)):
        high = v.astype(BF16).astype(F32)
        base[k] = high
        base[2 + k] = v - high
        base[4 + k] = jnp.zeros_like(v)
        base[6 + k] = jnp.zeros_like(v)


def near_sums(group, chans, base_flat, q_ref, a_ref, b_ref):
    outs = [nn(twice(base_flat[pl.ds(chan, 8, stride=chans), :].astype(BF16)), q_ref[chan]) for chan in group]
    for chan, out in zip(group, outs):
        a_ref[pl.ds(chan, 1), :] = out[0:1] + out[2:3]
        b_ref[pl.ds(chan, 1), :] = out[1:2] + out[3:4]


def groups(chans, size, body):
    size = min(size, chans)

    def step(k, carry):
        body([k * size + i for i in range(size)])
        return carry

    lax.fori_loop(0, chans // size, step, 0)


def finish(chans, ssm, a_ref, b_ref, g_ref):
    log_step, log_rate, frequency, coef = ssm
    step, rate, z, phi, slope = pole_parts(log_step, log_rate, frequency)
    b = (twice(coef[0]), twice(coef[1]))

    def dup(v):
        left = is_left(v.shape)
        moved = swap(v)
        return jnp.where(left, v, moved), jnp.where(left, moved, v)

    def total(ref):
        near, far = dup(ref[:chans, :]), dup(ref[chans:, :])
        far = cmul(far, z)
        return near[0] + far[0], near[1] + far[1]

    a, bb = total(a_ref), total(b_ref)
    residue = cmul(b, (step * phi[0], step * phi[1]))
    g_res = (2.0 * a[0], -2.0 * a[1])
    rb = cmul(residue, bb)
    g_pole = (2.0 * rb[0], -2.0 * rb[1])
    conj = lambda v: (v[0], -v[1])
    g_coef = cmul(conj((step * phi[0], step * phi[1])), g_res)
    bs = cmul(b, (step * slope[0], step * slope[1]))
    more = cmul(conj(bs), g_res)
    g_pole = (g_pole[0] + more[0], g_pole[1] + more[1])
    d_rate = -rate * g_pole[0]
    d_freq = step * g_pole[1]
    by_step = cmul(conj(cmul(b, phi)), g_res)[0] + g_pole[1] * twice(frequency)
    left = is_left(by_step.shape)
    d_step = step * jnp.sum(jnp.where(left, by_step, 0.0), axis=1, keepdims=True)
    return jnp.where(left, d_rate, d_freq), jnp.where(left, g_coef[0], g_coef[1]), d_step, g_ref[:, 0:1]


def n_consts(rows):
    return 2 * (4 + (rows - 1).bit_length() + 2)


def gelu_parts(v):
    scale = 0.7978845608028654
    square = v * v
    bend = jnp.tanh(scale * v * (1.0 + 0.044715 * square))
    half = 0.5 + 0.5 * bend
    slope = half + 0.5 * v * (1.0 - bend * bend) * (scale * (1.0 + 0.134145 * square))
    return v * half, slope


def layer_norm(values, gain, shift):
    center = values - jnp.mean(values, axis=-1, keepdims=True)
    scale = lax.rsqrt(jnp.mean(center * center, axis=-1, keepdims=True) + NORM_EPSILON)
    normed = center * scale
    return normed * gain + shift, normed, scale


def norm_back(grad_out, gain, normed, scale):
    scaled = grad_out * gain
    return scale * (
        scaled
        - jnp.mean(scaled, axis=-1, keepdims=True)
        - normed * jnp.mean(scaled * normed, axis=-1, keepdims=True)
    )


def token_sum(values):
    return jnp.sum(values, axis=0, keepdims=True)


class Links:
    def __init__(self, send, recv, n_dp, n_blk):
        self.send, self.recv, self.used, self.open = send, recv, 0, []
        self.n_dp, self.n_blk = n_dp, n_blk
        self.dp, self.blk = lax.axis_index("dp"), lax.axis_index("blk")

    def dp_peer(self, mask):
        return jnp.bitwise_xor(self.dp, mask)

    def blk_peer(self, mask):
        return jnp.bitwise_xor(self.blk, mask)

    def copy(self, src, dst, dp_mask, blk_mask):
        copy = pltpu.make_async_remote_copy(
            src_ref=src,
            dst_ref=dst,
            send_sem=self.send.at[self.used],
            recv_sem=self.recv.at[self.used],
            device_id=(self.dp_peer(dp_mask), self.blk_peer(blk_mask)),
            device_id_type=pl.DeviceIdType.MESH,
        )
        copy.start()
        self.used += 1
        self.open.append(copy)
        return copy

    def greet(self):
        barrier = pltpu.get_barrier_semaphore()
        for mask in range(1, self.n_dp):
            pl.semaphore_signal(
                barrier, inc=1, device_id=(self.dp_peer(mask), self.blk), device_id_type=pl.DeviceIdType.MESH
            )
        for mask in range(1, self.n_blk):
            pl.semaphore_signal(
                barrier, inc=1, device_id=(self.dp, self.blk_peer(mask)), device_id_type=pl.DeviceIdType.MESH
            )

    def meet(self):
        pl.semaphore_wait(pltpu.get_barrier_semaphore(), self.n_dp + self.n_blk - 2)

    def finish(self):
        for copy in self.open:
            copy.wait_send()

    def exchange(self, src, dst):
        copies = [
            self.copy(src.at[self.blk_peer(mask)], dst.at[self.blk], 0, mask) for mask in range(1, self.n_blk)
        ]
        dst[self.blk] = src[self.blk]
        return copies


def wait_all(copies):
    for copy in copies:
        copy.wait_recv()


class Gather:
    def __init__(self, links, buf):
        self.links, self.buf, self.got = links, buf, {}
        self.bits = [1 << k for k in range(links.n_dp.bit_length() - 1)]
        self.forward(0)

    def forward(self, mask):
        low = mask & -mask if mask else self.links.n_dp
        if mask:
            self.got[mask].wait_recv()
        slot = self.buf.at[self.links.dp_peer(mask)]
        for bit in reversed(self.bits):
            if bit < low:
                self.got[mask | bit] = self.links.copy(slot, slot, bit, 0)

    def relay(self):
        for mask in sorted(range(1, self.links.n_dp), key=lambda m: bin(m).count("1")):
            self.forward(mask)


class Chunk:
    def __init__(self, links, part, landing, view, order, late):
        self.links, self.part, self.landing, self.view = links, part, landing, view
        self.order, self.late = order, late
        self.rows = part.shape[0]
        self.walk = self.steps()

    def advance(self):
        next(self.walk, None)

    def steps(self):
        links, part = self.links, self.part
        low, size, lows = 0, self.rows, []
        for k, bit in enumerate(self.order):
            half = size // 2
            mine = (links.blk // bit) % 2
            keep = pl.multiple_of(low + mine * half, 8)
            away = pl.multiple_of(low + (1 - mine) * half, 8)
            slot = self.landing.at[pl.ds(self.rows - size, half), :]
            copy = links.copy(part.at[pl.ds(away, half), :], slot, 0, bit)
            yield
            copy.wait_recv()
            lows.append(low)
            low, size = keep, half
            total = part[pl.ds(low, size), :] + slot[...]
            if k + 1 < len(self.order):
                part[pl.ds(low, size), :] = total
            else:
                self.view(0, low, size)[...] = total
        held = [0]
        dp_bits = [1 << k for k in range(1, links.n_dp.bit_length() - 1)]
        plan = [("blk", bit) for bit in reversed(self.order)]
        plan = plan[: self.late] + [("dp", bit) for bit in dp_bits] + plan[self.late :]
        if links.n_dp > 1:
            plan.append(("dp", 1))
        for axis, bit in plan:
            place = [self.view(mask, low, size) for mask in held]
            if axis == "blk":
                copies = [links.copy(v, v, 0, bit) for v in place]
                low, size = lows.pop(), size * 2
            else:
                copies = [links.copy(v, v, bit, 0) for v in place]
                held = held + [mask | bit for mask in held]
            yield
            wait_all(copies)


VEC_ROWS = 16


def whole_kernel(
    n_dp, n_blk, x_ref, lengths, cot_ref, n1g, n1b, log_step, log_rate, frequency, out_coef, skip_gain, glu_hbm, glu_b,
    n2g, n2b, in_hbm, in_b, out_hbm, out_b,
    block_out, grad_in, grad_glu_out, grad_in_out, grad_out_out, vec_out, rate_out, freq_out, coef_out,
    send_sems, recv_sems, load_sems, glu_w, ffn_in, ffn_out, rate_own, freq_own, coef_own, columns,
    a_send, x_all, y_send, y_all, dy_send, dy_all, dx_send, dx_all,
    q_ref, t_ref, h_ref, consts, base, taps, a_ref, b_ref, g_ref,
    result_all, gelu_all, feed_all, dglu, dglu_all, hidden_grad, slice_grad, hidden_s, pre_s, conv_keep, unit_keep, residual_keep, gate_keep,
    acc_out, acc_feed, residual_grad,
    part_glu, part_in0, part_in1, part_out0, part_out1, land_glu, land_in0, land_in1, land_out0, land_out1,
    sum_glu, sum_in, sum_out, own_par, dp_par, sum_par, blk_par, all_par, vec, dp_vec, sum_vec, blk_vec,
):
    rows, width = x_ref.shape
    ff = ffn_in.shape[1]
    chans = width // n_blk
    quarter = chans // n_dp
    links = Links(send_sems, recv_sems, n_dp, n_blk)
    dp, blk = links.dp, links.blk
    first = pl.multiple_of(blk * chans, 8)

    loads = [
        pltpu.make_async_copy(src, dst, load_sems.at[k])
        for k, (src, dst) in enumerate([
            (log_rate.at[pl.ds(first, chans), :], rate_own),
            (frequency.at[pl.ds(first, chans), :], freq_own),
            (out_coef.at[:, pl.ds(first, chans), :], coef_own),
            (out_hbm, ffn_out),
            (glu_hbm, glu_w),
            (in_hbm, ffn_in),
        ])
    ]
    for load in loads:
        load.start()
    links.greet()

    places = blk * rows + iota((rows, 1), 0)
    live = (places < lengths[0]).astype(F32)
    inputs = x_ref[...].astype(F32)
    normed, unit, scale1 = layer_norm(inputs, n1g[...], n1b[...])
    unit_keep[...] = unit
    mixed = normed.astype(BF16) * live.astype(BF16)
    flip = jnp.where(iota((rows, rows), 0) + iota((rows, rows), 1) == rows - 1, 1.0, 0.0).astype(BF16)
    a_send[...] = nn(flip, mixed).T
    links.meet()
    to_x = links.exchange(a_send.reshape(n_blk, chans, rows), x_all)
    cot = cot_ref[...].astype(F32)
    result = live * cot
    result_all[dp] = result
    gather_result = Gather(links, result_all)

    columns[0] = jnp.broadcast_to(log_step[...], (128, width)).T
    columns[1] = jnp.broadcast_to(skip_gain[...], (128, width)).T
    own_step = columns[0, pl.ds(first, chans), :]
    own_skip = columns[1, pl.ds(first, chans), :]
    for load in loads[:3]:
        load.wait()

    def ssm():
        return columns[0, pl.ds(first, chans), :], rate_own[...], freq_own[...], (coef_own[0], coef_own[1])

    kern_slot = ssm_setup(n_blk, ssm(), consts, base)
    lead_slot = kern_slot - 1
    base_flat = base.reshape(8 * chans, 128)
    groups(chans, GROUP, lambda group: make_powers(group, chans, consts, kern_slot, base_flat, q_ref, taps))
    shift_taps(own_skip, taps, base)
    groups(chans, GROUP, lambda group: make_band(group, chans, base_flat, t_ref))

    x_flat = x_all.reshape(n_blk * chans, 128)
    y_flat = y_send.reshape(n_blk * chans, 128)
    wait_all(to_x)
    groups(chans, GROUP, lambda group: forward_group(group, chans, n_blk, consts, lead_slot, x_flat, q_ref, t_ref, h_ref, y_flat))
    to_y = links.exchange(y_send, y_all)

    gather_result.relay()
    loads[3].wait()
    low = result.astype(BF16)
    step = ff // 4
    for k in range(4):
        hidden_grad[:, k * step : (k + 1) * step] = nt(low, ffn_out[k * step : (k + 1) * step, :])
    part_ff = ff // n_dp
    rows_s = pl.multiple_of(dp * part_ff, 128)
    out_slice = ffn_out[pl.ds(rows_s, part_ff), :]
    for k in range(n_dp):
        slice_grad[k * rows : (k + 1) * rows, :] = nt(result_all[k].astype(BF16), out_slice)
    loads[4].wait()
    loads[5].wait()

    wait_all(to_y)
    conv = y_all.reshape(width, rows)[...].T
    gelu_out, gelu_slope = gelu_parts(conv)
    conv_keep[...] = gelu_slope
    gelu_low = gelu_out.astype(BF16)
    gelu_all[dp] = gelu_low.astype(F32)
    gather_gelu = Gather(links, gelu_all)
    glu_pre = nn(gelu_low, glu_w[...]) + glu_b[...]
    left = glu_pre[:, :width]
    gate = 0.5 + 0.5 * jnp.tanh(0.5 * glu_pre[:, width:])
    gate_keep[0] = left
    gate_keep[1] = gate
    residual = x_ref[...].astype(F32) + live * left * gate
    normed_mid, unit_mid, scale_mid = layer_norm(residual, n2g[...], n2b[...])
    feed = normed_mid.astype(BF16)
    feed_all[dp] = feed.astype(F32)
    gather_feed = Gather(links, feed_all)
    residual_keep[0] = residual
    residual_keep[1] = unit_mid

    for k in range(4):
        cut = slice(k * step, (k + 1) * step)
        hidden, slope = gelu_parts(nn(feed, ffn_in[:, cut]) + in_b[:, cut])
        grad_pre = (hidden_grad[:, cut] * slope).astype(BF16)
        forward = nn(hidden.astype(BF16), ffn_out[cut, :])
        back = nt(grad_pre, ffn_in[:, cut])
        acc_out[...] = forward if k == 0 else acc_out[...] + forward
        acc_feed[...] = back if k == 0 else acc_feed[...] + back
        vec[7 + k : 8 + k, :] = token_sum(grad_pre.astype(F32))
    gather_gelu.relay()
    gather_feed.relay()

    in_slice = ffn_in[:, pl.ds(rows_s, part_ff)]
    in_b_slice = in_b[:, pl.ds(rows_s, part_ff)]
    for k in range(n_dp):
        hidden, slope = gelu_parts(nn(feed_all[k].astype(BF16), in_slice) + in_b_slice)
        cut = slice(k * rows, (k + 1) * rows)
        hidden_s[cut, :] = hidden.astype(BF16)
        pre_s[cut, :] = (slice_grad[cut, :] * slope).astype(BF16)
    half = width // 2
    results = result_all[...].reshape(n_dp * rows, width).astype(BF16)

    def out_view(piece):
        def view(mask, row, size):
            at = pl.multiple_of(links.dp_peer(mask) * part_ff + row, 8)
            return sum_out.at[pl.ds(at, size), pl.ds(piece * half, half)]
        return view

    half_ff = part_ff // 2

    def in_view(piece):
        def view(mask, row, size):
            at = pl.multiple_of(links.dp_peer(mask) * part_ff + piece * half_ff, 128)
            return sum_in.at[pl.ds(pl.multiple_of(row, 8), size), pl.ds(at, half_ff)]
        return view

    part_gl = 2 * width // n_dp

    def glu_view(mask, row, size):
        at = pl.multiple_of(links.dp_peer(mask) * part_gl, 128)
        return sum_glu.at[pl.ds(pl.multiple_of(row, 8), size), pl.ds(at, part_gl)]

    bits = [1 << k for k in range(n_blk.bit_length() - 1)]
    orders = [(bits, 2), ([bits[1], bits[0]] + bits[2:], len(bits))]

    part_out0[...] = tn(hidden_s[...], results[:, :half])
    out0 = Chunk(links, part_out0, land_out0, out_view(0), *orders[0])
    out0.advance()
    part_out1[...] = tn(hidden_s[...], results[:, half:])
    out1 = Chunk(links, part_out1, land_out1, out_view(1), *orders[1])
    out1.advance()
    feeds = feed_all[...].reshape(n_dp * rows, width).astype(BF16)
    part_in0[...] = tn(feeds, pre_s[:, :half_ff])
    in0 = Chunk(links, part_in0, land_in0, in_view(0), *orders[0])
    in0.advance()
    part_in1[...] = tn(feeds, pre_s[:, half_ff:])
    in1 = Chunk(links, part_in1, land_in1, in_view(1), *orders[1])
    in1.advance()

    grad_feed = acc_feed[...]
    unit_mid = residual_keep[1]
    vec[2:3, :] = token_sum(grad_feed * unit_mid)
    vec[3:4, :] = token_sum(grad_feed)
    vec[4:5, :] = token_sum(result)
    grad_res = cot_ref[...].astype(F32) + norm_back(grad_feed, n2g[...], unit_mid, scale_mid)
    residual_grad[...] = grad_res
    grad_left = live * grad_res
    left, gate = gate_keep[0], gate_keep[1]
    dglu[:, :width] = (grad_left * gate).astype(BF16).astype(F32)
    dglu[:, width:] = (grad_left * left * gate * (1.0 - gate)).astype(BF16).astype(F32)
    to_glu = []
    for mask in range(1, n_dp):
        at = pl.multiple_of(links.dp_peer(mask) * part_gl, 128)
        to_glu.append(links.copy(dglu.at[:, pl.ds(at, part_gl)], dglu_all.at[dp], mask, 0))
    dglu_all[dp] = dglu[:, pl.ds(pl.multiple_of(dp * part_gl, 128), part_gl)]
    vec[5:6, :] = token_sum(dglu[:, :width])
    vec[6:7, :] = token_sum(dglu[:, width:])
    grad_gelu = nt(dglu[...].astype(BF16), glu_w[...])
    dy_send[...] = (grad_gelu * conv_keep[...]).T
    to_dy = links.exchange(dy_send.reshape(n_blk, chans, rows), dy_all)
    block_out[...] = (residual_keep[0] + live * (acc_out[...] + out_b[...])).astype(BF16)

    out0.advance()
    out1.advance()
    wait_all(to_glu)
    gelus = gelu_all[...].reshape(n_dp * rows, width).astype(BF16)
    part_glu[...] = tn(gelus, dglu_all[...].reshape(n_dp * rows, part_gl).astype(BF16))
    glu = Chunk(links, part_glu, land_glu, glu_view, *orders[0])
    glu.advance()
    in0.advance()
    in1.advance()
    out0.advance()
    out1.advance()

    wait_all(to_dy)
    dy_flat = dy_all.reshape(n_blk * chans, 128)
    dx_flat = dx_send.reshape(n_blk * chans, 128)
    groups(chans, GROUP, lambda group: backward_group(group, chans, n_blk, consts, lead_slot, x_flat, dy_flat, q_ref, t_ref, h_ref, dx_flat, a_ref, b_ref, g_ref))
    to_dx = links.exchange(dx_send, dx_all)
    for chunk in (in0, in1, glu, out0, out1):
        chunk.advance()
    split_lags(g_ref, base)
    groups(chans, GROUP, lambda group: near_sums(group, chans, base_flat, q_ref, a_ref, b_ref))
    rate_freq, coefs, d_step, d_skip = finish(chans, ssm(), a_ref, b_ref, g_ref)
    own_par[:, 0, :] = rate_freq
    own_par[:, 1, :] = coefs
    pair = jnp.where(iota((chans, 128), 1) == 0, d_step, jnp.where(iota((chans, 128), 1) == 1, d_skip, 0.0))
    if chans < 128:
        pair = jnp.concatenate([pair, jnp.zeros((128 - chans, 128), F32)], axis=0)
    pair = pair.T[0:8]
    if width > 128:
        pair = jnp.concatenate([pair, jnp.zeros((8, width - 128), F32)], axis=1)
    pair = pltpu.roll(pair, blk * chans, 1)
    vec[11:13, :] = pair[0:2]
    vec[13:16, :] = jnp.zeros((3, width), F32)
    for chunk in (in0, in1, glu, out0, out1):
        chunk.advance()

    wait_all(to_dx)
    back = dx_all.reshape(width, rows)[...].T
    high, rest = split(back)
    rest, last = split(back - high.astype(F32))
    grad_normed = live * (nn(flip, high) + (nn(flip, rest) + nn(flip, last)))
    unit = unit_keep[...]
    vec[0:1, :] = token_sum(grad_normed * unit)
    vec[1:2, :] = token_sum(grad_normed)
    grad_in[...] = residual_grad[...] + norm_back(grad_normed, n1g[...], unit, scale1)

    waits = []
    for mask in range(1, n_dp):
        at = links.dp_peer(mask) * quarter
        waits.append(links.copy(own_par.at[pl.ds(at, quarter)], dp_par.at[dp], mask, 0))
        waits.append(links.copy(vec, dp_vec.at[dp], mask, 0))
    dp_par[dp] = own_par[pl.ds(dp * quarter, quarter)]
    dp_vec[dp] = vec[...]
    for chunk in (in0, in1, glu, out0, out1):
        chunk.advance()
    wait_all(waits)
    sum_par[...] = sum_slots(dp_par, n_dp)
    sum_vec[...] = sum_slots(dp_vec, n_dp)
    waits = []
    for mask in range(1, n_blk):
        waits.append(links.copy(sum_par, blk_par.at[blk], 0, mask))
        waits.append(links.copy(sum_vec, blk_vec.at[blk], 0, mask))
    blk_par[blk] = sum_par[...]
    blk_vec[blk] = sum_vec[...]
    for chunk in (in0, in1, glu, out0, out1):
        chunk.advance()
    wait_all(waits)
    all_par[dp] = blk_par[...]
    gather_par = Gather(links, all_par)
    vec_out[...] = sum_slots(blk_vec, n_blk)
    for chunk in (in0, in1, glu, out0, out1):
        chunk.advance()
    gather_par.relay()
    state = rate_out.shape[1]
    for b in range(n_blk):
        for d in range(n_dp):
            at = b * chans + d * quarter
            block = all_par[d, b]
            rate_out[at : at + quarter, :] = block[:, 0, :state]
            freq_out[at : at + quarter, :] = block[:, 0, state:]
            coef_out[0, at : at + quarter, :] = block[:, 1, :state]
            coef_out[1, at : at + quarter, :] = block[:, 1, state:]
    for _ in range(8):
        for chunk in (in0, in1, glu, out0, out1):
            chunk.advance()
    stores = [
        pltpu.make_async_copy(src, dst, load_sems.at[k])
        for k, (src, dst) in enumerate([(sum_glu, grad_glu_out), (sum_in, grad_in_out), (sum_out, grad_out_out)])
    ]
    for store in stores:
        store.start()
    links.finish()
    for store in stores:
        store.wait()


def sum_slots(ref, count):
    total = ref[0]
    for k in range(1, count):
        total = total + ref[k]
    return total


def on_device(n_dp, n_blk, block_in, seq_lengths, norm1_gain, norm1_bias, log_step, log_rate, frequency, out_coef, skip_gain, glu_weight, glu_bias, norm2_gain, norm2_bias, ffn_in, ffn_in_bias, ffn_out, ffn_out_bias, cotangent):
    _, rows, width = block_in.shape
    ff = ffn_in.shape[1]
    states = log_rate.shape[1]
    chans, quarter = width // n_blk, width // n_blk // n_dp
    row = lambda v: v.reshape(1, -1)
    vmem, anywhere = pl.BlockSpec(memory_space=VMEM), pl.BlockSpec(memory_space=pl.ANY)
    shape = jax.ShapeDtypeStruct
    outs = [
        (shape((rows, width), BF16), vmem),
        (shape((rows, width), F32), vmem),
        (shape((width, 2 * width), F32), anywhere),
        (shape((width, ff), F32), anywhere),
        (shape((ff, width), F32), anywhere),
        (shape((VEC_ROWS, width), F32), vmem),
        (shape((width, states), F32), vmem),
        (shape((width, states), F32), vmem),
        (shape((2, width, states), F32), vmem),
    ]
    part_ff, part_gl = ff // n_dp, 2 * width // n_dp
    tokens = n_dp * rows
    parts = [(width, part_gl), (width, part_ff // 2), (width, part_ff // 2), (part_ff, width // 2), (part_ff, width // 2)]
    f32 = lambda *dims: VMEM(dims, F32)
    bf16 = lambda *dims: VMEM(dims, BF16)
    dma = lambda n: pltpu.SemaphoreType.DMA((n,))
    scratch = [
        dma(LINK_SEMS), dma(LINK_SEMS), dma(8),
        bf16(width, 2 * width), bf16(width, ff), bf16(ff, width),
        f32(chans, states), f32(chans, states), f32(2, chans, states), f32(2, width, 128),
        f32(width, rows), f32(n_blk, chans, rows), f32(n_blk, chans, rows), f32(n_blk, chans, rows),
        f32(width, rows), f32(n_blk, chans, rows), f32(n_blk, chans, rows), f32(n_blk, chans, rows),
        bf16(chans, 256, 128), bf16(chans, 256, 128), f32(chans, n_blk, 128), f32(n_consts(n_blk), chans, 128),
        f32(8, chans, 128), f32(chans, 128), f32(2 * chans, 128), f32(2 * chans, 128), f32(chans, 128),
        f32(n_dp, rows, width), f32(n_dp, rows, width), f32(n_dp, rows, width),
        f32(rows, 2 * width), f32(n_dp, rows, part_gl),
        f32(rows, ff), f32(tokens, part_ff), bf16(tokens, part_ff), bf16(tokens, part_ff),
        f32(rows, width), f32(rows, width), f32(2, rows, width), f32(2, rows, width),
        f32(rows, width), f32(rows, width), f32(rows, width),
        *[f32(*p) for p in parts], *[f32(*p) for p in parts],
        f32(width, 2 * width), f32(width, ff), f32(ff, width),
        f32(chans, 2, 128), f32(n_dp, quarter, 2, 128), f32(quarter, 2, 128), f32(n_blk, quarter, 2, 128), f32(n_dp, n_blk, quarter, 2, 128),
        f32(VEC_ROWS, width), f32(n_dp, VEC_ROWS, width), f32(VEC_ROWS, width), f32(n_blk, VEC_ROWS, width),
    ]
    out = pl.pallas_call(
        functools.partial(whole_kernel, n_dp, n_blk),
        out_shape=[o[0] for o in outs],
        out_specs=[o[1] for o in outs],
        in_specs=[vmem, pl.BlockSpec(memory_space=pltpu.SMEM), vmem, vmem, vmem, vmem, anywhere, anywhere, anywhere, vmem, anywhere, vmem, vmem, vmem, anywhere, vmem, anywhere, vmem],
        scratch_shapes=scratch,
        compiler_params=pltpu.CompilerParams(collective_id=0, has_side_effects=True, vmem_limit_bytes=60 * 2**20),
    )(
        block_in[0], seq_lengths, cotangent[0], row(norm1_gain), row(norm1_bias), row(log_step), log_rate, frequency, out_coef,
        row(skip_gain), glu_weight, row(glu_bias), row(norm2_gain), row(norm2_bias), ffn_in, row(ffn_in_bias), ffn_out, row(ffn_out_bias),
    )
    block_out, grad_in, g_glu, g_in, g_out, vec, rate, freq, coef = out
    return (
        block_out[None], grad_in[None], vec[0], vec[1], vec[11], rate, freq, coef, vec[12],
        g_glu, vec[5:7].reshape(-1), vec[2], vec[3], g_in, vec[7:11].reshape(-1), g_out, vec[4],
    )


def solution(mesh):
    split_spec, whole = P("dp", "blk", None), P()
    return jax.shard_map(
        functools.partial(on_device, mesh.shape["dp"], mesh.shape["blk"]),
        mesh=mesh,
        in_specs=(split_spec, P("dp")) + (whole,) * 15 + (split_spec,),
        out_specs=(split_spec, split_spec) + (whole,) * 15,
        check_vma=False,
    )
```

time: 391 us -> 187 us (0.48)
  waiting for transfers between devices: 161 us -> 0 us
  Pallas kernels: 59.2 us -> 157 us
  blocking collectives: 86.4 us -> 0 us
  matrix products: 18.2 us -> 0 us
  starting transfers between devices: 15.1 us -> 0 us
  between operations: 15.3 us -> 1.32 us
  other arithmetic: 7.69 us -> 0 us
    psum x2 -> x0, waiting for transfers between devices: 154 us -> none  [the longest x1 132 us: on_device(): lax.psum((grad_norm1_gain, grad_norm1_bias, grad_glu_weight, grad_glu_bia...]
    pallas_call x2 -> x1, Pallas kernels: 59.2 us -> 157 us  [on_device(): pl.pallas_call(functools.partial(whole_kernel, n_dp, n_blk), out_shape=[o...]
    psum x1 -> x0, blocking collectives: 39.9 us -> none  [on_device(): lax.psum((grad_norm1_gain, grad_norm1_bias, grad_glu_weight, grad_glu_bia...]
    all_gather x1 -> x0, blocking collectives: 34.3 us -> none  [on_device(): own = lax.all_gather(lax.psum(own, 'dp'), 'blk', axis=0, tiled=True)]
    dot_general x9 -> x0, matrix products: 18.2 us -> none  [dot(): return jnp.einsum(spec, a, b, preferred_element_type=F32)]
    all_to_all x3 -> x0, starting transfers between devices: 15.1 us -> none  [the longest x2 10.9 us: to_channels(): return lax.all_to_all(parts, 'blk', 0, 0)]
    all_to_all x1 -> x0, blocking collectives: 12.2 us -> none  [to_tokens(): parts = lax.all_to_all(v, 'blk', 0, 0)]
    unnamed x79 -> x19, local copies, waits for them, and re-layouts: 16.7 us -> 25.7 us
  transfers between devices with their start and end apart: 5 -> 0, of which waited for: 4 -> 0; matrix products, arithmetic and copies ran while one was open for 6% -> 0% of each run, Pallas kernels for 0% -> 0%
where the time goes in v2:
time: 187 us; the launch traced here: 186 us
  Pallas kernels  157 us (84%)
  local copies, waits for them, and re-layouts  27.2 us (15%)
    pallas_call x1, Pallas kernels, on_device(): pl.pallas_call(functools.partial(whole_kernel, n_dp, n_blk), out_shape=[o...  157 us
    unnamed x19, local copies, waits for them, and re-layouts  25.7 us

profile of v2, /device:TPU:0, one launch (start us, length us, event | category | flops | bytes accessed | tf_op | source)
XLA Modules:
  0.0 185.8 jit_solution(6170911336551588961)
XLA Ops:
  1.3 1.7 copy.35.log_rate
  3.0 1.7 copy.36.frequency
  4.8 1.9 %copy.37.out_coef = f32[2,512,64]{2,1,0:T(8,128)} copy(f32[2,512,64]{1,2,0:T(8,128)} %param.25) | data formatting | bytes 524288 | tf_op args[7]
  6.7 157.2 %shard_map.305 = (bf16[128,512]{1,0:T(8,128)(2,1)}, f32[128,512]{1,0:T(8,128)}, f32[512,1024]{1,0:T(8,128)}, f32[512,2048]{1,0:T(8,128)}, f32[2048,512]{1,0:T(8,...) custom-call(bf16[128,512]{1,0:T(8,128)(2,1)} %bitcast.27, ...), custom_call_target="tpu_custom_call" | custom-call | tf_op jit(solution)/shard_map/pallas_call | solution.py:811
  163.9 0.7 slice_bitcast_fusion.1
  164.6 0.6 copy.41
  165.2 0.8 slice_bitcast_fusion
  166.0 1.5 fusion
  167.5 0.6 copy.42
  168.1 1.7 copy.38
  169.8 1.7 copy.39
  171.6 1.9 %copy.40 = f32[2,512,64]{1,2,0:T(8,128)} copy(f32[2,512,64]{2,1,0:T(8,128)} %get-tuple-element.42) | data formatting | bytes 524288
  173.5 0.0 copy-start.1
  173.5 1.7 copy.49
  175.2 1.7 copy.50
  176.9 3.2 %copy.51 = f32[512,1024]{1,0:T(8,128)} copy(f32[512,1024]{1,0:T(8,128)} %get-tuple-element.85) | data formatting | bytes 4194304
  180.0 0.0 copy-done.1
  180.0 0.0 copy-start
  180.0 2.1 %copy.52 = f32[512,2048]{1,0:T(8,128)} copy(f32[512,2048]{1,0:T(8,128)S(1)} %copy-done.1) | data formatting | bytes 8388608
  182.2 1.6 copy-done
  183.7 2.0 %copy.53 = f32[2048,512]{1,0:T(8,128)} copy(f32[2048,512]{1,0:T(8,128)S(1)} %copy-done) | data formatting | bytes 8388608
Async XLA Ops:
  173.5 6.6 %copy-start.1 = (f32[512,2048]{1,0:T(8,128)S(1)}, f32[512,2048]{1,0:T(8,128)}, u32[]{:S(2)}) copy-start(f32[512,2048]{1,0:T(8,128)} %get-tuple-element.89) | copy-start | bytes 12582916
  180.0 3.7 %copy-start = (f32[2048,512]{1,0:T(8,128)S(1)}, f32[2048,512]{1,0:T(8,128)}, u32[]{:S(2)}) copy-start(f32[2048,512]{1,0:T(8,128)} %get-tuple-element.91) | copy-start | bytes 12582916

commit v3 on v2

--- a/solution.py
+++ b/solution.py
@@ -13,7 +13,40 @@
 PRECISE = lax.Precision.HIGHEST
 SERIES = 16
 GROUP = 16
-LINK_SEMS = 128
+LINK_SEMS = 256
+BIG_PARTS = 4
+GLU_PLANS = (
+    (("c", "y", "x", "z0", "z1"), 0),
+    (("c", "z0", "y", "x", "z1"), 2),
+)
+FFN_PLANS = (
+    (("x", "z0", "z1"), 3),
+    (("x", "z0", "z1"), 2),
+    (("x", "z0", "z1"), 3),
+    (("x", "z0", "z1"), 2),
+    (("x", "z1", "z0"), 3),
+    (("x", "z0", "z1"), 3),
+    (("x", "z0", "z1"), 2),
+    (("x", "z0", "z1"), 3),
+    (("x", "z0", "z1"), 1),
+    (("z0", "x", "z1"), 3),
+    (("x", "z0", "z1"), 1),
+    (("x", "z1", "z0"), 1),
+    (("z1", "x", "z0"), 3),
+    (("x", "z0", "z1"), 3),
+    (("z0", "x", "z1"), 2),
+    (("x", "z0", "z1"), 2),
+)
+ORDER = (
+    "own", "glubwd", "dy", "part0", "part1", 0, 1, "slice", "part2", "part3", "part4", "part5", "part6",
+    "part7", "part8", "part9", "part10", "part11", 2, "part12", 0, "part13", 3, 1, "part14", "part15",
+    "part16", 4, 11, 2, "part17", 5, 3, "bwd0", 6, 1, 7, 14, 16, 4, 8, 2, 5, 3, 9, 6, 7, 10, 4, 8, 12, 2,
+    "bwd1", 5, 3, 9, 6, 0, 7, 10, 4, 13, 8, 12, 15, 2, 11, 5, 3, "bwd2", 6, 9, 17, 0, 1, 7, 14, 10, 16, 3, 4,
+    2, 13, 8, "bwd3", 12, 15, 11, 5, 6, "near", 3, 9, 2, 17, 4, 0, 5, 1, 7, 14, 10, 3, 2, 13, 16, 8, 4, 0, 10,
+    4, 6, 8, "ln1", 12, 15, 5, "s0", 11, 9, 7, 17, 6, 12, 5, 14, 1, 13, 16, 8, 6, "s1", 11, 9, 8, 0, 10, 14,
+    15, 7, 17, 13, 1, 12, 16, 7, "s2", 9, 11, 10, 9, 1, 0, 10, 16, 12, 15, 17, 14, 12, "s3", 13, 11, 0, 17,
+    15, 11, 1, 0, 14, 13, 1, 16, 14, 15, 13, 17, 16, 15, 17,
+)
 VMEM = pltpu.VMEM
 
 
@@ -270,14 +303,15 @@
         b_ref[pl.ds(chan, 1), :] = out[1:2] + out[3:4]
 
 
-def groups(chans, size, body):
-    size = min(size, chans)
+def groups(first, count, body):
+    size = min(GROUP, count)
 
     def step(k, carry):
-        body([k * size + i for i in range(size)])
+        body([first + k * size + i for i in range(size)])
         return carry
 
-    lax.fori_loop(0, chans // size, step, 0)
+    if count > 0:
+        lax.fori_loop(0, count // size, step, 0)
 
 
 def finish(chans, ssm, a_ref, b_ref, g_ref):
@@ -346,6 +380,26 @@
     return jnp.sum(values, axis=0, keepdims=True)
 
 
+class Transfer:
+    def __init__(self, copy):
+        self.copy, self.arrived = copy, False
+
+    def wait_recv(self):
+        self.arrived = True
+        self.copy.wait_recv()
+
+
+class Load:
+    def __init__(self, src, dst, sem):
+        self.copy, self.done = pltpu.make_async_copy(src, dst, sem), False
+        self.copy.start()
+
+    def wait(self):
+        if not self.done:
+            self.done = True
+            self.copy.wait()
+
+
 class Links:
     def __init__(self, send, recv, n_dp, n_blk):
         self.send, self.recv, self.used, self.open = send, recv, 0, []
@@ -369,6 +423,7 @@
         )
         copy.start()
         self.used += 1
+        copy = Transfer(copy)
         self.open.append(copy)
         return copy
 
@@ -387,14 +442,24 @@
         pl.semaphore_wait(pltpu.get_barrier_semaphore(), self.n_dp + self.n_blk - 2)
 
     def finish(self):
-        for copy in self.open:
-            copy.wait_send()
-
-    def exchange(self, src, dst):
+        for transfer in self.open:
+            transfer.copy.wait_send()
+
+    def stop(self):
+        for transfer in self.open:
+            if not transfer.arrived:
+                transfer.wait_recv()
+        for load in self.loads:
+            load.wait()
+        self.finish()
+
+    def exchange(self, src, dst, first, size):
+        part = pl.ds(first, size)
         copies = [
-            self.copy(src.at[self.blk_peer(mask)], dst.at[self.blk], 0, mask) for mask in range(1, self.n_blk)
+            self.copy(src.at[self.blk_peer(mask), part], dst.at[self.blk, part], 0, mask)
+            for mask in range(1, self.n_blk)
         ]
-        dst[self.blk] = src[self.blk]
+        dst[self.blk, part] = src[self.blk, part]
         return copies
 
 
@@ -423,43 +488,62 @@
             self.forward(mask)
 
 
+def bit_names(n_dp, n_blk):
+    blk = [("blk", 1 << k) for k in range(n_blk.bit_length() - 1)]
+    dp = [("dp", 1 << k) for k in range(n_dp.bit_length() - 1)]
+    return {"x": blk[:1], "z0": blk[1:2], "z1": blk[2:], "c": dp[:1], "y": dp[1:]}
+
+
 class Chunk:
-    def __init__(self, links, part, landing, view, order, late):
-        self.links, self.part, self.landing, self.view = links, part, landing, view
-        self.order, self.late = order, late
-        self.rows = part.shape[0]
+    def __init__(self, links, rows, part, out, landing, every, plan):
+        names = bit_names(links.n_dp, links.n_blk)
+        order, late = plan
+        spread = lambda tokens: [bit for token in tokens for bit in names[token]]
+        self.links, self.rows, self.part, self.out, self.landing = links, rows, part, out, landing
+        self.halving = spread(order)
+        back = [token for token in reversed(order) if token not in "cy"]
+        back = back[:late] + ["y"] + back[late:] + ["c"]
+        self.doubling = []
+        for token in back:
+            bits = names[token]
+            self.doubling += bits if token in "cy" else bits[::-1]
+        self.held = list(range(links.n_dp)) if every else [0]
         self.walk = self.steps()
+        self.live = True
 
     def advance(self):
-        next(self.walk, None)
+        self.live = next(self.walk, "end") != "end"
 
     def steps(self):
-        links, part = self.links, self.part
-        low, size, lows = 0, self.rows, []
-        for k, bit in enumerate(self.order):
-            half = size // 2
-            mine = (links.blk // bit) % 2
-            keep = pl.multiple_of(low + mine * half, 8)
-            away = pl.multiple_of(low + (1 - mine) * half, 8)
-            slot = self.landing.at[pl.ds(self.rows - size, half), :]
-            copy = links.copy(part.at[pl.ds(away, half), :], slot, 0, bit)
+        links = self.links
+        held, low, size, lows, at = self.held, 0, self.rows, [], 0
+        for k, (axis, bit) in enumerate(self.halving):
+            last = k + 1 == len(self.halving)
+            if axis == "blk":
+                half = size // 2
+                mine = (links.blk // bit) % 2
+                keep = pl.multiple_of(low + mine * half, 8)
+                away = pl.multiple_of(low + (1 - mine) * half, 8)
+                moves = [(mask, mask, away) for mask in held]
+                lows.append(low)
+                low, size = keep, half
+            else:
+                moves = [(mask, mask ^ bit, low) for mask in held if mask & bit]
+                held = [mask for mask in held if not mask & bit]
+            slots, copies = {}, []
+            for mask, there, row in moves:
+                slots[there] = self.landing.at[pl.ds(at, size), :]
+                at += size
+                dp_mask, blk_mask = (0, bit) if axis == "blk" else (bit, 0)
+                copies.append(links.copy(self.part(mask, row, size), slots[there], dp_mask, blk_mask))
             yield
-            copy.wait_recv()
-            lows.append(low)
-            low, size = keep, half
-            total = part[pl.ds(low, size), :] + slot[...]
-            if k + 1 < len(self.order):
-                part[pl.ds(low, size), :] = total
-            else:
-                self.view(0, low, size)[...] = total
-        held = [0]
-        dp_bits = [1 << k for k in range(1, links.n_dp.bit_length() - 1)]
-        plan = [("blk", bit) for bit in reversed(self.order)]
-        plan = plan[: self.late] + [("dp", bit) for bit in dp_bits] + plan[self.late :]
-        if links.n_dp > 1:
-            plan.append(("dp", 1))
-        for axis, bit in plan:
-            place = [self.view(mask, low, size) for mask in held]
+            wait_all(copies)
+            for mask in held:
+                own = self.part(mask, low, size)
+                goal = self.out(mask, low, size) if last else own
+                goal[...] = own[...] + slots[mask][...]
+        for axis, bit in self.doubling:
+            place = [self.out(mask, low, size) for mask in held]
             if axis == "blk":
                 copies = [links.copy(v, v, 0, bit) for v in place]
                 low, size = lows.pop(), size * 2
@@ -470,42 +554,55 @@
             wait_all(copies)
 
 
+def landing_rows(rows, order, n_dp, n_blk, every):
+    names, held, total = bit_names(n_dp, n_blk), n_dp if every else 1, 0
+    for token in order:
+        for axis, _ in names[token]:
+            if axis == "blk":
+                rows //= 2
+            else:
+                held //= 2
+            total += held * rows
+    return total
+
+
 VEC_ROWS = 16
 
 
 def whole_kernel(
     n_dp, n_blk, x_ref, lengths, cot_ref, n1g, n1b, log_step, log_rate, frequency, out_coef, skip_gain, glu_hbm, glu_b,
     n2g, n2b, in_hbm, in_b, out_hbm, out_b,
-    block_out, grad_in, grad_glu_out, grad_in_out, grad_out_out, vec_out, rate_out, freq_out, coef_out,
-    send_sems, recv_sems, load_sems, glu_w, ffn_in, ffn_out, rate_own, freq_own, coef_own, columns,
+    block_out, grad_in, sum_glu, sum_in, sum_out, vec_out, par_out,
+    send_sems, recv_sems, load_sems, glu_w, ffn_in, ffn_out, windows, rate_own, freq_own, coef_own, columns,
     a_send, x_all, y_send, y_all, dy_send, dy_all, dx_send, dx_all,
     q_ref, t_ref, h_ref, consts, base, taps, a_ref, b_ref, g_ref,
-    result_all, gelu_all, feed_all, dglu, dglu_all, hidden_grad, slice_grad, hidden_s, pre_s, conv_keep, unit_keep, residual_keep, gate_keep,
-    acc_out, acc_feed, residual_grad,
-    part_glu, part_in0, part_in1, part_out0, part_out1, land_glu, land_in0, land_in1, land_out0, land_out1,
-    sum_glu, sum_in, sum_out, own_par, dp_par, sum_par, blk_par, all_par, vec, dp_vec, sum_vec, blk_vec,
+    result_all, feed_all, dglu, hidden_grad, slice_grad, hidden_s, pre_s, slope_keep, unit_keep, residual_keep, gate_keep,
+    gelu_keep, acc_out, acc_feed, residual_grad, part_glu, part_in, part_out,
+    own_par, dp_par, sum_par, blk_par, all_par, flat_par, vec, dp_vec, sum_vec, blk_vec, *landings,
 ):
     rows, width = x_ref.shape
     ff = ffn_in.shape[1]
     chans = width // n_blk
     quarter = chans // n_dp
+    half = max(chans // 2, 8)
+    halves = [(first, half) for first in range(0, chans, half)]
     links = Links(send_sems, recv_sems, n_dp, n_blk)
     dp, blk = links.dp, links.blk
     first = pl.multiple_of(blk * chans, 8)
+    lanes_at = pl.multiple_of(blk * chans // 128 * 128, 128)
 
     loads = [
-        pltpu.make_async_copy(src, dst, load_sems.at[k])
+        Load(src, dst, load_sems.at[k])
         for k, (src, dst) in enumerate([
-            (log_rate.at[pl.ds(first, chans), :], rate_own),
-            (frequency.at[pl.ds(first, chans), :], freq_own),
-            (out_coef.at[:, pl.ds(first, chans), :], coef_own),
+            (log_rate.at[:, pl.ds(lanes_at, 128)], windows.at[0]),
+            (frequency.at[:, pl.ds(lanes_at, 128)], windows.at[1]),
+            (out_coef.at[:, :, pl.ds(lanes_at, 128)], windows.at[pl.ds(2, 2)]),
             (out_hbm, ffn_out),
             (glu_hbm, glu_w),
             (in_hbm, ffn_in),
         ])
     ]
-    for load in loads:
-        load.start()
+    links.loads = loads
     links.greet()
 
     places = blk * rows + iota((rows, 1), 0)
@@ -517,7 +614,7 @@
     flip = jnp.where(iota((rows, rows), 0) + iota((rows, rows), 1) == rows - 1, 1.0, 0.0).astype(BF16)
     a_send[...] = nn(flip, mixed).T
     links.meet()
-    to_x = links.exchange(a_send.reshape(n_blk, chans, rows), x_all)
+    to_x = [links.exchange(a_send.reshape(n_blk, chans, rows), x_all, *part) for part in halves]
     cot = cot_ref[...].astype(F32)
     result = live * cot
     result_all[dp] = result
@@ -525,10 +622,12 @@
 
     columns[0] = jnp.broadcast_to(log_step[...], (128, width)).T
     columns[1] = jnp.broadcast_to(skip_gain[...], (128, width)).T
-    own_step = columns[0, pl.ds(first, chans), :]
     own_skip = columns[1, pl.ds(first, chans), :]
     for load in loads[:3]:
         load.wait()
+    turn = (128 - blk * chans % 128) % 128
+    own = [pltpu.roll(windows[k], turn, 1).T[:chans] for k in range(4)]
+    rate_own[...], freq_own[...], coef_own[0], coef_own[1] = own
 
     def ssm():
         return columns[0, pl.ds(first, chans), :], rate_own[...], freq_own[...], (coef_own[0], coef_own[1])
@@ -536,15 +635,17 @@
     kern_slot = ssm_setup(n_blk, ssm(), consts, base)
     lead_slot = kern_slot - 1
     base_flat = base.reshape(8 * chans, 128)
-    groups(chans, GROUP, lambda group: make_powers(group, chans, consts, kern_slot, base_flat, q_ref, taps))
+    groups(0, chans, lambda group: make_powers(group, chans, consts, kern_slot, base_flat, q_ref, taps))
     shift_taps(own_skip, taps, base)
-    groups(chans, GROUP, lambda group: make_band(group, chans, base_flat, t_ref))
+    groups(0, chans, lambda group: make_band(group, chans, base_flat, t_ref))
 
     x_flat = x_all.reshape(n_blk * chans, 128)
     y_flat = y_send.reshape(n_blk * chans, 128)
-    wait_all(to_x)
-    groups(chans, GROUP, lambda group: forward_group(group, chans, n_blk, consts, lead_slot, x_flat, q_ref, t_ref, h_ref, y_flat))
-    to_y = links.exchange(y_send, y_all)
+    to_y = []
+    for part, arriving in zip(halves, to_x):
+        wait_all(arriving)
+        groups(*part, lambda group: forward_group(group, chans, n_blk, consts, lead_slot, x_flat, q_ref, t_ref, h_ref, y_flat))
+        to_y += links.exchange(y_send, y_all, *part)
 
     gather_result.relay()
     loads[3].wait()
@@ -563,10 +664,9 @@
     wait_all(to_y)
     conv = y_all.reshape(width, rows)[...].T
     gelu_out, gelu_slope = gelu_parts(conv)
-    conv_keep[...] = gelu_slope
+    slope_keep[...] = gelu_slope
     gelu_low = gelu_out.astype(BF16)
-    gelu_all[dp] = gelu_low.astype(F32)
-    gather_gelu = Gather(links, gelu_all)
+    gelu_keep[...] = gelu_low
     glu_pre = nn(gelu_low, glu_w[...]) + glu_b[...]
     left = glu_pre[:, :width]
     gate = 0.5 + 0.5 * jnp.tanh(0.5 * glu_pre[:, width:])
@@ -580,182 +680,206 @@
     residual_keep[0] = residual
     residual_keep[1] = unit_mid
 
-    for k in range(4):
-        cut = slice(k * step, (k + 1) * step)
-        hidden, slope = gelu_parts(nn(feed, ffn_in[:, cut]) + in_b[:, cut])
-        grad_pre = (hidden_grad[:, cut] * slope).astype(BF16)
-        forward = nn(hidden.astype(BF16), ffn_out[cut, :])
-        back = nt(grad_pre, ffn_in[:, cut])
-        acc_out[...] = forward if k == 0 else acc_out[...] + forward
-        acc_feed[...] = back if k == 0 else acc_feed[...] + back
-        vec[7 + k : 8 + k, :] = token_sum(grad_pre.astype(F32))
-    gather_gelu.relay()
-    gather_feed.relay()
-
-    in_slice = ffn_in[:, pl.ds(rows_s, part_ff)]
-    in_b_slice = in_b[:, pl.ds(rows_s, part_ff)]
-    for k in range(n_dp):
-        hidden, slope = gelu_parts(nn(feed_all[k].astype(BF16), in_slice) + in_b_slice)
-        cut = slice(k * rows, (k + 1) * rows)
-        hidden_s[cut, :] = hidden.astype(BF16)
-        pre_s[cut, :] = (slice_grad[cut, :] * slope).astype(BF16)
-    half = width // 2
-    results = result_all[...].reshape(n_dp * rows, width).astype(BF16)
-
-    def out_view(piece):
+    pieces, arrivals = {}, {}
+
+    def piece(work):
+        pieces[work.__name__] = work
+
+    @piece
+    def own():
+        for k in range(4):
+            cut = slice(k * step, (k + 1) * step)
+            hidden, slope = gelu_parts(nn(feed, ffn_in[:, cut]) + in_b[:, cut])
+            grad_pre = (hidden_grad[:, cut] * slope).astype(BF16)
+            forward = nn(hidden.astype(BF16), ffn_out[cut, :])
+            back = nt(grad_pre, ffn_in[:, cut])
+            acc_out[...] = forward if k == 0 else acc_out[...] + forward
+            acc_feed[...] = back if k == 0 else acc_feed[...] + back
+            vec[7 + k : 8 + k, :] = token_sum(grad_pre.astype(F32))
+        block_out[...] = (residual_keep[0] + live * (acc_out[...] + out_b[...])).astype(BF16)
+
+    @piece
+    def glubwd():
+        grad_feed = acc_feed[...]
+        unit_mid = residual_keep[1]
+        vec[2:3, :] = token_sum(grad_feed * unit_mid)
+        vec[3:4, :] = token_sum(grad_feed)
+        vec[4:5, :] = token_sum(result_all[dp])
+        grad_res = cot_ref[...].astype(F32) + norm_back(grad_feed, n2g[...], unit_mid, scale_mid)
+        residual_grad[...] = grad_res
+        grad_left = live * grad_res
+        left, gate = gate_keep[0], gate_keep[1]
+        to_left = (grad_left * gate).astype(BF16)
+        to_gate = (grad_left * left * gate * (1.0 - gate)).astype(BF16)
+        dglu[:, :width] = to_left
+        dglu[:, width:] = to_gate
+        vec[5:6, :] = token_sum(to_left.astype(F32))
+        vec[6:7, :] = token_sum(to_gate.astype(F32))
+
+    @piece
+    def dy():
+        dy_send[...] = (nt(dglu[...], glu_w[...]) * slope_keep[...]).T
+        arrivals["dy"] = links.exchange(dy_send.reshape(n_blk, chans, rows), dy_all, 0, chans)
+
+    @piece
+    def slice_all():
+        gather_feed.relay()
+        in_slice = ffn_in[:, pl.ds(rows_s, part_ff)]
+        in_b_slice = in_b[:, pl.ds(rows_s, part_ff)]
+        for k in range(n_dp):
+            hidden, slope = gelu_parts(nn(feed_all[k].astype(BF16), in_slice) + in_b_slice)
+            cut = slice(k * rows, (k + 1) * rows)
+            hidden_s[cut, :] = hidden.astype(BF16)
+            pre_s[cut, :] = (slice_grad[cut, :] * slope).astype(BF16)
+
+    part_gl = 2 * width // n_dp
+    shapes = piece_shapes(n_dp, n_blk, width, ff)
+    chunks = {}
+
+    def window(ref, row0, col0, rows_at, cols):
         def view(mask, row, size):
-            at = pl.multiple_of(links.dp_peer(mask) * part_ff + row, 8)
-            return sum_out.at[pl.ds(at, size), pl.ds(piece * half, half)]
+            slot = links.dp_peer(mask)
+            row_at = pl.multiple_of(slot * rows_at[0] + row0 + row, 8)
+            col_at = pl.multiple_of(slot * rows_at[1] + col0, 128) if rows_at[1] else col0
+            return ref.at[pl.ds(row_at, size), pl.ds(col_at, cols)]
         return view
 
-    half_ff = part_ff // 2
-
-    def in_view(piece):
-        def view(mask, row, size):
-            at = pl.multiple_of(links.dp_peer(mask) * part_ff + piece * half_ff, 128)
-            return sum_in.at[pl.ds(pl.multiple_of(row, 8), size), pl.ds(at, half_ff)]
-        return view
-
-    part_gl = 2 * width // n_dp
-
-    def glu_view(mask, row, size):
-        at = pl.multiple_of(links.dp_peer(mask) * part_gl, 128)
-        return sum_glu.at[pl.ds(pl.multiple_of(row, 8), size), pl.ds(at, part_gl)]
-
-    bits = [1 << k for k in range(n_blk.bit_length() - 1)]
-    orders = [(bits, 2), ([bits[1], bits[0]] + bits[2:], len(bits))]
-
-    part_out0[...] = tn(hidden_s[...], results[:, :half])
-    out0 = Chunk(links, part_out0, land_out0, out_view(0), *orders[0])
-    out0.advance()
-    part_out1[...] = tn(hidden_s[...], results[:, half:])
-    out1 = Chunk(links, part_out1, land_out1, out_view(1), *orders[1])
-    out1.advance()
-    feeds = feed_all[...].reshape(n_dp * rows, width).astype(BF16)
-    part_in0[...] = tn(feeds, pre_s[:, :half_ff])
-    in0 = Chunk(links, part_in0, land_in0, in_view(0), *orders[0])
-    in0.advance()
-    part_in1[...] = tn(feeds, pre_s[:, half_ff:])
-    in1 = Chunk(links, part_in1, land_in1, in_view(1), *orders[1])
-    in1.advance()
-
-    grad_feed = acc_feed[...]
-    unit_mid = residual_keep[1]
-    vec[2:3, :] = token_sum(grad_feed * unit_mid)
-    vec[3:4, :] = token_sum(grad_feed)
-    vec[4:5, :] = token_sum(result)
-    grad_res = cot_ref[...].astype(F32) + norm_back(grad_feed, n2g[...], unit_mid, scale_mid)
-    residual_grad[...] = grad_res
-    grad_left = live * grad_res
-    left, gate = gate_keep[0], gate_keep[1]
-    dglu[:, :width] = (grad_left * gate).astype(BF16).astype(F32)
-    dglu[:, width:] = (grad_left * left * gate * (1.0 - gate)).astype(BF16).astype(F32)
-    to_glu = []
-    for mask in range(1, n_dp):
-        at = pl.multiple_of(links.dp_peer(mask) * part_gl, 128)
-        to_glu.append(links.copy(dglu.at[:, pl.ds(at, part_gl)], dglu_all.at[dp], mask, 0))
-    dglu_all[dp] = dglu[:, pl.ds(pl.multiple_of(dp * part_gl, 128), part_gl)]
-    vec[5:6, :] = token_sum(dglu[:, :width])
-    vec[6:7, :] = token_sum(dglu[:, width:])
-    grad_gelu = nt(dglu[...].astype(BF16), glu_w[...])
-    dy_send[...] = (grad_gelu * conv_keep[...]).T
-    to_dy = links.exchange(dy_send.reshape(n_blk, chans, rows), dy_all)
-    block_out[...] = (residual_keep[0] + live * (acc_out[...] + out_b[...])).astype(BF16)
-
-    out0.advance()
-    out1.advance()
-    wait_all(to_glu)
-    gelus = gelu_all[...].reshape(n_dp * rows, width).astype(BF16)
-    part_glu[...] = tn(gelus, dglu_all[...].reshape(n_dp * rows, part_gl).astype(BF16))
-    glu = Chunk(links, part_glu, land_glu, glu_view, *orders[0])
-    glu.advance()
-    in0.advance()
-    in1.advance()
-    out0.advance()
-    out1.advance()
-
-    wait_all(to_dy)
+    def start_chunk(k):
+        if k not in shapes:
+            return
+        kind, row0, col0, rows_k, cols_k, plan = shapes[k]
+        rows_cut, cols_cut = slice(row0, row0 + rows_k), slice(col0, col0 + cols_k)
+        if kind == "glu":
+            part_glu[rows_cut, :] = tn(gelu_keep[:, rows_cut], dglu[...])
+            part = window(part_glu, row0, 0, (0, part_gl), part_gl)
+            total = window(sum_glu, row0, 0, (0, part_gl), part_gl)
+        elif kind == "out":
+            results = result_all[:, :, cols_cut].reshape(n_dp * rows, cols_k).astype(BF16)
+            part_out[rows_cut, cols_cut] = tn(hidden_s[:, rows_cut], results)
+            part = window(part_out, row0, col0, (0, 0), cols_k)
+            total = window(sum_out, row0, col0, (part_ff, 0), cols_k)
+        else:
+            feeds = feed_all[:, :, rows_cut].reshape(n_dp * rows, rows_k).astype(BF16)
+            part_in[rows_cut, cols_cut] = tn(feeds, pre_s[:, cols_cut])
+            part = window(part_in, row0, col0, (0, 0), cols_k)
+            total = window(sum_in, row0, col0, (0, part_ff), cols_k)
+        chunks[k] = Chunk(links, rows_k, part, total, landings[k], kind == "glu", plan)
+        chunks[k].advance()
+
     dy_flat = dy_all.reshape(n_blk * chans, 128)
     dx_flat = dx_send.reshape(n_blk * chans, 128)
-    groups(chans, GROUP, lambda group: backward_group(group, chans, n_blk, consts, lead_slot, x_flat, dy_flat, q_ref, t_ref, h_ref, dx_flat, a_ref, b_ref, g_ref))
-    to_dx = links.exchange(dx_send, dx_all)
-    for chunk in (in0, in1, glu, out0, out1):
-        chunk.advance()
-    split_lags(g_ref, base)
-    groups(chans, GROUP, lambda group: near_sums(group, chans, base_flat, q_ref, a_ref, b_ref))
-    rate_freq, coefs, d_step, d_skip = finish(chans, ssm(), a_ref, b_ref, g_ref)
-    own_par[:, 0, :] = rate_freq
-    own_par[:, 1, :] = coefs
-    pair = jnp.where(iota((chans, 128), 1) == 0, d_step, jnp.where(iota((chans, 128), 1) == 1, d_skip, 0.0))
-    if chans < 128:
-        pair = jnp.concatenate([pair, jnp.zeros((128 - chans, 128), F32)], axis=0)
-    pair = pair.T[0:8]
-    if width > 128:
-        pair = jnp.concatenate([pair, jnp.zeros((8, width - 128), F32)], axis=1)
-    pair = pltpu.roll(pair, blk * chans, 1)
-    vec[11:13, :] = pair[0:2]
-    vec[13:16, :] = jnp.zeros((3, width), F32)
-    for chunk in (in0, in1, glu, out0, out1):
-        chunk.advance()
-
-    wait_all(to_dx)
-    back = dx_all.reshape(width, rows)[...].T
-    high, rest = split(back)
-    rest, last = split(back - high.astype(F32))
-    grad_normed = live * (nn(flip, high) + (nn(flip, rest) + nn(flip, last)))
-    unit = unit_keep[...]
-    vec[0:1, :] = token_sum(grad_normed * unit)
-    vec[1:2, :] = token_sum(grad_normed)
-    grad_in[...] = residual_grad[...] + norm_back(grad_normed, n1g[...], unit, scale1)
-
-    waits = []
-    for mask in range(1, n_dp):
-        at = links.dp_peer(mask) * quarter
-        waits.append(links.copy(own_par.at[pl.ds(at, quarter)], dp_par.at[dp], mask, 0))
-        waits.append(links.copy(vec, dp_vec.at[dp], mask, 0))
-    dp_par[dp] = own_par[pl.ds(dp * quarter, quarter)]
-    dp_vec[dp] = vec[...]
-    for chunk in (in0, in1, glu, out0, out1):
-        chunk.advance()
-    wait_all(waits)
-    sum_par[...] = sum_slots(dp_par, n_dp)
-    sum_vec[...] = sum_slots(dp_vec, n_dp)
-    waits = []
-    for mask in range(1, n_blk):
-        waits.append(links.copy(sum_par, blk_par.at[blk], 0, mask))
-        waits.append(links.copy(sum_vec, blk_vec.at[blk], 0, mask))
-    blk_par[blk] = sum_par[...]
-    blk_vec[blk] = sum_vec[...]
-    for chunk in (in0, in1, glu, out0, out1):
-        chunk.advance()
-    wait_all(waits)
-    all_par[dp] = blk_par[...]
-    gather_par = Gather(links, all_par)
-    vec_out[...] = sum_slots(blk_vec, n_blk)
-    for chunk in (in0, in1, glu, out0, out1):
-        chunk.advance()
-    gather_par.relay()
-    state = rate_out.shape[1]
-    for b in range(n_blk):
-        for d in range(n_dp):
-            at = b * chans + d * quarter
-            block = all_par[d, b]
-            rate_out[at : at + quarter, :] = block[:, 0, :state]
-            freq_out[at : at + quarter, :] = block[:, 0, state:]
-            coef_out[0, at : at + quarter, :] = block[:, 1, :state]
-            coef_out[1, at : at + quarter, :] = block[:, 1, state:]
-    for _ in range(8):
-        for chunk in (in0, in1, glu, out0, out1):
+
+    def backward(k):
+        if k == 0:
+            wait_all(arrivals["dy"])
+        size = min(GROUP, chans)
+        if k * size < chans:
+            backward_group([k * size + i for i in range(size)], chans, n_blk, consts, lead_slot, x_flat, dy_flat, q_ref, t_ref, h_ref, dx_flat, a_ref, b_ref, g_ref)
+        if k == 3:
+            groups(4 * size, chans - 4 * size, lambda group: backward_group(group, chans, n_blk, consts, lead_slot, x_flat, dy_flat, q_ref, t_ref, h_ref, dx_flat, a_ref, b_ref, g_ref))
+            arrivals["dx"] = links.exchange(dx_send, dx_all, 0, chans)
+
+    @piece
+    def near():
+        split_lags(g_ref, base)
+        groups(0, chans, lambda group: near_sums(group, chans, base_flat, q_ref, a_ref, b_ref))
+        rate_freq, coefs, d_step, d_skip = finish(chans, ssm(), a_ref, b_ref, g_ref)
+        own_par[:, 0, :] = rate_freq
+        own_par[:, 1, :] = coefs
+        lane = iota((chans, 128), 1)
+        pair = jnp.where(lane == 0, d_step, jnp.where(lane == 1, d_skip, 0.0))
+        if chans < 128:
+            pair = jnp.concatenate([pair, jnp.zeros((128 - chans, 128), F32)], axis=0)
+        pair = pair.T[0:8]
+        if width > 128:
+            pair = jnp.concatenate([pair, jnp.zeros((8, width - 128), F32)], axis=1)
+        pair = pltpu.roll(pair, blk * chans, 1)
+        vec[11:13, :] = pair[0:2]
+        vec[13:16, :] = jnp.zeros((3, width), F32)
+
+    @piece
+    def ln1():
+        wait_all(arrivals["dx"])
+        back = dx_all.reshape(width, rows)[...].T
+        high, rest = split(back)
+        rest, last = split(back - high.astype(F32))
+        grad_normed = live * (nn(flip, high) + (nn(flip, rest) + nn(flip, last)))
+        unit = unit_keep[...]
+        vec[0:1, :] = token_sum(grad_normed * unit)
+        vec[1:2, :] = token_sum(grad_normed)
+        grad_in[...] = residual_grad[...] + norm_back(grad_normed, n1g[...], unit, scale1)
+
+    @piece
+    def s0():
+        waits = arrivals["s0"] = []
+        for mask in range(1, n_dp):
+            at = links.dp_peer(mask) * quarter
+            waits.append(links.copy(own_par.at[pl.ds(at, quarter)], dp_par.at[dp], mask, 0))
+            waits.append(links.copy(vec, dp_vec.at[dp], mask, 0))
+        dp_par[dp] = own_par[pl.ds(dp * quarter, quarter)]
+        dp_vec[dp] = vec[...]
+
+    @piece
+    def s1():
+        wait_all(arrivals["s0"])
+        sum_par[...] = sum_slots(dp_par, n_dp)
+        sum_vec[...] = sum_slots(dp_vec, n_dp)
+        waits = arrivals["s1"] = []
+        for mask in range(1, n_blk):
+            waits.append(links.copy(sum_par, blk_par.at[blk], 0, mask))
+            waits.append(links.copy(sum_vec, blk_vec.at[blk], 0, mask))
+        blk_par[blk] = sum_par[...]
+        blk_vec[blk] = sum_vec[...]
+
+    @piece
+    def s2():
+        wait_all(arrivals["s1"])
+        all_par[dp] = blk_par[...]
+        arrivals["s2"] = Gather(links, all_par)
+        vec_out[...] = sum_slots(blk_vec, n_blk)
+
+    @piece
+    def s3():
+        arrivals["s2"].relay()
+        state = par_out.shape[0] // 4
+        for b in range(n_blk):
+            for d in range(n_dp):
+                at = b * chans + d * quarter
+                block = all_par[d, b]
+                flat_par[0, at : at + quarter, :] = block[:, 0, :]
+                flat_par[1, at : at + quarter, :] = block[:, 1, :]
+        par_out[: 2 * state, :] = flat_par[0].T
+        par_out[2 * state :, :] = flat_par[1].T
+
+    for token in ORDER:
+        if isinstance(token, int):
+            if token in chunks:
+                chunks[token].advance()
+        elif token.startswith("part"):
+            start_chunk(int(token[4:]))
+        elif token.startswith("bwd"):
+            backward(int(token[3:]))
+        else:
+            pieces["slice_all" if token == "slice" else token]()
+    while any(chunk.live for chunk in chunks.values()):
+        for chunk in chunks.values():
             chunk.advance()
-    stores = [
-        pltpu.make_async_copy(src, dst, load_sems.at[k])
-        for k, (src, dst) in enumerate([(sum_glu, grad_glu_out), (sum_in, grad_in_out), (sum_out, grad_out_out)])
-    ]
-    for store in stores:
-        store.start()
     links.finish()
-    for store in stores:
-        store.wait()
+
+
+def piece_shapes(n_dp, n_blk, width, ff):
+    shapes = {}
+    n_glu, n_ffn = len(GLU_PLANS), len(FFN_PLANS) // 2
+    size = width // n_glu
+    for k, plan in enumerate(GLU_PLANS):
+        shapes[k] = ("glu", k * size, 0, size, 2 * width // n_dp, plan)
+    for kind, at, height, breadth in (("out", n_glu, ff // n_dp, width), ("in", n_glu + n_ffn, width, ff // n_dp)):
+        cols = min(n_ffn, breadth // 128)
+        cuts = min(n_ffn // cols, height // (8 * n_blk))
+        high, wide = height // cuts, breadth // cols
+        for k in range(cols * cuts):
+            shapes[at + k] = (kind, k % cuts * high, k // cuts * wide, high, wide, FFN_PLANS[at - n_glu + k])
+    return shapes
 
 
 def sum_slots(ref, count):
@@ -763,6 +887,28 @@
     for k in range(1, count):
         total = total + ref[k]
     return total
+
+
+def deliver_kernel(big_in, vec, par, others, big_out, rows_out, rate, freq, coef, others_out, sems):
+    states = rate.shape[0]
+    moves = []
+    for src, dst in zip(big_in, big_out):
+        part = src.shape[0] // BIG_PARTS
+        moves += [(src.at[pl.ds(k * part, part)], dst.at[pl.ds(k * part, part)]) for k in range(BIG_PARTS)]
+    moves += list(zip(others, others_out))
+    moves += [(par.at[pl.ds(0, states)], rate), (par.at[pl.ds(states, states)], freq)]
+    moves += [(par.at[pl.ds((2 + k) * states, states)], coef.at[k]) for k in range(2)]
+    copies = [pltpu.make_async_copy(src, dst, sems.at[k]) for k, (src, dst) in enumerate(moves)]
+    for copy in copies:
+        copy.start()
+    row = 0
+    for out in rows_out:
+        count = out.shape[1] // vec.shape[1]
+        for k in range(count):
+            out[:, k * vec.shape[1] : (k + 1) * vec.shape[1]] = vec[row : row + 1, :]
+            row += 1
+    for copy in copies:
+        copy.wait()
 
 
 def on_device(n_dp, n_blk, block_in, seq_lengths, norm1_gain, norm1_bias, log_step, log_rate, frequency, out_coef, skip_gain, glu_weight, glu_bias, norm2_gain, norm2_bias, ffn_in, ffn_in_bias, ffn_out, ffn_out_bias, cotangent):
@@ -774,55 +920,76 @@
     vmem, anywhere = pl.BlockSpec(memory_space=VMEM), pl.BlockSpec(memory_space=pl.ANY)
     shape = jax.ShapeDtypeStruct
     outs = [
-        (shape((rows, width), BF16), vmem),
-        (shape((rows, width), F32), vmem),
-        (shape((width, 2 * width), F32), anywhere),
-        (shape((width, ff), F32), anywhere),
-        (shape((ff, width), F32), anywhere),
-        (shape((VEC_ROWS, width), F32), vmem),
-        (shape((width, states), F32), vmem),
-        (shape((width, states), F32), vmem),
-        (shape((2, width, states), F32), vmem),
+        shape((rows, width), BF16), shape((rows, width), F32),
+        shape((width, 2 * width), F32), shape((width, ff), F32), shape((ff, width), F32),
+        shape((VEC_ROWS, width), F32), shape((4 * states, width), F32),
     ]
     part_ff, part_gl = ff // n_dp, 2 * width // n_dp
     tokens = n_dp * rows
-    parts = [(width, part_gl), (width, part_ff // 2), (width, part_ff // 2), (part_ff, width // 2), (part_ff, width // 2)]
     f32 = lambda *dims: VMEM(dims, F32)
     bf16 = lambda *dims: VMEM(dims, BF16)
     dma = lambda n: pltpu.SemaphoreType.DMA((n,))
+    shapes = piece_shapes(n_dp, n_blk, width, ff)
+    landings = []
+    for k in range(len(GLU_PLANS) + len(FFN_PLANS)):
+        kind, _, _, rows_k, cols_k, plan = shapes.get(k, ("out", 0, 0, 8 * n_blk, 128, FFN_PLANS[0]))
+        landings.append(f32(landing_rows(rows_k, plan[0], n_dp, n_blk, kind == "glu"), cols_k))
     scratch = [
         dma(LINK_SEMS), dma(LINK_SEMS), dma(8),
         bf16(width, 2 * width), bf16(width, ff), bf16(ff, width),
-        f32(chans, states), f32(chans, states), f32(2, chans, states), f32(2, width, 128),
+        f32(4, states, 128), f32(chans, states), f32(chans, states), f32(2, chans, states), f32(2, width, 128),
         f32(width, rows), f32(n_blk, chans, rows), f32(n_blk, chans, rows), f32(n_blk, chans, rows),
         f32(width, rows), f32(n_blk, chans, rows), f32(n_blk, chans, rows), f32(n_blk, chans, rows),
         bf16(chans, 256, 128), bf16(chans, 256, 128), f32(chans, n_blk, 128), f32(n_consts(n_blk), chans, 128),
         f32(8, chans, 128), f32(chans, 128), f32(2 * chans, 128), f32(2 * chans, 128), f32(chans, 128),
-        f32(n_dp, rows, width), f32(n_dp, rows, width), f32(n_dp, rows, width),
-        f32(rows, 2 * width), f32(n_dp, rows, part_gl),
+        f32(n_dp, rows, width), f32(n_dp, rows, width),
+        bf16(rows, 2 * width),
         f32(rows, ff), f32(tokens, part_ff), bf16(tokens, part_ff), bf16(tokens, part_ff),
         f32(rows, width), f32(rows, width), f32(2, rows, width), f32(2, rows, width),
-        f32(rows, width), f32(rows, width), f32(rows, width),
-        *[f32(*p) for p in parts], *[f32(*p) for p in parts],
-        f32(width, 2 * width), f32(width, ff), f32(ff, width),
-        f32(chans, 2, 128), f32(n_dp, quarter, 2, 128), f32(quarter, 2, 128), f32(n_blk, quarter, 2, 128), f32(n_dp, n_blk, quarter, 2, 128),
+        bf16(rows, width), f32(rows, width), f32(rows, width), f32(rows, width),
+        f32(width, 2 * width), f32(width, part_ff), f32(part_ff, width),
+        f32(chans, 2, 128), f32(n_dp, quarter, 2, 128), f32(quarter, 2, 128), f32(n_blk, quarter, 2, 128),
+        f32(n_dp, n_blk, quarter, 2, 128), f32(2, width, 128),
         f32(VEC_ROWS, width), f32(n_dp, VEC_ROWS, width), f32(VEC_ROWS, width), f32(n_blk, VEC_ROWS, width),
+        *landings,
     ]
     out = pl.pallas_call(
         functools.partial(whole_kernel, n_dp, n_blk),
-        out_shape=[o[0] for o in outs],
-        out_specs=[o[1] for o in outs],
+        out_shape=[VMEM(v.shape, v.dtype) for v in outs],
+        out_specs=[vmem] * len(outs),
         in_specs=[vmem, pl.BlockSpec(memory_space=pltpu.SMEM), vmem, vmem, vmem, vmem, anywhere, anywhere, anywhere, vmem, anywhere, vmem, vmem, vmem, anywhere, vmem, anywhere, vmem],
         scratch_shapes=scratch,
-        compiler_params=pltpu.CompilerParams(collective_id=0, has_side_effects=True, vmem_limit_bytes=60 * 2**20),
+        compiler_params=pltpu.CompilerParams(collective_id=0, has_side_effects=True, vmem_limit_bytes=44 * 2**20),
     )(
-        block_in[0], seq_lengths, cotangent[0], row(norm1_gain), row(norm1_bias), row(log_step), log_rate, frequency, out_coef,
-        row(skip_gain), glu_weight, row(glu_bias), row(norm2_gain), row(norm2_bias), ffn_in, row(ffn_in_bias), ffn_out, row(ffn_out_bias),
+        block_in[0], seq_lengths, cotangent[0], row(norm1_gain), row(norm1_bias), row(log_step), log_rate.T, frequency.T,
+        out_coef.swapaxes(1, 2), row(skip_gain), glu_weight, row(glu_bias), row(norm2_gain), row(norm2_bias), ffn_in,
+        row(ffn_in_bias), ffn_out, row(ffn_out_bias),
     )
-    block_out, grad_in, g_glu, g_in, g_out, vec, rate, freq, coef = out
+    block_out, grad_in, g_glu, g_in, g_out, vec, par = out
+    widths = [width, width, width, width, width, 2 * width, ff, width, width]
+    made = [shape((rows, width), BF16), shape((rows, width), F32)]
+    big = [shape(v.shape, F32) for v in (g_glu, g_in, g_out)]
+    small = [shape((1, w), F32) for w in widths]
+    params = [shape((states, width), F32), shape((states, width), F32), shape((2, states, width), F32)]
+    out_shapes = made + big + small + params
+
+    def deliver(block_out, grad_in, g_glu, g_in, g_out, vec, par, *rest):
+        outs, sems = rest[:-1], rest[-1]
+        deliver_kernel([g_glu, g_in, g_out], vec, par, [block_out, grad_in], outs[2:5], outs[5:14], *outs[14:], outs[:2], sems)
+
+    done = pl.pallas_call(
+        deliver,
+        out_shape=out_shapes,
+        in_specs=[vmem] * 7,
+        out_specs=[anywhere] * 5 + [vmem] * 9 + [anywhere] * 3,
+        scratch_shapes=[dma(32)],
+        compiler_params=pltpu.CompilerParams(vmem_limit_bytes=8 * 2**20),
+    )(*out)
+    flat = [v.reshape(-1) for v in done[5:14]]
+    n1_gain, n1_bias, n2_gain, n2_bias, ffn_out_b, glu_b, ffn_in_b, d_step, d_skip = flat
     return (
-        block_out[None], grad_in[None], vec[0], vec[1], vec[11], rate, freq, coef, vec[12],
-        g_glu, vec[5:7].reshape(-1), vec[2], vec[3], g_in, vec[7:11].reshape(-1), g_out, vec[4],
+        done[0][None], done[1][None], n1_gain, n1_bias, d_step, done[14].T, done[15].T, done[16].swapaxes(1, 2), d_skip,
+        done[2], glu_b, n2_gain, n2_bias, done[3], ffn_in_b, done[4], ffn_out_b,
     )
 
 

time: 187 us -> 122 us (0.65)
  Pallas kernels: 157 us -> 120 us
  local copies, waits for them, and re-layouts: 27.2 us -> 0 us
    pallas_call x1 -> x2, Pallas kernels: 157 us -> 120 us  [the longest x1 115 us: on_device(): pl.pallas_call(functools.partial(whole_kernel, n_dp, n_blk), out_shape=[V...]
    unnamed x19 -> x0, local copies, waits for them, and re-layouts: 25.7 us -> none
where the time goes in v3:
time: 122 us; the launch traced here: 121 us
  Pallas kernels  120 us (98%)
  between operations  1.5 us (1%)
    pallas_call x1, Pallas kernels, on_device(): pl.pallas_call(functools.partial(whole_kernel, n_dp, n_blk), out_shape=[V...  115 us
    pallas_call x1, Pallas kernels, on_device(): pl.pallas_call(deliver, out_shape=out_shapes, in_specs=[vmem] * 7, out_sp...  5.09 us

profile of v3, /device:TPU:0, one launch (start us, length us, event | category | flops | bytes accessed | tf_op | source)
XLA Modules:
  0.0 121.5 jit_solution(16516584034026013585)
XLA Ops:
  1.3 114.9 %shard_map.305 = (bf16[128,512]{1,0:T(8,128)(2,1)S(1)}, f32[128,512]{1,0:T(8,128)S(1)}, f32[512,1024]{1,0:T(8,128)S(1)}, f32[512,2048]{1,0:T(8,128)S(1)}, f32[20...) custom-call(bf16[128,512]{1,0:T(8,128)(2,1)} %bitcast.29, s32[1]{0:T(128)S(6)} %copy.35.lengths, ...), custom_call_target="tpu_custom_call" | custom-call | tf_op jit(solution)/shard_map/pallas_call | solution.py:956
  116.2 5.1 %shard_map.306 = (bf16[128,512]{1,0:T(8,128)(2,1)}, f32[128,512]{1,0:T(8,128)}, f32[512,1024]{1,0:T(8,128)}, f32[512,2048]{1,0:T(8,128)}, f32[2048,512]{1,0:T(8,...) custom-call(bf16[128,512]{1,0:T(8,128)(2,1)S(1)} %get-tuple-element., ...), custom_call_target="tpu_custom_call" | custom-call | tf_op jit(solution)/shard_map/pallas_call | solution.py:980

commit v4 on v3

--- a/solution.py
+++ b/solution.py
@@ -13,39 +13,44 @@
 PRECISE = lax.Precision.HIGHEST
 SERIES = 16
 GROUP = 16
-LINK_SEMS = 256
-BIG_PARTS = 4
+SEND_SEMS = 43
+RECV_SEMS = 191
+BIG_PARTS = 1
+FIRST_WHOLE = False
 GLU_PLANS = (
-    (("c", "y", "x", "z0", "z1"), 0),
-    (("c", "z0", "y", "x", "z1"), 2),
+    (("c", "x", "z0", "y", "z1"), 3),
+    (("c", "y", "x", "z0", "z1"), 3),
+    (("c", "z0", "x", "y", "z1"), 2),
+    (("c", "y", "x", "z0", "z1"), 3),
 )
 FFN_PLANS = (
+    (("x", "z0", "z1"), 2),
+    (("x", "z1", "z0"), 2),
+    (("z1", "x", "z0"), 3),
+    (("x", "z0", "z1"), 2),
+    (("x", "z0", "z1"), 2),
+    (("z0", "x", "z1"), 2),
+    (("x", "z0", "z1"), 2),
+    (("x", "z0", "z1"), 2),
+    (("z1", "x", "z0"), 1),
     (("x", "z0", "z1"), 3),
-    (("x", "z0", "z1"), 2),
     (("x", "z0", "z1"), 3),
-    (("x", "z0", "z1"), 2),
-    (("x", "z1", "z0"), 3),
-    (("x", "z0", "z1"), 3),
-    (("x", "z0", "z1"), 2),
+    (("z0", "x", "z1"), 0),
+    (("x", "z1", "z0"), 2),
     (("x", "z0", "z1"), 3),
     (("x", "z0", "z1"), 1),
-    (("z0", "x", "z1"), 3),
-    (("x", "z0", "z1"), 1),
-    (("x", "z1", "z0"), 1),
-    (("z1", "x", "z0"), 3),
-    (("x", "z0", "z1"), 3),
-    (("z0", "x", "z1"), 2),
-    (("x", "z0", "z1"), 2),
+    (("x", "z0", "z1"), 0),
 )
 ORDER = (
-    "own", "glubwd", "dy", "part0", "part1", 0, 1, "slice", "part2", "part3", "part4", "part5", "part6",
-    "part7", "part8", "part9", "part10", "part11", 2, "part12", 0, "part13", 3, 1, "part14", "part15",
-    "part16", 4, 11, 2, "part17", 5, 3, "bwd0", 6, 1, 7, 14, 16, 4, 8, 2, 5, 3, 9, 6, 7, 10, 4, 8, 12, 2,
-    "bwd1", 5, 3, 9, 6, 0, 7, 10, 4, 13, 8, 12, 15, 2, 11, 5, 3, "bwd2", 6, 9, 17, 0, 1, 7, 14, 10, 16, 3, 4,
-    2, 13, 8, "bwd3", 12, 15, 11, 5, 6, "near", 3, 9, 2, 17, 4, 0, 5, 1, 7, 14, 10, 3, 2, 13, 16, 8, 4, 0, 10,
-    4, 6, 8, "ln1", 12, 15, 5, "s0", 11, 9, 7, 17, 6, 12, 5, 14, 1, 13, 16, 8, 6, "s1", 11, 9, 8, 0, 10, 14,
-    15, 7, 17, 13, 1, 12, 16, 7, "s2", 9, 11, 10, 9, 1, 0, 10, 16, 12, 15, 17, 14, 12, "s3", 13, 11, 0, 17,
-    15, 11, 1, 0, 14, 13, 1, 16, 14, 15, 13, 17, 16, 15, 17,
+    "own", "glubwd", "dy", "part0", "part1", "part2", "part3", 0, 1, 2, 3, "slice", "part4", "part5", "part6",
+    0, "part7", 1, "part8", "part9", "part10", 2, "part11", "part12", "part13", "part14", 4, "part15",
+    "part16", 3, "part17", "part18", 5, "part19", 0, 6, "bwd0", 7, 9, 1, 0, 8, 4, 12, "bwd1", 7, 5, 1, 10, 0,
+    11, 8, 15, 2, 4, "bwd2", 7, 5, 1, 14, 8, 11, 13, 10, 0, 16, 3, 2, 7, 5, 4, "bwd3", 1, 8, 14, 11, 17, 13,
+    19, 10, 0, 18, 6, "near", 9, 7, 12, 5, 3, 16, 2, 15, 4, 7, 0, 5, 1, 8, "ln1", 14, 11, 17, 7, 4, "s0", 13,
+    19, 0, 10, 18, 6, 7, 8, 5, 9, 12, 0, 3, 16, 1, 2, "s1", 5, 15, 14, 11, 17, 4, 13, 19, 10, 1, 6, 18, 15, 4,
+    8, 9, 12, 2, 11, 3, 16, 19, 1, "s2", 8, 14, 10, 9, 12, 17, 13, 6, 18, 2, 3, 15, 11, 16, 14, "s3", 11, 19,
+    17, 9, 18, 10, 16, 6, 12, 10, 2, 13, 14, 19, 3, 2, 15, 14, 6, 9, 17, 18, 6, 9, 13, 16, 13, 16, 3, 19, 12,
+    15, 3, 17, 19, 18, 12, 15, 17, 18,
 )
 VMEM = pltpu.VMEM
 
@@ -380,15 +385,6 @@
     return jnp.sum(values, axis=0, keepdims=True)
 
 
-class Transfer:
-    def __init__(self, copy):
-        self.copy, self.arrived = copy, False
-
-    def wait_recv(self):
-        self.arrived = True
-        self.copy.wait_recv()
-
-
 class Load:
     def __init__(self, src, dst, sem):
         self.copy, self.done = pltpu.make_async_copy(src, dst, sem), False
@@ -400,9 +396,48 @@
             self.copy.wait()
 
 
+class Batch:
+    def __init__(self, links, moves, total, send=None):
+        self.total, self.recv, self.arrived, self.left = total, links.recv.at[links.used_recv], False, False
+        links.used_recv += 1
+        if send is None:
+            send = links.send.at[links.used_send]
+            links.used_send += 1
+        self.send = send
+        links.open.append(self)
+        self.copies = []
+        for src, dst, dp_mask, blk_mask in moves:
+            copy = pltpu.make_async_remote_copy(
+                src_ref=src,
+                dst_ref=dst,
+                send_sem=self.send,
+                recv_sem=self.recv,
+                device_id=(links.dp_peer(dp_mask), links.blk_peer(blk_mask)),
+                device_id_type=pl.DeviceIdType.MESH,
+            )
+            copy.start()
+            self.copies.append(copy)
+
+    def wait_recv(self):
+        if not self.arrived:
+            self.arrived = True
+            if len(self.copies) == 1:
+                self.copies[0].wait_recv()
+            else:
+                pltpu.make_async_copy(self.total, self.total, self.recv).wait()
+
+    def wait_send(self):
+        if not self.left:
+            self.left = True
+            if len(self.copies) == 1:
+                self.copies[0].wait_send()
+            else:
+                pltpu.make_async_copy(self.total, self.total, self.send).wait()
+
+
 class Links:
     def __init__(self, send, recv, n_dp, n_blk):
-        self.send, self.recv, self.used, self.open = send, recv, 0, []
+        self.send, self.recv, self.used_send, self.used_recv, self.open = send, recv, 0, 0, []
         self.n_dp, self.n_blk = n_dp, n_blk
         self.dp, self.blk = lax.axis_index("dp"), lax.axis_index("blk")
 
@@ -411,21 +446,6 @@
 
     def blk_peer(self, mask):
         return jnp.bitwise_xor(self.blk, mask)
-
-    def copy(self, src, dst, dp_mask, blk_mask):
-        copy = pltpu.make_async_remote_copy(
-            src_ref=src,
-            dst_ref=dst,
-            send_sem=self.send.at[self.used],
-            recv_sem=self.recv.at[self.used],
-            device_id=(self.dp_peer(dp_mask), self.blk_peer(blk_mask)),
-            device_id_type=pl.DeviceIdType.MESH,
-        )
-        copy.start()
-        self.used += 1
-        copy = Transfer(copy)
-        self.open.append(copy)
-        return copy
 
     def greet(self):
         barrier = pltpu.get_barrier_semaphore()
@@ -442,30 +462,22 @@
         pl.semaphore_wait(pltpu.get_barrier_semaphore(), self.n_dp + self.n_blk - 2)
 
     def finish(self):
-        for transfer in self.open:
-            transfer.copy.wait_send()
+        for batch in self.open:
+            batch.wait_send()
 
     def stop(self):
-        for transfer in self.open:
-            if not transfer.arrived:
-                transfer.wait_recv()
+        for batch in self.open:
+            batch.wait_recv()
         for load in self.loads:
             load.wait()
         self.finish()
 
     def exchange(self, src, dst, first, size):
         part = pl.ds(first, size)
-        copies = [
-            self.copy(src.at[self.blk_peer(mask), part], dst.at[self.blk, part], 0, mask)
-            for mask in range(1, self.n_blk)
-        ]
+        moves = [(src.at[self.blk_peer(mask), part], dst.at[self.blk, part], 0, mask) for mask in range(1, self.n_blk)]
+        batch = Batch(self, moves, dst.at[pl.ds(0, self.n_blk - 1), part])
         dst[self.blk, part] = src[self.blk, part]
-        return copies
-
-
-def wait_all(copies):
-    for copy in copies:
-        copy.wait_recv()
+        return batch
 
 
 class Gather:
@@ -481,7 +493,7 @@
         slot = self.buf.at[self.links.dp_peer(mask)]
         for bit in reversed(self.bits):
             if bit < low:
-                self.got[mask | bit] = self.links.copy(slot, slot, bit, 0)
+                self.got[mask | bit] = Batch(self.links, [(slot, slot, bit, 0)], slot)
 
     def relay(self):
         for mask in sorted(range(1, self.links.n_dp), key=lambda m: bin(m).count("1")):
@@ -495,7 +507,8 @@
 
 
 class Chunk:
-    def __init__(self, links, rows, part, out, landing, every, plan):
+    def __init__(self, links, rows, part, out, landing, every, plan, measure):
+        self.measure = measure
         names = bit_names(links.n_dp, links.n_blk)
         order, late = plan
         spread = lambda tokens: [bit for token in tokens for bit in names[token]]
@@ -516,7 +529,15 @@
 
     def steps(self):
         links = self.links
-        held, low, size, lows, at = self.held, 0, self.rows, [], 0
+        held, low, size, lows, at, last_batch = self.held, 0, self.rows, [], 0, None
+        send = links.send.at[links.used_send]
+        links.used_send += 1
+
+        def move(moves, total):
+            if last_batch is not None:
+                last_batch.wait_send()
+            return Batch(links, moves, total, send)
+
         for k, (axis, bit) in enumerate(self.halving):
             last = k + 1 == len(self.halving)
             if axis == "blk":
@@ -530,28 +551,30 @@
             else:
                 moves = [(mask, mask ^ bit, low) for mask in held if mask & bit]
                 held = [mask for mask in held if not mask & bit]
-            slots, copies = {}, []
+            slots, copies, start = {}, [], at
+            dp_mask, blk_mask = (0, bit) if axis == "blk" else (bit, 0)
             for mask, there, row in moves:
                 slots[there] = self.landing.at[pl.ds(at, size), :]
                 at += size
-                dp_mask, blk_mask = (0, bit) if axis == "blk" else (bit, 0)
-                copies.append(links.copy(self.part(mask, row, size), slots[there], dp_mask, blk_mask))
+                copies.append((self.part(mask, row, size), slots[there], dp_mask, blk_mask))
+            last_batch = move(copies, self.landing.at[pl.ds(start, at - start), :])
             yield
-            wait_all(copies)
+            last_batch.wait_recv()
             for mask in held:
                 own = self.part(mask, low, size)
                 goal = self.out(mask, low, size) if last else own
                 goal[...] = own[...] + slots[mask][...]
         for axis, bit in self.doubling:
             place = [self.out(mask, low, size) for mask in held]
+            dp_mask, blk_mask = (0, bit) if axis == "blk" else (bit, 0)
+            total = self.measure.at[pl.ds(0, size * len(held)), pl.ds(0, place[0].shape[1])]
+            last_batch = move([(v, v, dp_mask, blk_mask) for v in place], total)
             if axis == "blk":
-                copies = [links.copy(v, v, 0, bit) for v in place]
                 low, size = lows.pop(), size * 2
             else:
-                copies = [links.copy(v, v, bit, 0) for v in place]
                 held = held + [mask | bit for mask in held]
             yield
-            wait_all(copies)
+            last_batch.wait_recv()
 
 
 def landing_rows(rows, order, n_dp, n_blk, every):
@@ -570,10 +593,10 @@
 
 
 def whole_kernel(
-    n_dp, n_blk, x_ref, lengths, cot_ref, n1g, n1b, log_step, log_rate, frequency, out_coef, skip_gain, glu_hbm, glu_b,
-    n2g, n2b, in_hbm, in_b, out_hbm, out_b,
+    n_dp, n_blk, x_hbm, lengths, cot_hbm, log_rate, frequency, out_coef, glu_hbm, in_hbm, out_hbm,
+    n1g_hbm, n1b_hbm, log_step_hbm, skip_hbm, glu_b_hbm, n2g_hbm, n2b_hbm, in_b_hbm, out_b_hbm,
     block_out, grad_in, sum_glu, sum_in, sum_out, vec_out, par_out,
-    send_sems, recv_sems, load_sems, glu_w, ffn_in, ffn_out, windows, rate_own, freq_own, coef_own, columns,
+    send_sems, recv_sems, load_sems, x_ref, cot_ref, n1g, n1b, log_step, skip_gain, glu_b, n2g, n2b, in_b, out_b, glu_w, ffn_in, ffn_out, windows, rate_own, freq_own, coef_own, columns,
     a_send, x_all, y_send, y_all, dy_send, dy_all, dx_send, dx_all,
     q_ref, t_ref, h_ref, consts, base, taps, a_ref, b_ref, g_ref,
     result_all, feed_all, dglu, hidden_grad, slice_grad, hidden_s, pre_s, slope_keep, unit_keep, residual_keep, gate_keep,
@@ -584,26 +607,38 @@
     ff = ffn_in.shape[1]
     chans = width // n_blk
     quarter = chans // n_dp
-    half = max(chans // 2, 8)
-    halves = [(first, half) for first in range(0, chans, half)]
+    size = min(GROUP, chans)
+    parts = [(first, size) for first in range(0, chans, size)]
+    first_parts = [(0, chans)] if FIRST_WHOLE else parts
     links = Links(send_sems, recv_sems, n_dp, n_blk)
     dp, blk = links.dp, links.blk
     first = pl.multiple_of(blk * chans, 8)
     lanes_at = pl.multiple_of(blk * chans // 128 * 128, 128)
 
-    loads = [
-        Load(src, dst, load_sems.at[k])
-        for k, (src, dst) in enumerate([
-            (log_rate.at[:, pl.ds(lanes_at, 128)], windows.at[0]),
-            (frequency.at[:, pl.ds(lanes_at, 128)], windows.at[1]),
-            (out_coef.at[:, :, pl.ds(lanes_at, 128)], windows.at[pl.ds(2, 2)]),
-            (out_hbm, ffn_out),
-            (glu_hbm, glu_w),
-            (in_hbm, ffn_in),
-        ])
-    ]
-    links.loads = loads
+    links.loads = []
+    sources = {
+        "x": (x_hbm, x_ref), "n1g": (n1g_hbm, n1g), "n1b": (n1b_hbm, n1b), "cot": (cot_hbm, cot_ref),
+        "rate": (log_rate.at[:, pl.ds(lanes_at, 128)], windows.at[0]),
+        "freq": (frequency.at[:, pl.ds(lanes_at, 128)], windows.at[1]),
+        "coef": (out_coef.at[:, :, pl.ds(lanes_at, 128)], windows.at[pl.ds(2, 2)]),
+        "step": (log_step_hbm, log_step), "skip": (skip_hbm, skip_gain), "out": (out_hbm, ffn_out),
+        "glu": (glu_hbm, glu_w), "glu_b": (glu_b_hbm, glu_b), "n2g": (n2g_hbm, n2g), "n2b": (n2b_hbm, n2b),
+        "in": (in_hbm, ffn_in), "in_b": (in_b_hbm, in_b), "out_b": (out_b_hbm, out_b),
+    }
+    loads = {}
+
+    def fetch(names):
+        for name in names:
+            loads[name] = Load(*sources[name], load_sems.at[len(loads)])
+            links.loads.append(loads[name])
+
+    def need(*names):
+        for name in names:
+            loads[name].wait()
+
     links.greet()
+    fetch(list(sources))
+    need("x", "n1g", "n1b")
 
     places = blk * rows + iota((rows, 1), 0)
     live = (places < lengths[0]).astype(F32)
@@ -614,17 +649,17 @@
     flip = jnp.where(iota((rows, rows), 0) + iota((rows, rows), 1) == rows - 1, 1.0, 0.0).astype(BF16)
     a_send[...] = nn(flip, mixed).T
     links.meet()
-    to_x = [links.exchange(a_send.reshape(n_blk, chans, rows), x_all, *part) for part in halves]
+    to_x = [links.exchange(a_send.reshape(n_blk, chans, rows), x_all, *part) for part in first_parts]
+    need("cot")
     cot = cot_ref[...].astype(F32)
     result = live * cot
     result_all[dp] = result
     gather_result = Gather(links, result_all)
 
+    need("step", "skip", "rate", "freq", "coef")
     columns[0] = jnp.broadcast_to(log_step[...], (128, width)).T
     columns[1] = jnp.broadcast_to(skip_gain[...], (128, width)).T
     own_skip = columns[1, pl.ds(first, chans), :]
-    for load in loads[:3]:
-        load.wait()
     turn = (128 - blk * chans % 128) % 128
     own = [pltpu.roll(windows[k], turn, 1).T[:chans] for k in range(4)]
     rate_own[...], freq_own[...], coef_own[0], coef_own[1] = own
@@ -637,18 +672,19 @@
     base_flat = base.reshape(8 * chans, 128)
     groups(0, chans, lambda group: make_powers(group, chans, consts, kern_slot, base_flat, q_ref, taps))
     shift_taps(own_skip, taps, base)
-    groups(0, chans, lambda group: make_band(group, chans, base_flat, t_ref))
 
     x_flat = x_all.reshape(n_blk * chans, 128)
     y_flat = y_send.reshape(n_blk * chans, 128)
     to_y = []
-    for part, arriving in zip(halves, to_x):
-        wait_all(arriving)
+    for k, part in enumerate(parts):
+        groups(*part, lambda group: make_band(group, chans, base_flat, t_ref))
+        if k < len(to_x):
+            to_x[k].wait_recv()
         groups(*part, lambda group: forward_group(group, chans, n_blk, consts, lead_slot, x_flat, q_ref, t_ref, h_ref, y_flat))
-        to_y += links.exchange(y_send, y_all, *part)
+        to_y.append(links.exchange(y_send, y_all, *part))
 
     gather_result.relay()
-    loads[3].wait()
+    need("out")
     low = result.astype(BF16)
     step = ff // 4
     for k in range(4):
@@ -658,10 +694,10 @@
     out_slice = ffn_out[pl.ds(rows_s, part_ff), :]
     for k in range(n_dp):
         slice_grad[k * rows : (k + 1) * rows, :] = nt(result_all[k].astype(BF16), out_slice)
-    loads[4].wait()
-    loads[5].wait()
-
-    wait_all(to_y)
+    need("glu", "glu_b", "n2g", "n2b", "in", "in_b", "out_b")
+
+    for batch in to_y:
+        batch.wait_recv()
     conv = y_all.reshape(width, rows)[...].T
     gelu_out, gelu_slope = gelu_parts(conv)
     slope_keep[...] = gelu_slope
@@ -763,7 +799,7 @@
             part_in[rows_cut, cols_cut] = tn(feeds, pre_s[:, cols_cut])
             part = window(part_in, row0, col0, (0, 0), cols_k)
             total = window(sum_in, row0, col0, (0, part_ff), cols_k)
-        chunks[k] = Chunk(links, rows_k, part, total, landings[k], kind == "glu", plan)
+        chunks[k] = Chunk(links, rows_k, part, total, landings[k], kind == "glu", plan, sum_out)
         chunks[k].advance()
 
     dy_flat = dy_all.reshape(n_blk * chans, 128)
@@ -771,7 +807,7 @@
 
     def backward(k):
         if k == 0:
-            wait_all(arrivals["dy"])
+            arrivals["dy"].wait_recv()
         size = min(GROUP, chans)
         if k * size < chans:
             backward_group([k * size + i for i in range(size)], chans, n_blk, consts, lead_slot, x_flat, dy_flat, q_ref, t_ref, h_ref, dx_flat, a_ref, b_ref, g_ref)
@@ -799,7 +835,7 @@
 
     @piece
     def ln1():
-        wait_all(arrivals["dx"])
+        arrivals["dx"].wait_recv()
         back = dx_all.reshape(width, rows)[...].T
         high, rest = split(back)
         rest, last = split(back - high.astype(F32))
@@ -811,29 +847,33 @@
 
     @piece
     def s0():
-        waits = arrivals["s0"] = []
-        for mask in range(1, n_dp):
-            at = links.dp_peer(mask) * quarter
-            waits.append(links.copy(own_par.at[pl.ds(at, quarter)], dp_par.at[dp], mask, 0))
-            waits.append(links.copy(vec, dp_vec.at[dp], mask, 0))
+        moves = [
+            (own_par.at[pl.ds(links.dp_peer(mask) * quarter, quarter)], dp_par.at[dp], mask, 0) for mask in range(1, n_dp)
+        ]
+        arrivals["s0"] = [
+            Batch(links, moves, dp_par.at[pl.ds(0, n_dp - 1)]),
+            Batch(links, [(vec, dp_vec.at[dp], mask, 0) for mask in range(1, n_dp)], dp_vec.at[pl.ds(0, n_dp - 1)]),
+        ]
         dp_par[dp] = own_par[pl.ds(dp * quarter, quarter)]
         dp_vec[dp] = vec[...]
 
     @piece
     def s1():
-        wait_all(arrivals["s0"])
+        for batch in arrivals["s0"]:
+            batch.wait_recv()
         sum_par[...] = sum_slots(dp_par, n_dp)
         sum_vec[...] = sum_slots(dp_vec, n_dp)
-        waits = arrivals["s1"] = []
-        for mask in range(1, n_blk):
-            waits.append(links.copy(sum_par, blk_par.at[blk], 0, mask))
-            waits.append(links.copy(sum_vec, blk_vec.at[blk], 0, mask))
+        arrivals["s1"] = [
+            Batch(links, [(src, dst.at[blk], 0, mask) for mask in range(1, n_blk)], dst.at[pl.ds(0, n_blk - 1)])
+            for src, dst in ((sum_par, blk_par), (sum_vec, blk_vec))
+        ]
         blk_par[blk] = sum_par[...]
         blk_vec[blk] = sum_vec[...]
 
     @piece
     def s2():
-        wait_all(arrivals["s1"])
+        for batch in arrivals["s1"]:
+            batch.wait_recv()
         all_par[dp] = blk_par[...]
         arrivals["s2"] = Gather(links, all_par)
         vec_out[...] = sum_slots(blk_vec, n_blk)
@@ -870,8 +910,9 @@
 def piece_shapes(n_dp, n_blk, width, ff):
     shapes = {}
     n_glu, n_ffn = len(GLU_PLANS), len(FFN_PLANS) // 2
-    size = width // n_glu
-    for k, plan in enumerate(GLU_PLANS):
+    cuts = min(n_glu, width // (8 * n_blk))
+    size = width // cuts
+    for k, plan in enumerate(GLU_PLANS[:cuts]):
         shapes[k] = ("glu", k * size, 0, size, 2 * width // n_dp, plan)
     for kind, at, height, breadth in (("out", n_glu, ff // n_dp, width), ("in", n_glu + n_ffn, width, ff // n_dp)):
         cols = min(n_ffn, breadth // 128)
@@ -935,7 +976,9 @@
         kind, _, _, rows_k, cols_k, plan = shapes.get(k, ("out", 0, 0, 8 * n_blk, 128, FFN_PLANS[0]))
         landings.append(f32(landing_rows(rows_k, plan[0], n_dp, n_blk, kind == "glu"), cols_k))
     scratch = [
-        dma(LINK_SEMS), dma(LINK_SEMS), dma(8),
+        dma(SEND_SEMS), dma(RECV_SEMS), dma(20),
+        bf16(rows, width), bf16(rows, width), f32(1, width), f32(1, width), f32(1, width), f32(1, width), f32(1, 2 * width),
+        f32(1, width), f32(1, width), f32(1, ff), f32(1, width),
         bf16(width, 2 * width), bf16(width, ff), bf16(ff, width),
         f32(4, states, 128), f32(chans, states), f32(chans, states), f32(2, chans, states), f32(2, width, 128),
         f32(width, rows), f32(n_blk, chans, rows), f32(n_blk, chans, rows), f32(n_blk, chans, rows),
@@ -957,13 +1000,13 @@
         functools.partial(whole_kernel, n_dp, n_blk),
         out_shape=[VMEM(v.shape, v.dtype) for v in outs],
         out_specs=[vmem] * len(outs),
-        in_specs=[vmem, pl.BlockSpec(memory_space=pltpu.SMEM), vmem, vmem, vmem, vmem, anywhere, anywhere, anywhere, vmem, anywhere, vmem, vmem, vmem, anywhere, vmem, anywhere, vmem],
+        in_specs=[anywhere, pl.BlockSpec(memory_space=pltpu.SMEM)] + [anywhere] * 16,
         scratch_shapes=scratch,
         compiler_params=pltpu.CompilerParams(collective_id=0, has_side_effects=True, vmem_limit_bytes=44 * 2**20),
     )(
-        block_in[0], seq_lengths, cotangent[0], row(norm1_gain), row(norm1_bias), row(log_step), log_rate.T, frequency.T,
-        out_coef.swapaxes(1, 2), row(skip_gain), glu_weight, row(glu_bias), row(norm2_gain), row(norm2_bias), ffn_in,
-        row(ffn_in_bias), ffn_out, row(ffn_out_bias),
+        block_in[0], seq_lengths, cotangent[0], log_rate.T, frequency.T, out_coef.swapaxes(1, 2), glu_weight, ffn_in, ffn_out,
+        row(norm1_gain), row(norm1_bias), row(log_step), row(skip_gain), row(glu_bias), row(norm2_gain), row(norm2_bias),
+        row(ffn_in_bias), row(ffn_out_bias),
     )
     block_out, grad_in, g_glu, g_in, g_out, vec, par = out
     widths = [width, width, width, width, width, 2 * width, ff, width, width]

time: 122 us -> 113 us (0.926)
  Pallas kernels: 120 us -> 112 us
    pallas_call x1, Pallas kernels: 115 us -> 106 us  [on_device(): pl.pallas_call(functools.partial(whole_kernel, n_dp, n_blk), out_shape=[V...]
where the time goes in v4:
time: 113 us
  Pallas kernels  112 us (99%)
  between operations  1.48 us (1%)
    pallas_call x1, Pallas kernels, on_device(): pl.pallas_call(functools.partial(whole_kernel, n_dp, n_blk), out_shape=[V...  106 us
    pallas_call x1, Pallas kernels, on_device(): pl.pallas_call(deliver, out_shape=out_shapes, in_specs=[vmem] * 7, out_sp...  5.15 us

profile of v4, /device:TPU:0, one launch (start us, length us, event | category | flops | bytes accessed | tf_op | source)
XLA Modules:
  0.0 113.0 jit_solution(18090656610957875471)
XLA Ops:
  1.3 106.4 %shard_map.305 = (bf16[128,512]{1,0:T(8,128)(2,1)S(1)}, f32[128,512]{1,0:T(8,128)S(1)}, f32[512,1024]{1,0:T(8,128)S(1)}, f32[512,2048]{1,0:T(8,128)S(1)}, f32[20...) custom-call(bf16[128,512]{1,0:T(8,128)(2,1)} %bitcast.29, s32[1]{0:T(128)S(6)} %copy.35.lengths, ...), custom_call_target="tpu_custom_call" | custom-call | tf_op jit(solution)/shard_map/pallas_call | solution.py:999
  107.7 5.1 %shard_map.306 = (bf16[128,512]{1,0:T(8,128)(2,1)}, f32[128,512]{1,0:T(8,128)}, f32[512,1024]{1,0:T(8,128)}, f32[512,2048]{1,0:T(8,128)}, f32[2048,512]{1,0:T(8,...) custom-call(bf16[128,512]{1,0:T(8,128)(2,1)S(1)} %get-tuple-element., ...), custom_call_target="tpu_custom_call" | custom-call | tf_op jit(solution)/shard_map/pallas_call | solution.py:1023

commit v5 on v4

--- a/solution.py
+++ b/solution.py
@@ -46,7 +46,7 @@
     0, "part7", 1, "part8", "part9", "part10", 2, "part11", "part12", "part13", "part14", 4, "part15",
     "part16", 3, "part17", "part18", 5, "part19", 0, 6, "bwd0", 7, 9, 1, 0, 8, 4, 12, "bwd1", 7, 5, 1, 10, 0,
     11, 8, 15, 2, 4, "bwd2", 7, 5, 1, 14, 8, 11, 13, 10, 0, 16, 3, 2, 7, 5, 4, "bwd3", 1, 8, 14, 11, 17, 13,
-    19, 10, 0, 18, 6, "near", 9, 7, 12, 5, 3, 16, 2, 15, 4, 7, 0, 5, 1, 8, "ln1", 14, 11, 17, 7, 4, "s0", 13,
+    19, 10, 0, 18, 6, "late", "near", 9, 7, 12, 5, 3, 16, 2, 15, 4, 7, 0, 5, 1, 8, "ln1", 14, 11, 17, 7, 4, "s0", 13,
     19, 0, 10, 18, 6, 7, 8, 5, 9, 12, 0, 3, 16, 1, 2, "s1", 5, 15, 14, 11, 17, 4, 13, 19, 10, 1, 6, 18, 15, 4,
     8, 9, 12, 2, 11, 3, 16, 19, 1, "s2", 8, 14, 10, 9, 12, 17, 13, 6, 18, 2, 3, 15, 11, 16, 14, "s3", 11, 19,
     17, 9, 18, 10, 16, 6, 12, 10, 2, 13, 14, 19, 3, 2, 15, 14, 6, 9, 17, 18, 6, 9, 13, 16, 13, 16, 3, 19, 12,
@@ -308,8 +308,8 @@
         b_ref[pl.ds(chan, 1), :] = out[1:2] + out[3:4]
 
 
-def groups(first, count, body):
-    size = min(GROUP, count)
+def groups(first, count, body, size=GROUP):
+    size = min(size, count)
 
     def step(k, carry):
         body([first + k * size + i for i in range(size)])
@@ -599,7 +599,7 @@
     send_sems, recv_sems, load_sems, x_ref, cot_ref, n1g, n1b, log_step, skip_gain, glu_b, n2g, n2b, in_b, out_b, glu_w, ffn_in, ffn_out, windows, rate_own, freq_own, coef_own, columns,
     a_send, x_all, y_send, y_all, dy_send, dy_all, dx_send, dx_all,
     q_ref, t_ref, h_ref, consts, base, taps, a_ref, b_ref, g_ref,
-    result_all, feed_all, dglu, hidden_grad, slice_grad, hidden_s, pre_s, slope_keep, unit_keep, residual_keep, gate_keep,
+    result_all, feed_all, dglu, hidden_grad, slice_grad, hidden_s, pre_s, hidden_own, pre_own, slope_keep, unit_keep, residual_keep, gate_keep,
     gelu_keep, acc_out, acc_feed, residual_grad, part_glu, part_in, part_out,
     own_par, dp_par, sum_par, blk_par, all_par, flat_par, vec, dp_vec, sum_vec, blk_vec, *landings,
 ):
@@ -670,7 +670,7 @@
     kern_slot = ssm_setup(n_blk, ssm(), consts, base)
     lead_slot = kern_slot - 1
     base_flat = base.reshape(8 * chans, 128)
-    groups(0, chans, lambda group: make_powers(group, chans, consts, kern_slot, base_flat, q_ref, taps))
+    groups(0, chans, lambda group: make_powers(group, chans, consts, kern_slot, base_flat, q_ref, taps), 2 * GROUP)
     shift_taps(own_skip, taps, base)
 
     x_flat = x_all.reshape(n_blk * chans, 128)
@@ -727,30 +727,35 @@
             cut = slice(k * step, (k + 1) * step)
             hidden, slope = gelu_parts(nn(feed, ffn_in[:, cut]) + in_b[:, cut])
             grad_pre = (hidden_grad[:, cut] * slope).astype(BF16)
-            forward = nn(hidden.astype(BF16), ffn_out[cut, :])
+            hidden_own[:, cut] = hidden.astype(BF16)
+            pre_own[:, cut] = grad_pre
             back = nt(grad_pre, ffn_in[:, cut])
-            acc_out[...] = forward if k == 0 else acc_out[...] + forward
             acc_feed[...] = back if k == 0 else acc_feed[...] + back
-            vec[7 + k : 8 + k, :] = token_sum(grad_pre.astype(F32))
-        block_out[...] = (residual_keep[0] + live * (acc_out[...] + out_b[...])).astype(BF16)
 
     @piece
     def glubwd():
-        grad_feed = acc_feed[...]
         unit_mid = residual_keep[1]
-        vec[2:3, :] = token_sum(grad_feed * unit_mid)
-        vec[3:4, :] = token_sum(grad_feed)
-        vec[4:5, :] = token_sum(result_all[dp])
-        grad_res = cot_ref[...].astype(F32) + norm_back(grad_feed, n2g[...], unit_mid, scale_mid)
+        grad_res = cot_ref[...].astype(F32) + norm_back(acc_feed[...], n2g[...], unit_mid, scale_mid)
         residual_grad[...] = grad_res
         grad_left = live * grad_res
         left, gate = gate_keep[0], gate_keep[1]
-        to_left = (grad_left * gate).astype(BF16)
-        to_gate = (grad_left * left * gate * (1.0 - gate)).astype(BF16)
-        dglu[:, :width] = to_left
-        dglu[:, width:] = to_gate
-        vec[5:6, :] = token_sum(to_left.astype(F32))
-        vec[6:7, :] = token_sum(to_gate.astype(F32))
+        dglu[:, :width] = (grad_left * gate).astype(BF16)
+        dglu[:, width:] = (grad_left * left * gate * (1.0 - gate)).astype(BF16)
+
+    @piece
+    def late():
+        for k in range(4):
+            cut = slice(k * step, (k + 1) * step)
+            forward = nn(hidden_own[:, cut], ffn_out[cut, :])
+            acc_out[...] = forward if k == 0 else acc_out[...] + forward
+            vec[7 + k : 8 + k, :] = token_sum(pre_own[:, cut].astype(F32))
+        block_out[...] = (residual_keep[0] + live * (acc_out[...] + out_b[...])).astype(BF16)
+        grad_feed = acc_feed[...]
+        vec[2:3, :] = token_sum(grad_feed * residual_keep[1])
+        vec[3:4, :] = token_sum(grad_feed)
+        vec[4:5, :] = token_sum(result_all[dp])
+        vec[5:6, :] = token_sum(dglu[:, :width].astype(F32))
+        vec[6:7, :] = token_sum(dglu[:, width:].astype(F32))
 
     @piece
     def dy():
@@ -930,24 +935,21 @@
     return total
 
 
-def deliver_kernel(big_in, vec, par, others, big_out, rows_out, rate, freq, coef, others_out, sems):
+def deliver_kernel(big_in, vec, par, rows_out, big_out, rate, freq, coef, rows_buf, sems):
     states = rate.shape[0]
-    moves = []
-    for src, dst in zip(big_in, big_out):
-        part = src.shape[0] // BIG_PARTS
-        moves += [(src.at[pl.ds(k * part, part)], dst.at[pl.ds(k * part, part)]) for k in range(BIG_PARTS)]
-    moves += list(zip(others, others_out))
+    moves = list(zip(big_in, big_out))
     moves += [(par.at[pl.ds(0, states)], rate), (par.at[pl.ds(states, states)], freq)]
     moves += [(par.at[pl.ds((2 + k) * states, states)], coef.at[k]) for k in range(2)]
     copies = [pltpu.make_async_copy(src, dst, sems.at[k]) for k, (src, dst) in enumerate(moves)]
     for copy in copies:
         copy.start()
     row = 0
-    for out in rows_out:
-        count = out.shape[1] // vec.shape[1]
-        for k in range(count):
-            out[:, k * vec.shape[1] : (k + 1) * vec.shape[1]] = vec[row : row + 1, :]
+    for k, (buf, out) in enumerate(zip(rows_buf, rows_out)):
+        for part in range(out.shape[1] // vec.shape[1]):
+            buf[:, part * vec.shape[1] : (part + 1) * vec.shape[1]] = vec[row : row + 1, :]
             row += 1
+        copies.append(pltpu.make_async_copy(buf, out, sems.at[len(moves) + k]))
+        copies[-1].start()
     for copy in copies:
         copy.wait()
 
@@ -987,7 +989,7 @@
         f32(8, chans, 128), f32(chans, 128), f32(2 * chans, 128), f32(2 * chans, 128), f32(chans, 128),
         f32(n_dp, rows, width), f32(n_dp, rows, width),
         bf16(rows, 2 * width),
-        f32(rows, ff), f32(tokens, part_ff), bf16(tokens, part_ff), bf16(tokens, part_ff),
+        f32(rows, ff), f32(tokens, part_ff), bf16(tokens, part_ff), bf16(tokens, part_ff), bf16(rows, ff), bf16(rows, ff),
         f32(rows, width), f32(rows, width), f32(2, rows, width), f32(2, rows, width),
         bf16(rows, width), f32(rows, width), f32(rows, width), f32(rows, width),
         f32(width, 2 * width), f32(width, part_ff), f32(part_ff, width),
@@ -1017,15 +1019,16 @@
     out_shapes = made + big + small + params
 
     def deliver(block_out, grad_in, g_glu, g_in, g_out, vec, par, *rest):
-        outs, sems = rest[:-1], rest[-1]
-        deliver_kernel([g_glu, g_in, g_out], vec, par, [block_out, grad_in], outs[2:5], outs[5:14], *outs[14:], outs[:2], sems)
+        outs, rows_buf, sems = rest[:17], rest[17:-1], rest[-1]
+        big = [g_out, g_in, g_glu, grad_in, block_out]
+        deliver_kernel(big, vec, par, outs[5:14], [outs[4], outs[3], outs[2], outs[1], outs[0]], *outs[14:], rows_buf, sems)
 
     done = pl.pallas_call(
         deliver,
         out_shape=out_shapes,
         in_specs=[vmem] * 7,
-        out_specs=[anywhere] * 5 + [vmem] * 9 + [anywhere] * 3,
-        scratch_shapes=[dma(32)],
+        out_specs=[anywhere] * 17,
+        scratch_shapes=[f32(1, w) for w in widths] + [dma(18)],
         compiler_params=pltpu.CompilerParams(vmem_limit_bytes=8 * 2**20),
     )(*out)
     flat = [v.reshape(-1) for v in done[5:14]]

time: 113 us -> 113 us (level)
  no operation moved by 1% of the time
where the time goes in v5:
time: 113 us
  Pallas kernels  111 us (98%)
  between operations  1.48 us (1%)
    pallas_call x1, Pallas kernels, on_device(): pl.pallas_call(functools.partial(whole_kernel, n_dp, n_blk), out_shape=[V...  107 us
    pallas_call x1, Pallas kernels, on_device(): pl.pallas_call(deliver, out_shape=out_shapes, in_specs=[vmem] * 7, out_sp...  4.35 us

profile of v5, /device:TPU:0, one launch (start us, length us, event | category | flops | bytes accessed | tf_op | source)
XLA Modules:
  0.0 112.6 jit_solution(795926588704768053)
XLA Ops:
  1.3 106.8 %shard_map.305 = (bf16[128,512]{1,0:T(8,128)(2,1)S(1)}, f32[128,512]{1,0:T(8,128)S(1)}, f32[512,1024]{1,0:T(8,128)S(1)}, f32[512,2048]{1,0:T(8,128)S(1)}, f32[20...) custom-call(bf16[128,512]{1,0:T(8,128)(2,1)} %bitcast.29, s32[1]{0:T(128)S(6)} %copy.35.lengths, ...), custom_call_target="tpu_custom_call" | custom-call | tf_op jit(solution)/shard_map/pallas_call | solution.py:1001
  108.1 4.3 %shard_map.306 = (bf16[128,512]{1,0:T(8,128)(2,1)}, f32[128,512]{1,0:T(8,128)}, f32[512,1024]{1,0:T(8,128)}, f32[512,2048]{1,0:T(8,128)}, f32[2048,512]{1,0:T(8,...) custom-call(bf16[128,512]{1,0:T(8,128)(2,1)S(1)} %get-tuple-element., ...), custom_call_target="tpu_custom_call" | custom-call | tf_op jit(solution)/shard_map/pallas_call | solution.py:1026

commit v6 on v5

--- a/solution.py
+++ b/solution.py
@@ -596,7 +596,7 @@
     n_dp, n_blk, x_hbm, lengths, cot_hbm, log_rate, frequency, out_coef, glu_hbm, in_hbm, out_hbm,
     n1g_hbm, n1b_hbm, log_step_hbm, skip_hbm, glu_b_hbm, n2g_hbm, n2b_hbm, in_b_hbm, out_b_hbm,
     block_out, grad_in, sum_glu, sum_in, sum_out, vec_out, par_out,
-    send_sems, recv_sems, load_sems, x_ref, cot_ref, n1g, n1b, log_step, skip_gain, glu_b, n2g, n2b, in_b, out_b, glu_w, ffn_in, ffn_out, windows, rate_own, freq_own, coef_own, columns,
+    send_sems, recv_sems, load_sems, x_ref, cot_ref, n1g, n1b, log_step, skip_gain, glu_b, n2g, n2b, in_b, out_b, glu_w, ffn_in, ffn_out, windows, rate_own, freq_own, coef_own, step_own,
     a_send, x_all, y_send, y_all, dy_send, dy_all, dx_send, dx_all,
     q_ref, t_ref, h_ref, consts, base, taps, a_ref, b_ref, g_ref,
     result_all, feed_all, dglu, hidden_grad, slice_grad, hidden_s, pre_s, hidden_own, pre_own, slope_keep, unit_keep, residual_keep, gate_keep,
@@ -612,7 +612,6 @@
     first_parts = [(0, chans)] if FIRST_WHOLE else parts
     links = Links(send_sems, recv_sems, n_dp, n_blk)
     dp, blk = links.dp, links.blk
-    first = pl.multiple_of(blk * chans, 8)
     lanes_at = pl.multiple_of(blk * chans // 128 * 128, 128)
 
     links.loads = []
@@ -657,15 +656,15 @@
     gather_result = Gather(links, result_all)
 
     need("step", "skip", "rate", "freq", "coef")
-    columns[0] = jnp.broadcast_to(log_step[...], (128, width)).T
-    columns[1] = jnp.broadcast_to(skip_gain[...], (128, width)).T
-    own_skip = columns[1, pl.ds(first, chans), :]
     turn = (128 - blk * chans % 128) % 128
     own = [pltpu.roll(windows[k], turn, 1).T[:chans] for k in range(4)]
     rate_own[...], freq_own[...], coef_own[0], coef_own[1] = own
+    column = lambda ref: pltpu.roll(jnp.broadcast_to(ref[:, pl.ds(lanes_at, 128)], (128, 128)), turn, 1).T[:chans]
+    step_own[...] = column(log_step)
+    own_skip = column(skip_gain)
 
     def ssm():
-        return columns[0, pl.ds(first, chans), :], rate_own[...], freq_own[...], (coef_own[0], coef_own[1])
+        return step_own[...], rate_own[...], freq_own[...], (coef_own[0], coef_own[1])
 
     kern_slot = ssm_setup(n_blk, ssm(), consts, base)
     lead_slot = kern_slot - 1
@@ -982,7 +981,7 @@
         bf16(rows, width), bf16(rows, width), f32(1, width), f32(1, width), f32(1, width), f32(1, width), f32(1, 2 * width),
         f32(1, width), f32(1, width), f32(1, ff), f32(1, width),
         bf16(width, 2 * width), bf16(width, ff), bf16(ff, width),
-        f32(4, states, 128), f32(chans, states), f32(chans, states), f32(2, chans, states), f32(2, width, 128),
+        f32(4, states, 128), f32(chans, states), f32(chans, states), f32(2, chans, states), f32(chans, 128),
         f32(width, rows), f32(n_blk, chans, rows), f32(n_blk, chans, rows), f32(n_blk, chans, rows),
         f32(width, rows), f32(n_blk, chans, rows), f32(n_blk, chans, rows), f32(n_blk, chans, rows),
         bf16(chans, 256, 128), bf16(chans, 256, 128), f32(chans, n_blk, 128), f32(n_consts(n_blk), chans, 128),

time: 113 us -> 113 us (level)
  no operation moved by 1% of the time
where the time goes in v6:
time: 113 us
  Pallas kernels  111 us (98%)
  between operations  1.48 us (1%)
    pallas_call x1, Pallas kernels, on_device(): pl.pallas_call(functools.partial(whole_kernel, n_dp, n_blk), out_shape=[V...  107 us
    pallas_call x1, Pallas kernels, on_device(): pl.pallas_call(deliver, out_shape=out_shapes, in_specs=[vmem] * 7, out_sp...  4.35 us

profile of v6, /device:TPU:0, one launch (start us, length us, event | category | flops | bytes accessed | tf_op | source)
XLA Modules:
  0.0 112.6 jit_solution(12250095785492739012)
XLA Ops:
  1.3 106.8 %shard_map.305 = (bf16[128,512]{1,0:T(8,128)(2,1)S(1)}, f32[128,512]{1,0:T(8,128)S(1)}, f32[512,1024]{1,0:T(8,128)S(1)}, f32[512,2048]{1,0:T(8,128)S(1)}, f32[20...) custom-call(bf16[128,512]{1,0:T(8,128)(2,1)} %bitcast.29, s32[1]{0:T(128)S(6)} %copy.35.lengths, ...), custom_call_target="tpu_custom_call" | custom-call | tf_op jit(solution)/shard_map/pallas_call | solution.py:1000
  108.1 4.3 %shard_map.306 = (bf16[128,512]{1,0:T(8,128)(2,1)}, f32[128,512]{1,0:T(8,128)}, f32[512,1024]{1,0:T(8,128)}, f32[512,2048]{1,0:T(8,128)}, f32[2048,512]{1,0:T(8,...) custom-call(bf16[128,512]{1,0:T(8,128)(2,1)S(1)} %get-tuple-element., ...), custom_call_target="tpu_custom_call" | custom-call | tf_op jit(solution)/shard_map/pallas_call | solution.py:1025
